TPU v7x, 32 devices: a whole 2x2x4 slice. The times are simulated.
32 devices in a mesh: sec: 2 (over core), seq: 8 (over z, x), tp: 2 (over y).
Axes of the slice: x: 2, y: 2, z: 4, core: 2. Of those that a mesh axis runs over, the one named last changes fastest.
Arguments:
- hidden_rows: bfloat16 [2, 512, 5120], P('sec', 'seq'), may hold values from -10 to 10
- carried: bfloat16 [2, 512, 5120], P('sec', 'seq'), may hold values from -6 to 6
- query_weight: bfloat16 [2, 5120, 4096], P('sec', 'seq', 'tp'), may hold values from -6 to 6
- response_cache: bfloat16 [2, 512, 2048], P('sec', 'seq', 'tp'), may hold values from -8.375 to 8.375
- prompt_cache: bfloat16 [2, 8, 16384, 2048], P('sec', None, 'seq', 'tp'), may hold values from -5 to 5
- prompt_lengths: int32 [8], replicated, may hold values from 1 to 16384, 81920 in all
- response_lengths: int32 [2, 8], replicated, may hold values from 1 to 64, 320 in all within a row
- block_prompts: int32 [2, 8, 1], replicated, may hold values from 0 to 7
Outputs:
- attended: bfloat16 [2, 512, 4096], P('sec', 'seq', 'tp')
All inputs are finite; a program needn't handle non-finite values.
Results may differ from a plain program's by a relative error of at most 0.0096.
Values may be sent and summed in bfloat16 or wider, within the bound.
No kernel may reach another device: no remote copies, remote signals or barrier semaphores. Data moves between devices by JAX's collectives and lax.ppermute only.
A program may use at most 192 MiB of HBM per device.

v0:
```python
import functools
import math

import jax
import jax.numpy as jnp
from jax import lax
from jax.experimental import pallas as pl
from jax.experimental.pallas import tpu as pltpu
from jax.sharding import PartitionSpec as P

HD = 128
GR = 4
NEG = -1e30
LOG2E = 1.4426950408889634
CHUNK = 512
PIECE = 1024
ROUND = 32
EXTRA = 128
SLOT = 16
BIG = 2.0 ** 100
MIB = 1024 * 1024


def dot_nt(a, b):
    return lax.dot_general(a, b, (((1,), (1,)), ((), ())), preferred_element_type=jnp.float32)


class Grid:
    def __init__(self, count):
        self.n = count
        self.xs = 1 << ((count.bit_length() - 1) // 2)
        self.zs = count // self.xs

    def owner(self, shard, kx, kz):
        z, x = shard // self.xs, shard % self.xs
        return (z ^ kz) * self.xs + (x ^ kx)

    def swap(self, value, kx, kz):
        pairs = [(s, self.owner(s, kx, kz)) for s in range(self.n)]
        return lax.ppermute(value, "seq", pairs)


class Facts:
    def __init__(self, n, meta):
        self.n, self.meta = n, meta
        self.section, self.shard = meta[0], meta[1]

    def length(self, block):
        return self.meta[2 + self.section * self.n + block]

    def prompt(self, block):
        return self.meta[2 + (2 + self.section) * self.n + block]

    def prompt_length(self, prompt):
        return self.meta[2 + 4 * self.n + prompt]


def split_kernel(grid, depth, meta, hidden_ref, handed_ref, *out_refs):
    for kx in range(grid.xs):
        for kz in range(grid.zs):
            at = pl.multiple_of(grid.owner(meta[1], kx, kz) * depth, HD)
            total = hidden_ref[0, :, pl.ds(at, depth)].astype(jnp.float32) + handed_ref[
                0, :, pl.ds(at, depth)
            ].astype(jnp.float32)
            out_refs[kx * grid.zs + kz][...] = total.astype(jnp.bfloat16)


def split(grid, meta, hidden, handed, depth):
    bl = hidden.shape[1]
    if depth % HD:
        total = (hidden[0].astype(jnp.float32) + handed[0].astype(jnp.float32)).astype(jnp.bfloat16)
        return [
            lax.dynamic_slice_in_dim(total, grid.owner(meta[1], kx, kz) * depth, depth, 1)
            for kx in range(grid.xs) for kz in range(grid.zs)
        ]
    whole = pl.BlockSpec(hidden.shape, lambda i, *m: (0, 0, 0))
    return pl.pallas_call(
        functools.partial(split_kernel, grid, depth),
        grid_spec=pltpu.PrefetchScalarGridSpec(
            num_scalar_prefetch=1,
            grid=(1,),
            in_specs=[whole, whole],
            out_specs=[pl.BlockSpec((bl, depth), lambda i, *m: (0, 0))] * grid.n,
        ),
        out_shape=[jax.ShapeDtypeStruct((bl, depth), jnp.bfloat16)] * grid.n,
        compiler_params=pltpu.CompilerParams(vmem_limit_bytes=16 * MIB),
        name="split",
    )(meta, hidden, handed)


def run_moves(moves):
    for needed, move in moves:
        if needed is None:
            move.start()
        else:
            pl.when(needed)(move.start)
    for needed, move in moves:
        if needed is None:
            move.wait()
        else:
            pl.when(needed)(move.wait)


def fetch_kernel(*refs):
    count = len(refs) // 2
    run_moves([
        (None, pltpu.make_async_copy(refs[i], refs[count + i], refs[-1].at[i]))
        for i in range(count)
    ])


def fetch(arrays):
    anywhere, near = pl.BlockSpec(memory_space=pltpu.HBM), pl.BlockSpec(memory_space=pltpu.VMEM)
    size = sum(math.prod(array.shape) for array in arrays)
    out = pl.pallas_call(
        fetch_kernel,
        in_specs=[anywhere] * len(arrays),
        out_specs=[near] * len(arrays),
        scratch_shapes=[pltpu.SemaphoreType.DMA((len(arrays),))],
        out_shape=[pltpu.VMEM(array.shape, array.dtype) for array in arrays],
        compiler_params=pltpu.CompilerParams(vmem_limit_bytes=4 * MIB),
        cost_estimate=pl.CostEstimate(flops=0, bytes_accessed=2 * size, transcendentals=0),
        name="fetch",
    )(*[pltpu.with_memory_space_constraint(array, pltpu.HBM) for array in arrays])
    return [pltpu.with_memory_space_constraint(array, pltpu.VMEM) for array in out]


def fetch_cache_kernel(n, chunk, width, first, meta, cache_ref, kv_ref, sem):
    count, tile_len = kv_ref.shape[:2]
    facts = Facts(n, meta)
    moves = []
    for p in range(count):
        asked = facts.prompt(0) == p
        for b in range(1, n):
            asked = asked | (facts.prompt(b) == p)
        for c in range(tile_len // chunk):
            at = pl.ds(c * chunk, chunk)
            needed = asked & (facts.prompt_length(p) > facts.shard * tile_len + c * chunk)
            moves.append((needed, pltpu.make_async_copy(
                cache_ref.at[0, p, at, pl.ds(first * width, width)], kv_ref.at[p, at],
                sem.at[p, c],
            )))
    run_moves(moves)


def fetch_cache(n, meta, cache, width, first):
    count, tile_len = cache.shape[1:3]
    chunk = min(PIECE, tile_len)
    shape = (count, tile_len, width)
    out = pl.pallas_call(
        functools.partial(fetch_cache_kernel, n, chunk, width, first),
        grid_spec=pltpu.PrefetchScalarGridSpec(
            num_scalar_prefetch=1,
            grid=(1,),
            in_specs=[pl.BlockSpec(memory_space=pltpu.HBM)],
            out_specs=pl.BlockSpec(memory_space=pltpu.VMEM),
            scratch_shapes=[pltpu.SemaphoreType.DMA((count, tile_len // chunk))],
        ),
        out_shape=pltpu.VMEM(shape, cache.dtype),
        compiler_params=pltpu.CompilerParams(vmem_limit_bytes=4 * MIB),
        cost_estimate=pl.CostEstimate(
            flops=0, bytes_accessed=2 * math.prod(shape), transcendentals=0
        ),
        name="fetch_cache",
    )(meta, pltpu.with_memory_space_constraint(cache, pltpu.HBM))
    return pltpu.with_memory_space_constraint(out, pltpu.VMEM)


def project_kernel(grid, bl, share, meta, *refs):
    x_refs, w_ref, refs = refs[:grid.n], refs[grid.n], refs[grid.n + 1:]
    out_refs, (xp_ref, starts) = refs[:-2], refs[-2:]

    @pl.when(pl.program_id(0) == 0)
    def _():
        facts = Facts(grid.n, meta)
        shard = facts.shard
        offset = jnp.int32(0)
        for b in range(grid.n):
            starts[b] = offset
            offset = offset + facts.length(b)
        lane = lax.broadcasted_iota(jnp.int32, (8, grid.n * bl), 1)
        target = jnp.full(lane.shape, -1, jnp.int32)
        owners = [
            grid.owner(shard, kx, kz) for kx in range(grid.xs) for kz in range(grid.zs)
        ]
        for k, b in enumerate(owners):
            order = lane - k * bl
            used = (order >= 0) & (order < facts.length(b))
            target = jnp.where(used, order + starts[b], target)
        row = lax.broadcasted_iota(jnp.int32, (share, grid.n * bl), 0)
        target = jnp.broadcast_to(target[:1], row.shape)
        picks = [jnp.where(row + b * share == target, 1.0, 0.0) for b in owners]
        pick = jnp.concatenate(picks, axis=0).astype(jnp.bfloat16)
        x = jnp.concatenate([ref[...] for ref in x_refs], axis=0)
        chosen = jnp.dot(pick, x, preferred_element_type=jnp.float32)
        xp_ref[...] = chosen.astype(jnp.bfloat16)

    result = jnp.dot(xp_ref[...], w_ref[0], preferred_element_type=jnp.float32)
    rows = grid.zs * share
    for i, out_ref in enumerate(out_refs):
        chunk, kx = i // grid.xs, i % grid.xs

        @pl.when(pl.program_id(0) == chunk)
        def _(out_ref=out_ref, kx=kx):
            out_ref[...] = result[kx * rows:(kx + 1) * rows]


def project(grid, meta, xs, w, bl, share, chunks):
    k, cols = w.shape[1:]
    rows = grid.n * share
    tile = cols // chunks
    piece = (grid.zs * share, tile)
    return pl.pallas_call(
        functools.partial(project_kernel, grid, bl, share),
        grid_spec=pltpu.PrefetchScalarGridSpec(
            num_scalar_prefetch=1,
            grid=(chunks,),
            in_specs=[pl.BlockSpec((bl, k), lambda j, *m: (0, 0))] * grid.n
            + [pl.BlockSpec((1, k, tile), lambda j, *m: (0, 0, j))],
            out_specs=[pl.BlockSpec(piece, lambda j, *m: (0, 0))] * (chunks * grid.xs),
            scratch_shapes=[
                pltpu.VMEM((rows, k), jnp.bfloat16), pltpu.SMEM((grid.n,), jnp.int32)
            ],
        ),
        out_shape=[jax.ShapeDtypeStruct(piece, jnp.float32)] * (chunks * grid.xs),
        compiler_params=pltpu.CompilerParams(vmem_limit_bytes=20 * MIB),
        cost_estimate=pl.CostEstimate(
            flops=2 * rows * k * cols, bytes_accessed=2 * k * cols + 4 * rows * cols,
            transcendentals=0,
        ),
        name="project",
    )(meta, *xs, w)


def three_terms(value):
    high = value.astype(jnp.bfloat16).astype(jnp.float32)
    mid = (value - high).astype(jnp.bfloat16).astype(jnp.float32)
    return [high, mid, value - high - mid]


def encode(peak, total):
    lane = lax.broadcasted_iota(jnp.int32, peak.shape, 1)
    out = jnp.zeros(peak.shape, jnp.float32)
    for i, term in enumerate(three_terms(peak) + three_terms(total)):
        term = jnp.where(lane < SLOT, term, 0.0)
        out = out + (pltpu.roll(term, i * SLOT, 1) if i else term)
    return out.astype(jnp.bfloat16)


def decode(tile):
    terms = tile.astype(jnp.float32)
    parts = [terms] + [pltpu.roll(terms, EXTRA - i * SLOT, 1) for i in range(1, 6)]
    return parts[0] + parts[1] + parts[2], parts[3] + parts[4] + parts[5]


def merge(refs, heads):
    width = heads * HD
    peaks, totals = zip(*[decode(ref[:, width:]) for ref in refs])
    rows = peaks[0].shape[0]
    peak = functools.reduce(jnp.maximum, peaks)
    weights = [jnp.exp2(one - peak) for one in peaks]
    total = functools.reduce(jnp.add, [w * one for w, one in zip(weights, totals)])
    out = []
    for h in range(heads):
        terms = [
            jnp.broadcast_to(weight[:, h:h + 1], (rows, HD))
            * ref[:, h * HD:(h + 1) * HD].astype(jnp.float32)
            for weight, ref in zip(weights, refs)
        ]
        out.append(functools.reduce(jnp.add, terms))
    return out, peak, total


def merge_kernel(zs, heads, *refs):
    sources, outs = refs[:-zs], refs[-zs:]
    for kz in range(zs):
        parts, peak, total = merge([ref.at[kz] for ref in sources], heads)
        for h in range(heads):
            outs[kz][:, h * HD:(h + 1) * HD] = parts[h].astype(jnp.bfloat16)
        outs[kz][:, heads * HD:] = encode(peak, total)


def merge_column(sources, heads):
    zs, bl, width = sources[0].shape
    return pl.pallas_call(
        functools.partial(merge_kernel, zs, heads),
        out_shape=[jax.ShapeDtypeStruct((bl, width), jnp.bfloat16)] * zs,
        compiler_params=pltpu.CompilerParams(vmem_limit_bytes=16 * MIB),
        name="merge",
    )(*sources)


def attend_kernel(grid, kx, bl, share, first, heads, tile_len, coords, meta, *refs):
    q_refs, refs = refs[:len(coords)], refs[len(coords):]
    kv_refs, refs = refs[:heads], refs[heads:]
    own_ref, out_ref, q32_ref, acc_ref, m_ref = refs
    facts = Facts(grid.n, meta)
    shard = facts.shard
    rows = grid.n * share
    for q_ref, places in zip(q_refs, coords):
        for i, (fx, fz) in enumerate(places):
            at = pl.multiple_of(grid.owner(shard, fx, fz) * share, 8)
            q32_ref[pl.ds(at, share), :] = q_ref[i].astype(jnp.float32)
    q32_ref[rows:, :] = jnp.zeros((bl + 8, q32_ref.shape[1]), jnp.float32)
    acc_ref[...] = jnp.zeros_like(acc_ref)
    m_ref[...] = jnp.full_like(m_ref, NEG)

    def one(kz, carry):
        attend_block(
            grid, kx, bl, first, heads, tile_len, kz, facts,
            kv_refs, own_ref, out_ref, q32_ref, acc_ref, m_ref,
        )
        return carry

    lax.fori_loop(0, grid.zs, one, 0)


def attend_block(grid, kx, bl, first, heads, tile_len, step, facts,
                 kv_refs, own_ref, out_ref, q32_ref, acc_ref, m_ref):
    block = grid.owner(facts.shard, kx, step)
    offset = jnp.int32(0)
    for b in range(grid.n):
        offset = offset + jnp.where(b < block, facts.length(b), 0)
    prompt = facts.prompt(block)
    valid = jnp.clip(facts.prompt_length(prompt) - facts.shard * tile_len, 0, tile_len)
    c2 = LOG2E / math.sqrt(HD)
    chunk = min(CHUNK, tile_len)
    width = heads * GR * HD

    rest = offset % 8
    window = q32_ref[pl.ds(pl.multiple_of(offset - rest, 8), bl + 8), :]
    window = pltpu.roll(window, jnp.where(rest == 0, 0, bl + 8 - rest), 0)
    queries = window[:bl].astype(jnp.bfloat16)

    def group(g, used):
        return jnp.concatenate(
            [queries[:used, (g * GR + r) * HD:(g * GR + r + 1) * HD] for r in range(GR)], axis=0
        )

    def with_ones(v):
        return jnp.concatenate([v, jnp.ones(v.shape, jnp.bfloat16)], axis=1)

    def sums(p, v):
        return jnp.dot(p, with_ones(v), preferred_element_type=jnp.float32)

    def keys(g, at, size):
        return kv_refs[g][prompt, pl.ds(at, size), :HD]

    def vals(g, at, size):
        return kv_refs[g][prompt, pl.ds(at, size), HD:]

    def put(g, used, acc, m):
        m = jnp.broadcast_to(m, (GR * used, HD))
        for r in range(GR):
            acc_ref[g, r * bl:r * bl + used] = acc[r * used:(r + 1) * used]
            m_ref[g, r * bl:r * bl + used] = m[r * used:(r + 1) * used]

    def update(g, s, seen, v):
        s = jnp.where(seen, s, NEG)
        before = m_ref[g][:, :1]
        m = jnp.maximum(before, jnp.max(s, axis=1, keepdims=True))
        p = jnp.where(seen, jnp.exp2((s - m) * c2), 0.0).astype(jnp.bfloat16)
        acc_ref[g] = acc_ref[g] * jnp.exp2((before - m) * c2) + sums(p, v)
        m_ref[g] = jnp.broadcast_to(m, m_ref.shape[1:])

    def exact():
        acc_ref[...] = jnp.zeros_like(acc_ref)
        m_ref[...] = jnp.full_like(m_ref, NEG)

        def one(c, carry):
            at = pl.multiple_of(c * chunk, chunk)
            for g in range(heads):
                s = dot_nt(group(g, bl), keys(g, at, chunk))
                here = lax.broadcasted_iota(jnp.int32, s.shape, 1) + at
                update(g, s, here < valid, vals(g, at, chunk))
            return carry

        lax.fori_loop(0, (valid + chunk - 1) // chunk, one, 0)

    length = facts.length(block)

    @pl.when(valid == 0)
    def _():
        acc_ref[...] = jnp.zeros_like(acc_ref)
        m_ref[...] = jnp.full_like(m_ref, NEG)

    step_of = min(PIECE, tile_len) // chunk

    def single_pass(used, count):
        items = [(g, c) for c in range(count) for g in range(heads)]
        q = [group(g, used) for g in range(heads)]
        peaks = [None] * heads
        accs = [None] * heads
        ahead = dot_nt(q[0], keys(0, 0, chunk))
        for i, (g, c) in enumerate(items):
            s = ahead
            if i + 1 < len(items):
                ng, nc = items[i + 1]
                ahead = dot_nt(q[ng], keys(ng, nc * chunk, chunk))
            if (c + 1) * chunk > (count - step_of) * chunk:
                here = lax.broadcasted_iota(jnp.int32, s.shape, 1) + c * chunk
                s = jnp.where(here < valid, s, NEG)
            if c == 0:
                peaks[g] = jnp.max(s, axis=1, keepdims=True)
            p = jnp.exp2((s - peaks[g]) * c2).astype(jnp.bfloat16)
            part = sums(p, vals(g, c * chunk, chunk))
            accs[g] = part if c == 0 else accs[g] + part
        for g in range(heads):
            put(g, used, accs[g], peaks[g])

    for count in range(step_of, tile_len // chunk + 1, step_of):
        for used in range(ROUND, bl + 1, ROUND):
            some_keys = (valid > (count - step_of) * chunk) & (valid <= count * chunk)
            some_rows = (length > used - ROUND) & (length <= used)
            pl.when(some_keys & some_rows)(functools.partial(single_pass, used, count))

    def own_part():
        @pl.when(step == 0)
        def _():
            for g in range(heads):
                base = (first + g) * 2 * HD
                s = dot_nt(group(g, bl), own_ref[0, :, base:base + HD])
                row = lax.broadcasted_iota(jnp.int32, s.shape, 0) % bl
                col = lax.broadcasted_iota(jnp.int32, s.shape, 1)
                update(g, s, col <= row, own_ref[0, :, base + HD:base + 2 * HD])

    def write():
        lane = lax.broadcasted_iota(jnp.int32, (bl, EXTRA), 1)
        total = jnp.zeros((bl, EXTRA), jnp.float32)
        peak = jnp.zeros((bl, EXTRA), jnp.float32)
        for g in range(heads):
            for r in range(GR):
                h = g * GR + r
                at = slice(r * bl, (r + 1) * bl)
                out_ref[step, :, h * HD:(h + 1) * HD] = acc_ref[g, at, :HD].astype(jnp.bfloat16)
                total = jnp.where(lane == h, acc_ref[g, at, HD:], total)
                peak = jnp.where(lane == h, m_ref[g, at], peak)
        out_ref[step, :, width:] = encode(peak * c2, total)
        return total

    if kx == 0:
        own_part()
    total = write()

    @pl.when(jnp.max(jnp.where(total < BIG, 0.0, 1.0)) > 0.5)
    def _():
        exact()
        if kx == 0:
            own_part()
        write()


def attend(grid, kx, meta, queries, coords, caches, own, first, heads):
    zs = grid.zs
    _, share, cols = queries[0].shape
    bl = own.shape[1]
    tile_len = caches[0].shape[1]
    width = heads * GR * HD + EXTRA
    whole = pl.BlockSpec(memory_space=pltpu.VMEM)
    return pl.pallas_call(
        functools.partial(attend_kernel, grid, kx, bl, share, first, heads, tile_len, coords),
        grid_spec=pltpu.PrefetchScalarGridSpec(
            num_scalar_prefetch=1,
            grid=(1,),
            in_specs=[whole] * (len(queries) + heads + 1),
            out_specs=whole,
            scratch_shapes=[
                pltpu.VMEM((grid.n * share + bl + 8, cols), jnp.float32),
                pltpu.VMEM((heads, GR * bl, 2 * HD), jnp.float32),
                pltpu.VMEM((heads, GR * bl, HD), jnp.float32),
            ],
        ),
        out_shape=jax.ShapeDtypeStruct((zs, bl, width), jnp.bfloat16),
        compiler_params=pltpu.CompilerParams(vmem_limit_bytes=20 * MIB),
        cost_estimate=pl.CostEstimate(
            flops=8 * zs * bl * cols * tile_len,
            bytes_accessed=2 * zs * tile_len * heads * 2 * HD,
            transcendentals=zs * bl * heads * GR * tile_len,
        ),
        name="attend",
    )(meta, *queries, *caches, own)


def finish_kernel(n, heads, bl, done, meta, *refs):
    sources, out_ref = refs[:-1], refs[-1]
    pieces = sources[done:]
    facts = Facts(n, meta)
    length = facts.length(facts.shard)
    row = lax.broadcasted_iota(jnp.int32, (bl, HD), 0)
    width = heads * GR * HD
    for c in range(done):
        out_ref[0, :, c * width:(c + 1) * width] = sources[c][0]
    parts, _, total = merge(pieces, heads * GR)
    for h in range(heads * GR):
        at = done * width + h * HD
        value = parts[h] / jnp.broadcast_to(total[:, h:h + 1], (bl, HD))
        out_ref[0, :, at:at + HD] = jnp.where(row < length, value, 0.0).astype(jnp.bfloat16)


def finish(n, meta, done, pieces, heads):
    bl = pieces[0].shape[0]
    whole = pl.BlockSpec(memory_space=pltpu.VMEM)
    sources = list(done) + list(pieces)
    return pl.pallas_call(
        functools.partial(finish_kernel, n, heads, bl, len(done)),
        grid_spec=pltpu.PrefetchScalarGridSpec(
            num_scalar_prefetch=1,
            grid=(1,),
            in_specs=[whole] * len(sources),
            out_specs=whole,
        ),
        out_shape=jax.ShapeDtypeStruct((1, bl, (len(done) + 1) * heads * GR * HD), jnp.bfloat16),
        compiler_params=pltpu.CompilerParams(vmem_limit_bytes=16 * MIB),
        name="finish",
    )(meta, *sources)


def shards(
    hidden_rows,
    carried,
    query_weight,
    response_cache,
    prompt_cache,
    prompt_lengths,
    response_lengths,
    block_prompts,
):
    grid = Grid(lax.axis_size("seq"))
    bl = hidden_rows.shape[1]
    local_kv = response_cache.shape[2] // (2 * HD)
    share = bl * 5 // 8
    chunks = 2 if local_kv % 2 == 0 else 1
    heads = local_kv // chunks
    part_cols = heads * GR * HD
    place = jnp.stack([lax.axis_index("sec"), lax.axis_index("seq")]).astype(jnp.int32)

    def after(value, done):
        return lax.optimization_barrier((value, done))[0]

    def fetched(head, done=()):
        return fetch_cache(grid.n, after(meta, done), prompt_cache, 2 * HD, head)

    handed = lax.ppermute(carried, "sec", [(0, 1)])
    depth = query_weight.shape[1]
    hidden = hidden_rows if depth % HD else fetch([hidden_rows])[0]
    slices = split(grid, place, hidden, handed, depth)
    later_place = after(place, slices[0])
    prompts = block_prompts[:, :, 0]
    meta = jnp.concatenate(
        [later_place] + [a[i] for a in (response_lengths, prompts) for i in range(2)]
        + [prompt_lengths]
    )
    weight, own = fetch([query_weight, response_cache])
    x = [slices[0]] + [None] * (grid.n - 1)
    for kz in reversed(range(grid.zs)):
        for kx in reversed(range(grid.xs)):
            k = kx * grid.zs + kz
            if k:
                x[k] = grid.swap(slices[k], kx, kz)
    part = project(grid, meta, x, weight, bl, share, chunks)
    part = [piece.reshape(grid.zs, share, part_cols) for piece in part]
    part = [part[c * grid.xs:(c + 1) * grid.xs] for c in range(chunks)]

    def narrow(value):
        return (value * 0.125).astype(jnp.float16)

    def widen(value):
        return value.astype(jnp.float32) * 8.0

    def both(first, second):
        return lax.optimization_barrier((first, second))

    def reduce_x(parts, done=()):
        got = [grid.swap(after(narrow(parts[kx]), done), kx, 0) for kx in range(1, grid.xs)]
        return functools.reduce(jnp.add, [parts[0]] + [widen(value) for value in got])

    def narrow_z(held):
        return [narrow(held[kz]) for kz in range(1, grid.zs)]

    def sum_z(held, sends, beside):
        got = [grid.swap(send, 0, kz + 1) for kz, send in enumerate(sends)]
        parts = [after(held[0], beside)] + [widen(value) for value in got]
        return functools.reduce(jnp.add, parts).astype(jnp.bfloat16)

    def gather_z(value):
        return [value] + [grid.swap(value, 0, kz) for kz in range(1, grid.zs)]

    def gather_x(value):
        return [value] + [grid.swap(value, kx, 0) for kx in range(1, grid.xs)]

    z_then_x = [[(kx, kz) for kz in range(grid.zs)] for kx in range(grid.xs)]
    x_then_z = [[(kx, kz) for kx in range(grid.xs)] for kz in range(grid.zs)]

    def call(c, kx, queries):
        return attend(
            grid, kx, meta, queries, x_then_z if c else z_then_x,
            caches[c * heads:(c + 1) * heads], own, c * heads, heads,
        )

    def call_far(c, queries):
        outs = [call(c, kx, queries) for kx in range(1, grid.xs)]
        return outs, [grid.swap(out, kx + 1, 0) for kx, out in enumerate(outs)]

    def send_z(merged):
        return [merged[0]] + [grid.swap(merged[kz], 0, kz) for kz in range(1, grid.zs)]

    half = (local_kv + 1) // 4
    caches = [fetched(head) for head in range(half)]
    part[0][0] = after(part[0][0], caches)
    held = reduce_x(part[0])
    sends = narrow_z(held)
    if chunks > 1:
        sends, part[1][1] = both(sends, part[1][1])
        later = reduce_x(part[1])
    caches += [fetched(head, sends) for head in range(half, heads)]
    mine = sum_z(held, sends, caches)
    column = gather_z(mine)
    if chunks > 1:
        caches += [fetched(head, mine) for head in range(heads, heads + half)]
        sends = narrow_z(after(later, mine))
        column = after(column, (caches, sends))
    queries = gather_x(jnp.stack(column))
    if chunks == 1:
        outs, mets = call_far(0, queries)
        queries[0] = after(queries[0], outs)
        pieces = send_z(merge_column([call(0, 0, queries)] + mets, heads * GR))
        return finish(grid.n, meta, [], pieces, heads)
    caches += [fetched(head, sends) for head in range(heads + half, local_kv)]
    mine = sum_z(later, sends, caches)
    queries[0] = after(queries[0], mine)
    near = jnp.stack(gather_x(mine))
    outs, mets = call_far(0, queries)
    near = after(near, outs)
    queries[0] = after(queries[0], near)
    later = gather_z(near)
    held = call(0, 0, queries)
    merged = merge_column([held] + mets, heads * GR)
    later[0] = after(later[0], merged)
    outs, mets = call_far(1, later)
    merged, later[0] = both(after(merged, outs), later[0])
    pieces = send_z(merged)
    held = call(1, 0, later)
    done = finish(grid.n, meta, [], pieces, heads)
    pieces = send_z(merge_column([held] + mets, heads * GR))
    return finish(grid.n, meta, [done], pieces, heads)


def solution(mesh):
    placed = (
        P("sec", "seq", None),
        P("sec", "seq", None),
        P("sec", "seq", "tp"),
        P("sec", "seq", "tp"),
        P("sec", None, "seq", "tp"),
        P(),
        P(),
        P(),
    )
    return jax.shard_map(
        shards, mesh=mesh, in_specs=placed, out_specs=P("sec", "seq", "tp"), check_vma=False
    )
```

profile of v0, /device:TPU:0, one launch (start us, length us, event | category | flops | bytes accessed | tf_op | source)
XLA Modules:
  0.0 122.5 jit_solution(4468991482344028020)
XLA Ops:
  0.0 2.4 %collective-permute-start = (bf16[1,64,5120]{2,1,0:T(8,128)(2,1)}, bf16[1,64,5120]{2,1,0:T(8,128)(2,1)S(1)}, u32[]{:S(2)}, u32[]{:S(2)}) collective-permute-start(bf16[1,64,5120]{2,1,0:T(8,128)(2,1)} %param.9), channel_id=1, source_target_pairs={{0,16},{1,17},{2,18},{3,19},{4,20},{5,21},{6,22},{7,23},{8,24},{9,... | collective-permute-start | bytes 1966088 | tf_op jit(solution)/shard_map/ppermute | solution.py:543
  2.4 1.1 fetch.2.hidden_ref
  3.6 0.7 collective-permute-done.handed_ref
  4.3 1.3 %split.1 = (bf16[64,640]{1,0:T(8,128)(2,1)S(1)}, bf16[64,640]{1,0:T(8,128)(2,1)S(1)}, bf16[64,640]{1,0:T(8,128)(2,1)S(1)}, bf16[64,640]{1,0:T(8,128)(2,1)}, bf16...) custom-call(s32[2]{0:T(128)S(1)} %pad_add_fusion.meta, ...), custom_call_target="tpu_custom_call" | custom-call | tf_op jit(solution)/shard_map/split/pallas_call | solution.py:77
  5.6 2.4 %collective-permute-start.1 = (bf16[64,640]{1,0:T(8,128)(2,1)S(1)}, bf16[64,640]{1,0:T(8,128)(2,1)S(1)}, u32[]{:S(2)}, u32[]{:S(2)}) collective-permute-start(bf16[64,640]{1,0:T(8,128)(2,1)S(1)} %get-tuple-element.58), channel_id=1, source_target_pairs={{0,4},{2,6},{4,0},{6,2},{8,12},{10,14},{12,8},{14,10},{1,5},{3,7},... | collective-permute-start | bytes 245768 | tf_op jit(solution)/shard_map/ppermute | solution.py:40
  8.0 2.6 %collective-permute-start.2 = (bf16[64,640]{1,0:T(8,128)(2,1)S(1)}, bf16[64,640]{1,0:T(8,128)(2,1)S(1)}, u32[]{:S(2)}, u32[]{:S(2)}) collective-permute-start(bf16[64,640]{1,0:T(8,128)(2,1)S(1)} %get-tuple-element.59), channel_id=1, source_target_pairs={{0,8},{2,10},{4,12},{6,14},{8,0},{10,2},{12,4},{14,6},{1,9},{3,11}... | collective-permute-start | bytes 245768 | tf_op jit(solution)/shard_map/ppermute | solution.py:40
  10.6 0.8 slice_bitcast_fusion.4
  11.3 1.7 %collective-permute-start.4 = (bf16[64,640]{1,0:T(8,128)(2,1)}, bf16[64,640]{1,0:T(8,128)(2,1)S(1)}, u32[]{:S(2)}, u32[]{:S(2)}) collective-permute-start(bf16[64,640]{1,0:T(8,128)(2,1)} %get-tuple-element.61), channel_id=1, source_target_pairs={{0,2},{2,0},{4,6},{6,4},{8,10},{10,8},{12,14},{14,12},{1,3},{3,1},... | collective-permute-start | bytes 245768 | tf_op jit(solution)/shard_map/ppermute | solution.py:40
  13.0 0.6 collective-permute-start.5
  13.7 4.4 %collective-permute-start.6 = (bf16[64,640]{1,0:T(8,128)(2,1)}, bf16[64,640]{1,0:T(8,128)(2,1)S(1)}, u32[]{:S(2)}, u32[]{:S(2)}) collective-permute-start(bf16[64,640]{1,0:T(8,128)(2,1)} %get-tuple-element.63), channel_id=1, source_target_pairs={{0,10},{2,8},{4,14},{6,12},{8,2},{10,0},{12,6},{14,4},{1,11},{3,9}... | collective-permute-start | bytes 245768 | tf_op jit(solution)/shard_map/ppermute | solution.py:40
  18.1 2.8 %collective-permute-start.7 = (bf16[64,640]{1,0:T(8,128)(2,1)S(1)}, bf16[64,640]{1,0:T(8,128)(2,1)S(1)}, u32[]{:S(2)}, u32[]{:S(2)}) collective-permute-start(bf16[64,640]{1,0:T(8,128)(2,1)S(1)} %get-tuple-element.64), channel_id=1, source_target_pairs={{0,14},{2,12},{4,10},{6,8},{8,6},{10,4},{12,2},{14,0},{1,15},{3,13... | collective-permute-start | bytes 245768 | tf_op jit(solution)/shard_map/ppermute | solution.py:40
  21.0 0.7 slice_bitcast_fusion.2
  21.6 1.8 %fetch.3 = (bf16[1,640,2048]{2,1,0:T(8,128)(2,1)S(1)}, bf16[1,64,1024]{2,1,0:T(8,128)(2,1)S(1)}) custom-call(bf16[1,640,2048]{2,1,0:T(8,128)(2,1)} %refs_0_.3, bf16[1,64,1024]{2,1,0:T(8,128)(2,1)} %refs_1_.1), custom_call_target="tpu_custom_call" | custom-call | bytes 2752512 | tf_op jit(solution)/shard_map/fetch/pallas_call | solution.py:115
  23.4 0.7 concatenate.3.meta
  24.2 1.2 collective-permute-done.7.refs_7_
  25.4 2.7 %project.1 = (f32[160,1024]{1,0:T(8,128)S(1)}, f32[160,1024]{1,0:T(8,128)S(1)}, f32[160,1024]{1,0:T(8,128)S(1)}, f32[160,1024]{1,0:T(8,128)S(1)}) custom-call(s32[42]{0:T(128)S(1)} %concatenate.3.meta, bf16[64,640]{1,0:T(8,128)(2,1)S(1)} %get-tuple-element.56.refs_0_, bf16[64,640]{1,0:T(8,128)(2,1)S(1)} %collective-permute-done.1.refs_1_, ...), custom_call_target="tpu_custom_call" | custom-call | flops 838860800 | bytes 5242880 | tf_op jit(solution)/shard_map/project/pallas_call | solution.py:213
  28.7 3.6 %fetch_cache.4.refs_2_ = bf16[8,2048,256]{2,1,0:T(8,128)(2,1)S(1)} custom-call(s32[42]{0:T(128)S(1)} %concatenate.3.meta, bf16[1,8,2048,1024]{3,2,1,0:T(8,128)(2,1)} %cache_ref.7), custom_call_target="tpu_custom_call" | custom-call | bytes 8388608 | tf_op jit(solution)/shard_map/fetch_cache/pallas_call | solution.py:150
  32.3 4.1 %collective-permute-done.8 = f16[4,40,1024]{2,1,0:T(8,128)(2,1)S(1)} collective-permute-done((f16[4,40,1024]{2,1,0:T(8,128)(2,1)S(1)}, f16[4,40,1024]{2,1,0:T(8,128)(2,1)S(1)}, u32[]{:S(2)}, u32[]{:S(2)}) %collective-permute-start.8) | collective-permute-done | bytes 327712 | tf_op jit(solution)/shard_map/ppermute | solution.py:40
  37.1 3.2 %collective-permute-start.9 = (f16[40,1024]{1,0:T(8,128)(2,1)S(1)}, f16[40,1024]{1,0:T(8,128)(2,1)S(1)}, u32[]{:S(2)}, u32[]{:S(2)}) collective-permute-start(f16[40,1024]{1,0:T(8,128)(2,1)S(1)} %get-tuple-element.70), channel_id=1, source_target_pairs={{0,4},{2,6},{4,0},{6,2},{8,12},{10,14},{12,8},{14,10},{1,5},{3,7},... | collective-permute-start | bytes 245768 | tf_op jit(solution)/shard_map/ppermute | solution.py:40
  40.3 0.6 collective-permute-start.10
  40.9 1.7 %collective-permute-start.11 = (f16[40,1024]{1,0:T(8,128)(2,1)S(1)}, f16[40,1024]{1,0:T(8,128)(2,1)S(1)}, u32[]{:S(2)}, u32[]{:S(2)}) collective-permute-start(f16[40,1024]{1,0:T(8,128)(2,1)S(1)} %get-tuple-element.72), channel_id=1, source_target_pairs={{0,12},{2,14},{4,8},{6,10},{8,4},{10,6},{12,0},{14,2},{1,13},{3,15... | collective-permute-start | bytes 245768 | tf_op jit(solution)/shard_map/ppermute | solution.py:40
  42.6 3.6 %fetch_cache.5.refs_3_ = bf16[8,2048,256]{2,1,0:T(8,128)(2,1)S(1)} custom-call(s32[42]{0:T(128)S(1)} %concatenate.3.meta, bf16[1,8,2048,1024]{3,2,1,0:T(8,128)(2,1)} %cache_ref.7), custom_call_target="tpu_custom_call" | custom-call | bytes 8388608 | tf_op jit(solution)/shard_map/fetch_cache/pallas_call | solution.py:150
  46.2 2.1 %collective-permute-done.10 = f16[40,1024]{1,0:T(8,128)(2,1)S(1)} collective-permute-done((f16[40,1024]{1,0:T(8,128)(2,1)S(1)}, f16[40,1024]{1,0:T(8,128)(2,1)S(1)}, u32[]{:S(2)}, u32[]{:S(2)}) %collective-permute-start.10) | collective-permute-done | bytes 81952 | tf_op jit(solution)/shard_map/ppermute | solution.py:40
  48.4 1.7 %collective-permute-start.14 = (bf16[40,1024]{1,0:T(8,128)(2,1)S(1)}, bf16[40,1024]{1,0:T(8,128)(2,1)S(1)}, u32[]{:S(2)}, u32[]{:S(2)}) collective-permute-start(bf16[40,1024]{1,0:T(8,128)(2,1)S(1)} %add_convert_fusion.1), channel_id=1, source_target_pairs={{0,12},{2,14},{4,8},{6,10},{8,4},{10,6},{12,0},{14,2},{1,13},{3,15... | collective-permute-start | bytes 245768 | tf_op jit(solution)/shard_map/ppermute | solution.py:40
  50.1 1.4 %collective-permute-start.13 = (bf16[40,1024]{1,0:T(8,128)(2,1)S(1)}, bf16[40,1024]{1,0:T(8,128)(2,1)S(1)}, u32[]{:S(2)}, u32[]{:S(2)}) collective-permute-start(bf16[40,1024]{1,0:T(8,128)(2,1)S(1)} %add_convert_fusion.1), channel_id=1, source_target_pairs={{0,8},{2,10},{4,12},{6,14},{8,0},{10,2},{12,4},{14,6},{1,9},{3,11}... | collective-permute-start | bytes 245768 | tf_op jit(solution)/shard_map/ppermute | solution.py:40
  51.5 1.4 %collective-permute-start.12 = (bf16[40,1024]{1,0:T(8,128)(2,1)S(1)}, bf16[40,1024]{1,0:T(8,128)(2,1)S(1)}, u32[]{:S(2)}, u32[]{:S(2)}) collective-permute-start(bf16[40,1024]{1,0:T(8,128)(2,1)S(1)} %add_convert_fusion.1), channel_id=1, source_target_pairs={{0,4},{2,6},{4,0},{6,2},{8,12},{10,14},{12,8},{14,10},{1,5},{3,7},... | collective-permute-start | bytes 245768 | tf_op jit(solution)/shard_map/ppermute | solution.py:40
  52.8 3.6 %fetch_cache.6.refs_4_ = bf16[8,2048,256]{2,1,0:T(8,128)(2,1)S(1)} custom-call(s32[42]{0:T(128)S(1)} %concatenate.3.meta, bf16[1,8,2048,1024]{3,2,1,0:T(8,128)(2,1)} %cache_ref.7), custom_call_target="tpu_custom_call" | custom-call | bytes 8388608 | tf_op jit(solution)/shard_map/fetch_cache/pallas_call | solution.py:150
  56.6 1.0 collective-permute-start.18
  57.6 1.0 collective-permute-start.17
  58.6 2.4 %collective-permute-start.16 = (f16[40,1024]{1,0:T(8,128)(2,1)S(1)}, f16[40,1024]{1,0:T(8,128)(2,1)S(1)}, u32[]{:S(2)}, u32[]{:S(2)}) collective-permute-start(f16[40,1024]{1,0:T(8,128)(2,1)S(1)} %get-tuple-element.109), channel_id=1, source_target_pairs={{0,4},{2,6},{4,0},{6,2},{8,12},{10,14},{12,8},{14,10},{1,5},{3,7},... | collective-permute-start | bytes 245768 | tf_op jit(solution)/shard_map/ppermute | solution.py:40
  61.1 1.8 %collective-permute-start.20 = (bf16[4,40,1024]{2,1,0:T(8,128)(2,1)S(1)}, bf16[4,40,1024]{2,1,0:T(8,128)(2,1)S(1)}, u32[]{:S(2)}, u32[]{:S(2)}) collective-permute-start(bf16[4,40,1024]{2,1,0:T(8,128)(2,1)S(1)} %pad_maximum_fusion.refs_0_), channel_id=1, source_target_pairs={{0,2},{2,0},{4,6},{6,4},{8,10},{10,8},{12,14},{14,12},{1,3},{3,1},... | collective-permute-start | bytes 983048 | tf_op jit(solution)/shard_map/ppermute | solution.py:40
  62.9 3.6 %fetch_cache.7.refs_5_ = bf16[8,2048,256]{2,1,0:T(8,128)(2,1)S(1)} custom-call(s32[42]{0:T(128)S(1)} %concatenate.3.meta, bf16[1,8,2048,1024]{3,2,1,0:T(8,128)(2,1)} %cache_ref.7), custom_call_target="tpu_custom_call" | custom-call | bytes 8388608 | tf_op jit(solution)/shard_map/fetch_cache/pallas_call | solution.py:150
  67.0 2.2 %collective-permute-done.20.refs_1_ = bf16[4,40,1024]{2,1,0:T(8,128)(2,1)S(1)} collective-permute-done((bf16[4,40,1024]{2,1,0:T(8,128)(2,1)S(1)}, bf16[4,40,1024]{2,1,0:T(8,128)(2,1)S(1)}, u32[]{:S(2)}, u32[]{:S(2)}) %collective-permute-start.20) | collective-permute-done | bytes 327712 | tf_op jit(solution)/shard_map/ppermute | solution.py:40
  69.1 6.7 %attend.4 = bf16[4,64,1152]{2,1,0:T(8,128)(2,1)S(1)} custom-call(s32[42]{0:T(128)S(1)} %concatenate.3.meta, bf16[4,40,1024]{2,1,0:T(8,128)(2,1)S(1)} %pad_maximum_fusion.refs_0_, bf16[4,40,1024]{2,1,0:T(8,128)(2,1)S(1)} %collective-permute-done.20.refs_1_, bf16[8,2048,256]{2,1,0:T(8,128)(2,1)S(1)} %fetch_cache.4.refs_2_, ...), custom_call_target="tpu_custom_call" | custom-call | flops 4294967296 | bytes 8388608 | tf_op jit(solution)/shard_map/attend/pallas_call | solution.py:460
  75.8 1.4 %collective-permute-start.21 = (bf16[4,64,1152]{2,1,0:T(8,128)(2,1)S(1)}, bf16[4,64,1152]{2,1,0:T(8,128)(2,1)S(1)}, u32[]{:S(2)}, u32[]{:S(2)}) collective-permute-start(bf16[4,64,1152]{2,1,0:T(8,128)(2,1)S(1)} %attend.4), channel_id=1, source_target_pairs={{0,2},{2,0},{4,6},{6,4},{8,10},{10,8},{12,14},{14,12},{1,3},{3,1},... | collective-permute-start | bytes 1769480 | tf_op jit(solution)/shard_map/ppermute | solution.py:40
  77.9 3.8 %collective-permute-start.22 = (bf16[2,40,1024]{2,1,0:T(8,128)(2,1)S(1)}, bf16[2,40,1024]{2,1,0:T(8,128)(2,1)S(1)}, u32[]{:S(2)}, u32[]{:S(2)}) collective-permute-start(bf16[2,40,1024]{2,1,0:T(8,128)(2,1)S(1)} %pad_maximum_fusion.1.refs_0_), channel_id=1, source_target_pairs={{0,4},{2,6},{4,0},{6,2},{8,12},{10,14},{12,8},{14,10},{1,5},{3,7},... | collective-permute-start | bytes 491528 | tf_op jit(solution)/shard_map/ppermute | solution.py:40
  81.7 7.3 %attend.5.refs_0_ = bf16[4,64,1152]{2,1,0:T(8,128)(2,1)S(1)} custom-call(s32[42]{0:T(128)S(1)} %concatenate.3.meta, bf16[4,40,1024]{2,1,0:T(8,128)(2,1)S(1)} %pad_maximum_fusion.refs_0_, bf16[4,40,1024]{2,1,0:T(8,128)(2,1)S(1)} %collective-permute-done.20.refs_1_, bf16[8,2048,256]{2,1,0:T(8,128)(2,1)S(1)} %fetch_cache.4.refs_2_, ...), custom_call_target="tpu_custom_call" | custom-call | flops 4294967296 | bytes 8388608 | tf_op jit(solution)/shard_map/attend/pallas_call | solution.py:460
  89.0 1.5 %merge.2 = (bf16[64,1152]{1,0:T(8,128)(2,1)S(1)}, bf16[64,1152]{1,0:T(8,128)(2,1)S(1)}, bf16[64,1152]{1,0:T(8,128)(2,1)S(1)}, bf16[64,1152]{1,0:T(8,128)(2,1)S(1)}) custom-call(bf16[4,64,1152]{2,1,0:T(8,128)(2,1)S(1)} %attend.5.refs_0_, bf16[4,64,1152]{2,1,0:T(8,128)(2,1)S(1)} %collective-permute-done.21.refs_1_), custom_call_target="tpu_custom_call" | custom-call | tf_op jit(solution)/shard_map/merge/pallas_call | solution.py:285
  90.5 6.7 %attend.6 = bf16[4,64,1152]{2,1,0:T(8,128)(2,1)S(1)} custom-call(s32[42]{0:T(128)S(1)} %concatenate.3.meta, bf16[2,40,1024]{2,1,0:T(8,128)(2,1)S(1)} %pad_maximum_fusion.1.refs_0_, bf16[2,40,1024]{2,1,0:T(8,128)(2,1)S(1)} %collective-permute-done.22.refs_1_, bf16[2,40,1024]{2,1,0:T(8,128)(2,1)S(1)} %collective-permute-done.23.refs_2_, ...), custom_call_target="tpu_custom_call" | custom-call | flops 4294967296 | bytes 8388608 | tf_op jit(solution)/shard_map/attend/pallas_call | solution.py:460
  97.2 0.8 collective-permute-start.28
  98.0 4.4 %collective-permute-start.27 = (bf16[64,1152]{1,0:T(8,128)(2,1)S(1)}, bf16[64,1152]{1,0:T(8,128)(2,1)S(1)}, u32[]{:S(2)}, u32[]{:S(2)}) collective-permute-start(bf16[64,1152]{1,0:T(8,128)(2,1)S(1)} %get-tuple-element.101), channel_id=1, source_target_pairs={{0,12},{2,14},{4,8},{6,10},{8,4},{10,6},{12,0},{14,2},{1,13},{3,15... | collective-permute-start | bytes 442376 | tf_op jit(solution)/shard_map/ppermute | solution.py:40
  102.4 7.3 %attend.7.refs_0_ = bf16[4,64,1152]{2,1,0:T(8,128)(2,1)S(1)} custom-call(s32[42]{0:T(128)S(1)} %concatenate.3.meta, bf16[2,40,1024]{2,1,0:T(8,128)(2,1)S(1)} %pad_maximum_fusion.1.refs_0_, bf16[2,40,1024]{2,1,0:T(8,128)(2,1)S(1)} %collective-permute-done.22.refs_1_, bf16[2,40,1024]{2,1,0:T(8,128)(2,1)S(1)} %collective-permute-done.23.refs_2_, ...), custom_call_target="tpu_custom_call" | custom-call | flops 4294967296 | bytes 8388608 | tf_op jit(solution)/shard_map/attend/pallas_call | solution.py:460
  109.7 1.5 %merge.3 = (bf16[64,1152]{1,0:T(8,128)(2,1)S(1)}, bf16[64,1152]{1,0:T(8,128)(2,1)S(1)}, bf16[64,1152]{1,0:T(8,128)(2,1)S(1)}, bf16[64,1152]{1,0:T(8,128)(2,1)S(1)}) custom-call(bf16[4,64,1152]{2,1,0:T(8,128)(2,1)S(1)} %attend.7.refs_0_, bf16[4,64,1152]{2,1,0:T(8,128)(2,1)S(1)} %collective-permute-done.28.refs_1_), custom_call_target="tpu_custom_call" | custom-call | tf_op jit(solution)/shard_map/merge/pallas_call | solution.py:285
  111.4 4.3 %collective-permute-start.31 = (bf16[64,1152]{1,0:T(8,128)(2,1)S(1)}, bf16[64,1152]{1,0:T(8,128)(2,1)S(1)}, u32[]{:S(2)}, u32[]{:S(2)}) collective-permute-start(bf16[64,1152]{1,0:T(8,128)(2,1)S(1)} %get-tuple-element.106), channel_id=1, source_target_pairs={{0,12},{2,14},{4,8},{6,10},{8,4},{10,6},{12,0},{14,2},{1,13},{3,15... | collective-permute-start | bytes 442376 | tf_op jit(solution)/shard_map/ppermute | solution.py:40
  115.7 1.1 finish.2.refs_0_
  116.8 1.0 collective-permute-done.29.refs_2_
  117.9 2.7 %collective-permute-done.30.refs_3_ = bf16[64,1152]{1,0:T(8,128)(2,1)S(1)} collective-permute-done((bf16[64,1152]{1,0:T(8,128)(2,1)S(1)}, bf16[64,1152]{1,0:T(8,128)(2,1)S(1)}, u32[]{:S(2)}, u32[]{:S(2)}) %collective-permute-start.30) | collective-permute-done | bytes 147488 | tf_op jit(solution)/shard_map/ppermute | solution.py:40
  120.6 1.8 %finish.3 = bf16[1,64,2048]{2,1,0:T(8,128)(2,1)} custom-call(s32[42]{0:T(128)S(1)} %concatenate.3.meta, bf16[1,64,1024]{2,1,0:T(8,128)(2,1)S(1)} %finish.2.refs_0_, bf16[64,1152]{1,0:T(8,128)(2,1)S(1)} %get-tuple-element.103.refs_1_, bf16[64,1152]{1,0:T(8,128)(2,1)S(1)} %collective-permute-done.29.refs_2_, ...), custom_call_target="tpu_custom_call" | custom-call | tf_op jit(solution)/shard_map/finish/pallas_call | solution.py:504
  (47 shorter events, 2.9 us)
Async XLA Ops:
  0.0 4.3 %collective-permute-start = (bf16[1,64,5120]{2,1,0:T(8,128)(2,1)}, bf16[1,64,5120]{2,1,0:T(8,128)(2,1)S(1)}, u32[]{:S(2)}, u32[]{:S(2)}) collective-permute-start(bf16[1,64,5120]{2,1,0:T(8,128)(2,1)} %param.9), channel_id=1, source_target_pairs={{0,16},{1,17},{2,18},{3,19},{4,20},{5,21},{6,22},{7,23},{8,24},{9,... | collective-permute-start | bytes 1966088 | tf_op jit(solution)/shard_map/ppermute | solution.py:543
  5.6 8.1 %collective-permute-start.1 = (bf16[64,640]{1,0:T(8,128)(2,1)S(1)}, bf16[64,640]{1,0:T(8,128)(2,1)S(1)}, u32[]{:S(2)}, u32[]{:S(2)}) collective-permute-start(bf16[64,640]{1,0:T(8,128)(2,1)S(1)} %get-tuple-element.58), channel_id=1, source_target_pairs={{0,4},{2,6},{4,0},{6,2},{8,12},{10,14},{12,8},{14,10},{1,5},{3,7},... | collective-permute-start | bytes 245768 | tf_op jit(solution)/shard_map/ppermute | solution.py:40
  8.0 10.1 %collective-permute-start.2 = (bf16[64,640]{1,0:T(8,128)(2,1)S(1)}, bf16[64,640]{1,0:T(8,128)(2,1)S(1)}, u32[]{:S(2)}, u32[]{:S(2)}) collective-permute-start(bf16[64,640]{1,0:T(8,128)(2,1)S(1)} %get-tuple-element.59), channel_id=1, source_target_pairs={{0,8},{2,10},{4,12},{6,14},{8,0},{10,2},{12,4},{14,6},{1,9},{3,11}... | collective-permute-start | bytes 245768 | tf_op jit(solution)/shard_map/ppermute | solution.py:40
  11.3 12.8 %collective-permute-start.3 = (bf16[64,640]{1,0:T(8,128)(2,1)}, bf16[64,640]{1,0:T(8,128)(2,1)S(1)}, u32[]{:S(2)}, u32[]{:S(2)}) collective-permute-start(bf16[64,640]{1,0:T(8,128)(2,1)} %get-tuple-element.60), channel_id=1, source_target_pairs={{0,12},{2,14},{4,8},{6,10},{8,4},{10,6},{12,0},{14,2},{1,13},{3,15... | collective-permute-start | bytes 245768 | tf_op jit(solution)/shard_map/ppermute | solution.py:40
  11.3 12.8 %collective-permute-start.4 = (bf16[64,640]{1,0:T(8,128)(2,1)}, bf16[64,640]{1,0:T(8,128)(2,1)S(1)}, u32[]{:S(2)}, u32[]{:S(2)}) collective-permute-start(bf16[64,640]{1,0:T(8,128)(2,1)} %get-tuple-element.61), channel_id=1, source_target_pairs={{0,2},{2,0},{4,6},{6,4},{8,10},{10,8},{12,14},{14,12},{1,3},{3,1},... | collective-permute-start | bytes 245768 | tf_op jit(solution)/shard_map/ppermute | solution.py:40
  13.0 11.1 %collective-permute-start.5 = (bf16[64,640]{1,0:T(8,128)(2,1)}, bf16[64,640]{1,0:T(8,128)(2,1)S(1)}, u32[]{:S(2)}, u32[]{:S(2)}) collective-permute-start(bf16[64,640]{1,0:T(8,128)(2,1)} %get-tuple-element.62), channel_id=1, source_target_pairs={{0,6},{2,4},{4,2},{6,0},{8,14},{10,12},{12,10},{14,8},{1,7},{3,5},... | collective-permute-start | bytes 245768 | tf_op jit(solution)/shard_map/ppermute | solution.py:40
  13.7 10.5 %collective-permute-start.6 = (bf16[64,640]{1,0:T(8,128)(2,1)}, bf16[64,640]{1,0:T(8,128)(2,1)S(1)}, u32[]{:S(2)}, u32[]{:S(2)}) collective-permute-start(bf16[64,640]{1,0:T(8,128)(2,1)} %get-tuple-element.63), channel_id=1, source_target_pairs={{0,10},{2,8},{4,14},{6,12},{8,2},{10,0},{12,6},{14,4},{1,11},{3,9}... | collective-permute-start | bytes 245768 | tf_op jit(solution)/shard_map/ppermute | solution.py:40
  18.1 7.2 %collective-permute-start.7 = (bf16[64,640]{1,0:T(8,128)(2,1)S(1)}, bf16[64,640]{1,0:T(8,128)(2,1)S(1)}, u32[]{:S(2)}, u32[]{:S(2)}) collective-permute-start(bf16[64,640]{1,0:T(8,128)(2,1)S(1)} %get-tuple-element.64), channel_id=1, source_target_pairs={{0,14},{2,12},{4,10},{6,8},{8,6},{10,4},{12,2},{14,0},{1,15},{3,13... | collective-permute-start | bytes 245768 | tf_op jit(solution)/shard_map/ppermute | solution.py:40
  28.1 8.3 %collective-permute-start.8 = (f16[4,40,1024]{2,1,0:T(8,128)(2,1)S(1)}, f16[4,40,1024]{2,1,0:T(8,128)(2,1)S(1)}, u32[]{:S(2)}, u32[]{:S(2)}) collective-permute-start(f16[4,40,1024]{2,1,0:T(8,128)(2,1)S(1)} %bitcast.39), channel_id=1, source_target_pairs={{0,2},{2,0},{4,6},{6,4},{8,10},{10,8},{12,14},{14,12},{1,3},{3,1},... | collective-permute-start | bytes 983048 | tf_op jit(solution)/shard_map/ppermute | solution.py:40
  36.7 19.7 %collective-permute-start.15 = (f16[4,40,1024]{2,1,0:T(8,128)(2,1)S(1)}, f16[4,40,1024]{2,1,0:T(8,128)(2,1)S(1)}, u32[]{:S(2)}, u32[]{:S(2)}) collective-permute-start(f16[4,40,1024]{2,1,0:T(8,128)(2,1)S(1)} %multiply_convert_fusion), channel_id=1, source_target_pairs={{0,2},{2,0},{4,6},{6,4},{8,10},{10,8},{12,14},{14,12},{1,3},{3,1},... | collective-permute-start | bytes 983048 | tf_op jit(solution)/shard_map/ppermute | solution.py:40
  37.1 9.1 %collective-permute-start.9 = (f16[40,1024]{1,0:T(8,128)(2,1)S(1)}, f16[40,1024]{1,0:T(8,128)(2,1)S(1)}, u32[]{:S(2)}, u32[]{:S(2)}) collective-permute-start(f16[40,1024]{1,0:T(8,128)(2,1)S(1)} %get-tuple-element.70), channel_id=1, source_target_pairs={{0,4},{2,6},{4,0},{6,2},{8,12},{10,14},{12,8},{14,10},{1,5},{3,7},... | collective-permute-start | bytes 245768 | tf_op jit(solution)/shard_map/ppermute | solution.py:40
  40.3 8.0 %collective-permute-start.10 = (f16[40,1024]{1,0:T(8,128)(2,1)S(1)}, f16[40,1024]{1,0:T(8,128)(2,1)S(1)}, u32[]{:S(2)}, u32[]{:S(2)}) collective-permute-start(f16[40,1024]{1,0:T(8,128)(2,1)S(1)} %get-tuple-element.71), channel_id=1, source_target_pairs={{0,8},{2,10},{4,12},{6,14},{8,0},{10,2},{12,4},{14,6},{1,9},{3,11}... | collective-permute-start | bytes 245768 | tf_op jit(solution)/shard_map/ppermute | solution.py:40
  40.9 7.4 %collective-permute-start.11 = (f16[40,1024]{1,0:T(8,128)(2,1)S(1)}, f16[40,1024]{1,0:T(8,128)(2,1)S(1)}, u32[]{:S(2)}, u32[]{:S(2)}) collective-permute-start(f16[40,1024]{1,0:T(8,128)(2,1)S(1)} %get-tuple-element.72), channel_id=1, source_target_pairs={{0,12},{2,14},{4,8},{6,10},{8,4},{10,6},{12,0},{14,2},{1,13},{3,15... | collective-permute-start | bytes 245768 | tf_op jit(solution)/shard_map/ppermute | solution.py:40
  48.4 10.3 %collective-permute-start.14 = (bf16[40,1024]{1,0:T(8,128)(2,1)S(1)}, bf16[40,1024]{1,0:T(8,128)(2,1)S(1)}, u32[]{:S(2)}, u32[]{:S(2)}) collective-permute-start(bf16[40,1024]{1,0:T(8,128)(2,1)S(1)} %add_convert_fusion.1), channel_id=1, source_target_pairs={{0,12},{2,14},{4,8},{6,10},{8,4},{10,6},{12,0},{14,2},{1,13},{3,15... | collective-permute-start | bytes 245768 | tf_op jit(solution)/shard_map/ppermute | solution.py:40
  50.1 11.0 %collective-permute-start.13 = (bf16[40,1024]{1,0:T(8,128)(2,1)S(1)}, bf16[40,1024]{1,0:T(8,128)(2,1)S(1)}, u32[]{:S(2)}, u32[]{:S(2)}) collective-permute-start(bf16[40,1024]{1,0:T(8,128)(2,1)S(1)} %add_convert_fusion.1), channel_id=1, source_target_pairs={{0,8},{2,10},{4,12},{6,14},{8,0},{10,2},{12,4},{14,6},{1,9},{3,11}... | collective-permute-start | bytes 245768 | tf_op jit(solution)/shard_map/ppermute | solution.py:40
  51.5 9.6 %collective-permute-start.12 = (bf16[40,1024]{1,0:T(8,128)(2,1)S(1)}, bf16[40,1024]{1,0:T(8,128)(2,1)S(1)}, u32[]{:S(2)}, u32[]{:S(2)}) collective-permute-start(bf16[40,1024]{1,0:T(8,128)(2,1)S(1)} %add_convert_fusion.1), channel_id=1, source_target_pairs={{0,4},{2,6},{4,0},{6,2},{8,12},{10,14},{12,8},{14,10},{1,5},{3,7},... | collective-permute-start | bytes 245768 | tf_op jit(solution)/shard_map/ppermute | solution.py:40
  56.6 9.9 %collective-permute-start.18 = (f16[40,1024]{1,0:T(8,128)(2,1)S(1)}, f16[40,1024]{1,0:T(8,128)(2,1)S(1)}, u32[]{:S(2)}, u32[]{:S(2)}) collective-permute-start(f16[40,1024]{1,0:T(8,128)(2,1)S(1)} %get-tuple-element.107), channel_id=1, source_target_pairs={{0,12},{2,14},{4,8},{6,10},{8,4},{10,6},{12,0},{14,2},{1,13},{3,15... | collective-permute-start | bytes 245768 | tf_op jit(solution)/shard_map/ppermute | solution.py:40
  57.6 8.9 %collective-permute-start.17 = (f16[40,1024]{1,0:T(8,128)(2,1)S(1)}, f16[40,1024]{1,0:T(8,128)(2,1)S(1)}, u32[]{:S(2)}, u32[]{:S(2)}) collective-permute-start(f16[40,1024]{1,0:T(8,128)(2,1)S(1)} %get-tuple-element.108), channel_id=1, source_target_pairs={{0,8},{2,10},{4,12},{6,14},{8,0},{10,2},{12,4},{14,6},{1,9},{3,11}... | collective-permute-start | bytes 245768 | tf_op jit(solution)/shard_map/ppermute | solution.py:40
  58.6 7.9 %collective-permute-start.16 = (f16[40,1024]{1,0:T(8,128)(2,1)S(1)}, f16[40,1024]{1,0:T(8,128)(2,1)S(1)}, u32[]{:S(2)}, u32[]{:S(2)}) collective-permute-start(f16[40,1024]{1,0:T(8,128)(2,1)S(1)} %get-tuple-element.109), channel_id=1, source_target_pairs={{0,4},{2,6},{4,0},{6,2},{8,12},{10,14},{12,8},{14,10},{1,5},{3,7},... | collective-permute-start | bytes 245768 | tf_op jit(solution)/shard_map/ppermute | solution.py:40
  61.1 8.0 %collective-permute-start.20 = (bf16[4,40,1024]{2,1,0:T(8,128)(2,1)S(1)}, bf16[4,40,1024]{2,1,0:T(8,128)(2,1)S(1)}, u32[]{:S(2)}, u32[]{:S(2)}) collective-permute-start(bf16[4,40,1024]{2,1,0:T(8,128)(2,1)S(1)} %pad_maximum_fusion.refs_0_), channel_id=1, source_target_pairs={{0,2},{2,0},{4,6},{6,4},{8,10},{10,8},{12,14},{14,12},{1,3},{3,1},... | collective-permute-start | bytes 983048 | tf_op jit(solution)/shard_map/ppermute | solution.py:40
  66.6 10.6 %collective-permute-start.19 = (bf16[40,1024]{1,0:T(8,128)(2,1)S(1)}, bf16[40,1024]{1,0:T(8,128)(2,1)S(1)}, u32[]{:S(2)}, u32[]{:S(2)}) collective-permute-start(bf16[40,1024]{1,0:T(8,128)(2,1)S(1)} %add_convert_fusion), channel_id=1, source_target_pairs={{0,2},{2,0},{4,6},{6,4},{8,10},{10,8},{12,14},{14,12},{1,3},{3,1},... | collective-permute-start | bytes 245768 | tf_op jit(solution)/shard_map/ppermute | solution.py:40
  75.8 13.1 %collective-permute-start.21 = (bf16[4,64,1152]{2,1,0:T(8,128)(2,1)S(1)}, bf16[4,64,1152]{2,1,0:T(8,128)(2,1)S(1)}, u32[]{:S(2)}, u32[]{:S(2)}) collective-permute-start(bf16[4,64,1152]{2,1,0:T(8,128)(2,1)S(1)} %attend.4), channel_id=1, source_target_pairs={{0,2},{2,0},{4,6},{6,4},{8,10},{10,8},{12,14},{14,12},{1,3},{3,1},... | collective-permute-start | bytes 1769480 | tf_op jit(solution)/shard_map/ppermute | solution.py:40
  77.2 13.2 %collective-permute-start.24 = (bf16[2,40,1024]{2,1,0:T(8,128)(2,1)S(1)}, bf16[2,40,1024]{2,1,0:T(8,128)(2,1)S(1)}, u32[]{:S(2)}, u32[]{:S(2)}) collective-permute-start(bf16[2,40,1024]{2,1,0:T(8,128)(2,1)S(1)} %pad_maximum_fusion.1.refs_0_), channel_id=1, source_target_pairs={{0,12},{2,14},{4,8},{6,10},{8,4},{10,6},{12,0},{14,2},{1,13},{3,15... | collective-permute-start | bytes 491528 | tf_op jit(solution)/shard_map/ppermute | solution.py:40
  77.3 13.2 %collective-permute-start.23 = (bf16[2,40,1024]{2,1,0:T(8,128)(2,1)S(1)}, bf16[2,40,1024]{2,1,0:T(8,128)(2,1)S(1)}, u32[]{:S(2)}, u32[]{:S(2)}) collective-permute-start(bf16[2,40,1024]{2,1,0:T(8,128)(2,1)S(1)} %pad_maximum_fusion.1.refs_0_), channel_id=1, source_target_pairs={{0,8},{2,10},{4,12},{6,14},{8,0},{10,2},{12,4},{14,6},{1,9},{3,11}... | collective-permute-start | bytes 491528 | tf_op jit(solution)/shard_map/ppermute | solution.py:40
  77.9 12.6 %collective-permute-start.22 = (bf16[2,40,1024]{2,1,0:T(8,128)(2,1)S(1)}, bf16[2,40,1024]{2,1,0:T(8,128)(2,1)S(1)}, u32[]{:S(2)}, u32[]{:S(2)}) collective-permute-start(bf16[2,40,1024]{2,1,0:T(8,128)(2,1)S(1)} %pad_maximum_fusion.1.refs_0_), channel_id=1, source_target_pairs={{0,4},{2,6},{4,0},{6,2},{8,12},{10,14},{12,8},{14,10},{1,5},{3,7},... | collective-permute-start | bytes 491528 | tf_op jit(solution)/shard_map/ppermute | solution.py:40
  97.2 12.5 %collective-permute-start.28 = (bf16[4,64,1152]{2,1,0:T(8,128)(2,1)S(1)}, bf16[4,64,1152]{2,1,0:T(8,128)(2,1)S(1)}, u32[]{:S(2)}, u32[]{:S(2)}) collective-permute-start(bf16[4,64,1152]{2,1,0:T(8,128)(2,1)S(1)} %attend.6), channel_id=1, source_target_pairs={{0,2},{2,0},{4,6},{6,4},{8,10},{10,8},{12,14},{14,12},{1,3},{3,1},... | collective-permute-start | bytes 1769480 | tf_op jit(solution)/shard_map/ppermute | solution.py:40
  98.0 13.4 %collective-permute-start.25 = (bf16[64,1152]{1,0:T(8,128)(2,1)S(1)}, bf16[64,1152]{1,0:T(8,128)(2,1)S(1)}, u32[]{:S(2)}, u32[]{:S(2)}) collective-permute-start(bf16[64,1152]{1,0:T(8,128)(2,1)S(1)} %get-tuple-element.99), channel_id=1, source_target_pairs={{0,4},{2,6},{4,0},{6,2},{8,12},{10,14},{12,8},{14,10},{1,5},{3,7},... | collective-permute-start | bytes 442376 | tf_op jit(solution)/shard_map/ppermute | solution.py:40
  98.0 17.7 %collective-permute-start.26 = (bf16[64,1152]{1,0:T(8,128)(2,1)S(1)}, bf16[64,1152]{1,0:T(8,128)(2,1)S(1)}, u32[]{:S(2)}, u32[]{:S(2)}) collective-permute-start(bf16[64,1152]{1,0:T(8,128)(2,1)S(1)} %get-tuple-element.100), channel_id=1, source_target_pairs={{0,8},{2,10},{4,12},{6,14},{8,0},{10,2},{12,4},{14,6},{1,9},{3,11}... | collective-permute-start | bytes 442376 | tf_op jit(solution)/shard_map/ppermute | solution.py:40
  98.0 17.7 %collective-permute-start.27 = (bf16[64,1152]{1,0:T(8,128)(2,1)S(1)}, bf16[64,1152]{1,0:T(8,128)(2,1)S(1)}, u32[]{:S(2)}, u32[]{:S(2)}) collective-permute-start(bf16[64,1152]{1,0:T(8,128)(2,1)S(1)} %get-tuple-element.101), channel_id=1, source_target_pairs={{0,12},{2,14},{4,8},{6,10},{8,4},{10,6},{12,0},{14,2},{1,13},{3,15... | collective-permute-start | bytes 442376 | tf_op jit(solution)/shard_map/ppermute | solution.py:40
  111.2 6.6 %collective-permute-start.29 = (bf16[64,1152]{1,0:T(8,128)(2,1)S(1)}, bf16[64,1152]{1,0:T(8,128)(2,1)S(1)}, u32[]{:S(2)}, u32[]{:S(2)}) collective-permute-start(bf16[64,1152]{1,0:T(8,128)(2,1)S(1)} %get-tuple-element.104), channel_id=1, source_target_pairs={{0,4},{2,6},{4,0},{6,2},{8,12},{10,14},{12,8},{14,10},{1,5},{3,7},... | collective-permute-start | bytes 442376 | tf_op jit(solution)/shard_map/ppermute | solution.py:40
  111.3 9.3 %collective-permute-start.30 = (bf16[64,1152]{1,0:T(8,128)(2,1)S(1)}, bf16[64,1152]{1,0:T(8,128)(2,1)S(1)}, u32[]{:S(2)}, u32[]{:S(2)}) collective-permute-start(bf16[64,1152]{1,0:T(8,128)(2,1)S(1)} %get-tuple-element.105), channel_id=1, source_target_pairs={{0,8},{2,10},{4,12},{6,14},{8,0},{10,2},{12,4},{14,6},{1,9},{3,11}... | collective-permute-start | bytes 442376 | tf_op jit(solution)/shard_map/ppermute | solution.py:40
  111.4 9.2 %collective-permute-start.31 = (bf16[64,1152]{1,0:T(8,128)(2,1)S(1)}, bf16[64,1152]{1,0:T(8,128)(2,1)S(1)}, u32[]{:S(2)}, u32[]{:S(2)}) collective-permute-start(bf16[64,1152]{1,0:T(8,128)(2,1)S(1)} %get-tuple-element.106), channel_id=1, source_target_pairs={{0,12},{2,14},{4,8},{6,10},{8,4},{10,6},{12,0},{14,2},{1,13},{3,15... | collective-permute-start | bytes 442376 | tf_op jit(solution)/shard_map/ppermute | solution.py:40
where the time goes:
time: 123 us; the launch traced here: 122 us
  Pallas kernels  55.1 us (45%)
  starting transfers between devices  50 us (41%)
  waiting for transfers between devices  14.1 us (11%)
  local copies, waits for them, and re-layouts  2.18 us (2%)
    ppermute x31, starting transfers between devices, swap(): return lax.ppermute(value, 'seq', pairs)  47.6 us
    pallas_call x4, Pallas kernels, attend(): pl.pallas_call(functools.partial(attend_kernel, grid, kx, bl, share, firs...  28 us
    pallas_call x4, Pallas kernels, fetch_cache(): pl.pallas_call(functools.partial(fetch_cache_kernel, n, chunk, width, fir...  14.3 us
    ppermute x31, waiting for transfers between devices, swap(): return lax.ppermute(value, 'seq', pairs)  13.4 us
    pallas_call x2, Pallas kernels, merge_column(): pl.pallas_call(functools.partial(merge_kernel, zs, heads), out_shape=[jax...  3.01 us
    pallas_call x2, Pallas kernels, finish(): pl.pallas_call(functools.partial(finish_kernel, n, heads, bl, len(done)),...  2.96 us
    pallas_call x2, Pallas kernels, fetch(): pl.pallas_call(fetch_kernel, in_specs=[anywhere] * len(arrays), out_specs...  2.85 us
    pallas_call x1, Pallas kernels, project(): pl.pallas_call(functools.partial(project_kernel, grid, bl, share), grid_s...  2.71 us
  transfers between devices with their start and end apart: 32, of which 7 were waited for; matrix products, arithmetic and copies ran while one was open for 2% of the time, Pallas kernels for 35%

commit v1 on v0

--- a/solution.py
+++ b/solution.py
@@ -41,18 +41,18 @@
 
 
 class Facts:
-    def __init__(self, n, meta):
-        self.n, self.meta = n, meta
-        self.section, self.shard = meta[0], meta[1]
+    def __init__(self, meta):
+        self.meta = meta
+        self.section, self.shard = meta[5, 0], meta[5, 1]
 
     def length(self, block):
-        return self.meta[2 + self.section * self.n + block]
+        return self.meta[self.section, block]
 
     def prompt(self, block):
-        return self.meta[2 + (2 + self.section) * self.n + block]
+        return self.meta[2 + self.section, block]
 
     def prompt_length(self, prompt):
-        return self.meta[2 + 4 * self.n + prompt]
+        return self.meta[4, prompt]
 
 
 def split_kernel(grid, depth, meta, hidden_ref, handed_ref, *out_refs):
@@ -127,7 +127,7 @@
 
 def fetch_cache_kernel(n, chunk, width, first, meta, cache_ref, kv_ref, sem):
     count, tile_len = kv_ref.shape[:2]
-    facts = Facts(n, meta)
+    facts = Facts(meta)
     moves = []
     for p in range(count):
         asked = facts.prompt(0) == p
@@ -172,7 +172,7 @@
 
     @pl.when(pl.program_id(0) == 0)
     def _():
-        facts = Facts(grid.n, meta)
+        facts = Facts(meta)
         shard = facts.shard
         offset = jnp.int32(0)
         for b in range(grid.n):
@@ -290,11 +290,12 @@
     )(*sources)
 
 
-def attend_kernel(grid, kx, bl, share, first, heads, tile_len, coords, meta, *refs):
+def attend_kernel(grid, kx, bl, share, heads, tile_len, coords, meta, *refs):
     q_refs, refs = refs[:len(coords)], refs[len(coords):]
     kv_refs, refs = refs[:heads], refs[heads:]
-    own_ref, out_ref, q32_ref, acc_ref, m_ref = refs
-    facts = Facts(grid.n, meta)
+    out_ref, own_q_ref = refs[0], refs[1] if kx == 0 else None
+    q32_ref, acc_ref, m_ref, over_ref = refs[-4:]
+    facts = Facts(meta)
     shard = facts.shard
     rows = grid.n * share
     for q_ref, places in zip(q_refs, coords):
@@ -302,21 +303,47 @@
             at = pl.multiple_of(grid.owner(shard, fx, fz) * share, 8)
             q32_ref[pl.ds(at, share), :] = q_ref[i].astype(jnp.float32)
     q32_ref[rows:, :] = jnp.zeros((bl + 8, q32_ref.shape[1]), jnp.float32)
-    acc_ref[...] = jnp.zeros_like(acc_ref)
-    m_ref[...] = jnp.full_like(m_ref, NEG)
 
     def one(kz, carry):
         attend_block(
-            grid, kx, bl, first, heads, tile_len, kz, facts,
-            kv_refs, own_ref, out_ref, q32_ref, acc_ref, m_ref,
+            grid, kx, bl, heads, tile_len, kz, facts,
+            kv_refs, out_ref, own_q_ref, q32_ref, acc_ref, m_ref, over_ref,
         )
         return carry
 
     lax.fori_loop(0, grid.zs, one, 0)
 
 
-def attend_block(grid, kx, bl, first, heads, tile_len, step, facts,
-                 kv_refs, own_ref, out_ref, q32_ref, acc_ref, m_ref):
+def group_rows(queries, g, used):
+    return jnp.concatenate(
+        [queries[:used, (g * GR + r) * HD:(g * GR + r + 1) * HD] for r in range(GR)], axis=0
+    )
+
+
+def sums(p, v):
+    v = jnp.concatenate([v, jnp.ones(v.shape, jnp.bfloat16)], axis=1)
+    return jnp.dot(p, v, preferred_element_type=jnp.float32)
+
+
+def write_partial(accs, peaks, store, c2):
+    used = accs[0].shape[0] // GR
+    lane = lax.broadcasted_iota(jnp.int32, (used, EXTRA), 1)
+    total = jnp.zeros((used, EXTRA), jnp.float32)
+    peak = jnp.zeros((used, EXTRA), jnp.float32)
+    for g, (acc, m) in enumerate(zip(accs, peaks)):
+        for r in range(GR):
+            h = g * GR + r
+            at = slice(r * used, (r + 1) * used)
+            store(slice(h * HD, (h + 1) * HD), acc[at, :HD].astype(jnp.bfloat16))
+            total = jnp.where(lane == h, acc[at, HD:], total)
+            peak = jnp.where(lane == h, m[at], peak)
+    width = len(accs) * GR * HD
+    store(slice(width, width + EXTRA), encode(peak * c2, total))
+    return total
+
+
+def attend_block(grid, kx, bl, heads, tile_len, step, facts,
+                 kv_refs, out_ref, own_q_ref, q32_ref, acc_ref, m_ref, over_ref):
     block = grid.owner(facts.shard, kx, step)
     offset = jnp.int32(0)
     for b in range(grid.n):
@@ -332,16 +359,11 @@
     window = pltpu.roll(window, jnp.where(rest == 0, 0, bl + 8 - rest), 0)
     queries = window[:bl].astype(jnp.bfloat16)
 
-    def group(g, used):
-        return jnp.concatenate(
-            [queries[:used, (g * GR + r) * HD:(g * GR + r + 1) * HD] for r in range(GR)], axis=0
-        )
-
-    def with_ones(v):
-        return jnp.concatenate([v, jnp.ones(v.shape, jnp.bfloat16)], axis=1)
-
-    def sums(p, v):
-        return jnp.dot(p, with_ones(v), preferred_element_type=jnp.float32)
+    group = functools.partial(group_rows, queries)
+    if kx == 0:
+        @pl.when(step == 0)
+        def _():
+            own_q_ref[...] = queries
 
     def keys(g, at, size):
         return kv_refs[g][prompt, pl.ds(at, size), :HD]
@@ -349,11 +371,8 @@
     def vals(g, at, size):
         return kv_refs[g][prompt, pl.ds(at, size), HD:]
 
-    def put(g, used, acc, m):
-        m = jnp.broadcast_to(m, (GR * used, HD))
-        for r in range(GR):
-            acc_ref[g, r * bl:r * bl + used] = acc[r * used:(r + 1) * used]
-            m_ref[g, r * bl:r * bl + used] = m[r * used:(r + 1) * used]
+    def store(used, columns, value):
+        out_ref[step, :used, columns] = value
 
     def update(g, s, seen, v):
         s = jnp.where(seen, s, NEG)
@@ -376,13 +395,19 @@
             return carry
 
         lax.fori_loop(0, (valid + chunk - 1) // chunk, one, 0)
+        write_partial(
+            [acc_ref[g] for g in range(heads)], [m_ref[g] for g in range(heads)],
+            functools.partial(store, bl), c2,
+        )
 
     length = facts.length(block)
 
     @pl.when(valid == 0)
     def _():
-        acc_ref[...] = jnp.zeros_like(acc_ref)
-        m_ref[...] = jnp.full_like(m_ref, NEG)
+        over_ref[0] = 0
+        out_ref[step, :, :width] = jnp.zeros((bl, width), jnp.bfloat16)
+        none = jnp.zeros((bl, EXTRA), jnp.float32)
+        out_ref[step, :, width:] = encode(none + NEG, none)
 
     step_of = min(PIECE, tile_len) // chunk
 
@@ -405,8 +430,12 @@
             p = jnp.exp2((s - peaks[g]) * c2).astype(jnp.bfloat16)
             part = sums(p, vals(g, c * chunk, chunk))
             accs[g] = part if c == 0 else accs[g] + part
-        for g in range(heads):
-            put(g, used, accs[g], peaks[g])
+        total = write_partial(
+            accs, [jnp.broadcast_to(m, (GR * used, EXTRA)) for m in peaks],
+            functools.partial(store, used), c2,
+        )
+
+        over_ref[0] = (jnp.max(jnp.where(total < BIG, 0.0, 1.0)) > 0.5).astype(jnp.int32)
 
     for count in range(step_of, tile_len // chunk + 1, step_of):
         for used in range(ROUND, bl + 1, ROUND):
@@ -414,63 +443,63 @@
             some_rows = (length > used - ROUND) & (length <= used)
             pl.when(some_keys & some_rows)(functools.partial(single_pass, used, count))
 
-    def own_part():
-        @pl.when(step == 0)
-        def _():
-            for g in range(heads):
-                base = (first + g) * 2 * HD
-                s = dot_nt(group(g, bl), own_ref[0, :, base:base + HD])
-                row = lax.broadcasted_iota(jnp.int32, s.shape, 0) % bl
-                col = lax.broadcasted_iota(jnp.int32, s.shape, 1)
-                update(g, s, col <= row, own_ref[0, :, base + HD:base + 2 * HD])
-
-    def write():
-        lane = lax.broadcasted_iota(jnp.int32, (bl, EXTRA), 1)
-        total = jnp.zeros((bl, EXTRA), jnp.float32)
-        peak = jnp.zeros((bl, EXTRA), jnp.float32)
-        for g in range(heads):
-            for r in range(GR):
-                h = g * GR + r
-                at = slice(r * bl, (r + 1) * bl)
-                out_ref[step, :, h * HD:(h + 1) * HD] = acc_ref[g, at, :HD].astype(jnp.bfloat16)
-                total = jnp.where(lane == h, acc_ref[g, at, HD:], total)
-                peak = jnp.where(lane == h, m_ref[g, at], peak)
-        out_ref[step, :, width:] = encode(peak * c2, total)
-        return total
-
-    if kx == 0:
-        own_part()
-    total = write()
-
-    @pl.when(jnp.max(jnp.where(total < BIG, 0.0, 1.0)) > 0.5)
-    def _():
-        exact()
-        if kx == 0:
-            own_part()
-        write()
-
-
-def attend(grid, kx, meta, queries, coords, caches, own, first, heads):
+    pl.when(over_ref[0] > 0)(exact)
+
+
+def own_kernel(first, heads, bl, q_ref, own_ref, out_ref):
+    c2 = LOG2E / math.sqrt(HD)
+    queries = q_ref[...]
+    accs, peaks = [], []
+    for g in range(heads):
+        base = (first + g) * 2 * HD
+        s = dot_nt(group_rows(queries, g, bl), own_ref[0, :, base:base + HD])
+        row = lax.broadcasted_iota(jnp.int32, s.shape, 0) % bl
+        seen = lax.broadcasted_iota(jnp.int32, s.shape, 1) <= row
+        s = jnp.where(seen, s, NEG)
+        m = jnp.max(s, axis=1, keepdims=True)
+        p = jnp.where(seen, jnp.exp2((s - m) * c2), 0.0).astype(jnp.bfloat16)
+        accs.append(sums(p, own_ref[0, :, base + HD:base + 2 * HD]))
+        peaks.append(jnp.broadcast_to(m, (GR * bl, EXTRA)))
+
+    def store(columns, value):
+        out_ref[:, columns] = value
+
+    write_partial(accs, peaks, store, c2)
+
+
+def attend_own(queries, own, first, heads):
+    bl = own.shape[1]
+    return pl.pallas_call(
+        functools.partial(own_kernel, first, heads, bl),
+        out_shape=jax.ShapeDtypeStruct((bl, heads * GR * HD + EXTRA), jnp.bfloat16),
+        compiler_params=pltpu.CompilerParams(vmem_limit_bytes=16 * MIB),
+        name="attend_own",
+    )(queries, own)
+
+
+def attend(grid, kx, meta, queries, coords, caches, bl, heads):
     zs = grid.zs
     _, share, cols = queries[0].shape
-    bl = own.shape[1]
     tile_len = caches[0].shape[1]
     width = heads * GR * HD + EXTRA
     whole = pl.BlockSpec(memory_space=pltpu.VMEM)
+    shapes = [(zs, bl, width)] + [(bl, cols)] * (kx == 0)
+    outs = [jax.ShapeDtypeStruct(shape, jnp.bfloat16) for shape in shapes]
     return pl.pallas_call(
-        functools.partial(attend_kernel, grid, kx, bl, share, first, heads, tile_len, coords),
+        functools.partial(attend_kernel, grid, kx, bl, share, heads, tile_len, coords),
         grid_spec=pltpu.PrefetchScalarGridSpec(
             num_scalar_prefetch=1,
             grid=(1,),
-            in_specs=[whole] * (len(queries) + heads + 1),
-            out_specs=whole,
+            in_specs=[whole] * (len(queries) + heads),
+            out_specs=[whole] * len(outs),
             scratch_shapes=[
                 pltpu.VMEM((grid.n * share + bl + 8, cols), jnp.float32),
                 pltpu.VMEM((heads, GR * bl, 2 * HD), jnp.float32),
                 pltpu.VMEM((heads, GR * bl, HD), jnp.float32),
+                pltpu.SMEM((1,), jnp.int32),
             ],
         ),
-        out_shape=jax.ShapeDtypeStruct((zs, bl, width), jnp.bfloat16),
+        out_shape=outs,
         compiler_params=pltpu.CompilerParams(vmem_limit_bytes=20 * MIB),
         cost_estimate=pl.CostEstimate(
             flops=8 * zs * bl * cols * tile_len,
@@ -478,13 +507,13 @@
             transcendentals=zs * bl * heads * GR * tile_len,
         ),
         name="attend",
-    )(meta, *queries, *caches, own)
-
-
-def finish_kernel(n, heads, bl, done, meta, *refs):
+    )(meta, *queries, *caches)
+
+
+def finish_kernel(heads, bl, done, meta, *refs):
     sources, out_ref = refs[:-1], refs[-1]
     pieces = sources[done:]
-    facts = Facts(n, meta)
+    facts = Facts(meta)
     length = facts.length(facts.shard)
     row = lax.broadcasted_iota(jnp.int32, (bl, HD), 0)
     width = heads * GR * HD
@@ -497,12 +526,12 @@
         out_ref[0, :, at:at + HD] = jnp.where(row < length, value, 0.0).astype(jnp.bfloat16)
 
 
-def finish(n, meta, done, pieces, heads):
+def finish(meta, done, pieces, heads):
     bl = pieces[0].shape[0]
     whole = pl.BlockSpec(memory_space=pltpu.VMEM)
     sources = list(done) + list(pieces)
     return pl.pallas_call(
-        functools.partial(finish_kernel, n, heads, bl, len(done)),
+        functools.partial(finish_kernel, heads, bl, len(done)),
         grid_spec=pltpu.PrefetchScalarGridSpec(
             num_scalar_prefetch=1,
             grid=(1,),
@@ -544,13 +573,15 @@
     depth = query_weight.shape[1]
     hidden = hidden_rows if depth % HD else fetch([hidden_rows])[0]
     slices = split(grid, place, hidden, handed, depth)
-    later_place = after(place, slices[0])
-    prompts = block_prompts[:, :, 0]
-    meta = jnp.concatenate(
-        [later_place] + [a[i] for a in (response_lengths, prompts) for i in range(2)]
-        + [prompt_lengths]
-    )
-    weight, own = fetch([query_weight, response_cache])
+    n = grid.n
+    lane = lax.broadcasted_iota(jnp.int32, (1, n), 1)
+    section, shard = after((lax.axis_index("sec"), lax.axis_index("seq")), handed)
+    meta = jnp.concatenate([
+        response_lengths, block_prompts[:, :, 0],
+        jnp.pad(prompt_lengths, (0, n - prompt_lengths.shape[0]))[None],
+        jnp.where(lane == 0, section, shard).astype(jnp.int32),
+    ])
+    weight, own = fetch([query_weight, after(response_cache, handed)])
     x = [slices[0]] + [None] * (grid.n - 1)
     for kz in reversed(range(grid.zs)):
         for kx in reversed(range(grid.xs)):
@@ -594,11 +625,11 @@
     def call(c, kx, queries):
         return attend(
             grid, kx, meta, queries, x_then_z if c else z_then_x,
-            caches[c * heads:(c + 1) * heads], own, c * heads, heads,
+            caches[c * heads:(c + 1) * heads], bl, heads,
         )
 
     def call_far(c, queries):
-        outs = [call(c, kx, queries) for kx in range(1, grid.xs)]
+        outs = [call(c, kx, queries)[0] for kx in range(1, grid.xs)]
         return outs, [grid.swap(out, kx + 1, 0) for kx, out in enumerate(outs)]
 
     def send_z(merged):
@@ -623,8 +654,10 @@
     if chunks == 1:
         outs, mets = call_far(0, queries)
         queries[0] = after(queries[0], outs)
-        pieces = send_z(merge_column([call(0, 0, queries)] + mets, heads * GR))
-        return finish(grid.n, meta, [], pieces, heads)
+        held, own_q = call(0, 0, queries)
+        pieces = send_z(merge_column([held] + mets, heads * GR))
+        pieces.append(attend_own(own_q, own, 0, heads))
+        return finish(meta, [], pieces, heads)
     caches += [fetched(head, sends) for head in range(heads + half, local_kv)]
     mine = sum_z(later, sends, caches)
     queries[0] = after(queries[0], mine)
@@ -633,16 +666,18 @@
     near = after(near, outs)
     queries[0] = after(queries[0], near)
     later = gather_z(near)
-    held = call(0, 0, queries)
+    held, own_q = call(0, 0, queries)
     merged = merge_column([held] + mets, heads * GR)
     later[0] = after(later[0], merged)
     outs, mets = call_far(1, later)
     merged, later[0] = both(after(merged, outs), later[0])
     pieces = send_z(merged)
-    held = call(1, 0, later)
-    done = finish(grid.n, meta, [], pieces, heads)
-    pieces = send_z(merge_column([held] + mets, heads * GR))
-    return finish(grid.n, meta, [done], pieces, heads)
+    held, later_q = call(1, 0, later)
+    merged = merge_column([held] + mets, heads * GR)
+    own_q, later_q = after((own_q, later_q), merged)
+    done = finish(meta, [], pieces + [attend_own(own_q, own, 0, heads)], heads)
+    pieces = send_z(merged) + [attend_own(later_q, own, heads, heads)]
+    return finish(meta, [done], pieces, heads)
 
 
 def solution(mesh):

time: 123 us -> 119 us (0.967)
  Pallas kernels: 55.1 us -> 52 us
  waiting for transfers between devices: 14.1 us -> 16.4 us
  local copies, waits for them, and re-layouts: 2.18 us -> 0.01 us
  starting transfers between devices: 50 us -> 48.3 us
    pallas_call x4, Pallas kernels: 14.3 us -> 11.9 us  [fetch_cache(): pl.pallas_call(functools.partial(fetch_cache_kernel, n, chunk, width, fir...]
    ppermute x31, waiting for transfers between devices: 13.4 us -> 15.7 us  [swap(): return lax.ppermute(value, 'seq', pairs)]
    ppermute x31, starting transfers between devices: 47.6 us -> 45.9 us  [swap(): return lax.ppermute(value, 'seq', pairs)]
    squeeze x2 -> x0, local copies, waits for them, and re-layouts: 1.43 us -> none  [shards(): a[i]]
    pallas_call x6 -> x8, Pallas kernels: 31 us -> 30.7 us  [the longest x4 26 us: attend(): pl.pallas_call(functools.partial(attend_kernel, grid, kx, bl, share, head...]
  transfers between devices with their start and end apart: 32 -> 32, of which waited for: 7 -> 7; matrix products, arithmetic and copies ran while one was open for 2% -> 1% of each run, Pallas kernels for 35% -> 34%
where the time goes in v1:
time: 119 us
  Pallas kernels  52 us (44%)
  starting transfers between devices  48.3 us (41%)
  waiting for transfers between devices  16.4 us (14%)
  other arithmetic  1.41 us (1%)
    ppermute x31, starting transfers between devices, swap(): return lax.ppermute(value, 'seq', pairs)  45.9 us
    pallas_call x4, Pallas kernels, attend(): pl.pallas_call(functools.partial(attend_kernel, grid, kx, bl, share, head...  26 us
    ppermute x31, waiting for transfers between devices, swap(): return lax.ppermute(value, 'seq', pairs)  15.7 us
    pallas_call x4, Pallas kernels, fetch_cache(): pl.pallas_call(functools.partial(fetch_cache_kernel, n, chunk, width, fir...  11.9 us
    pallas_call x2, Pallas kernels, finish(): pl.pallas_call(functools.partial(finish_kernel, heads, bl, len(done)), gr...  3.27 us
    pallas_call x2, Pallas kernels, merge_column(): pl.pallas_call(functools.partial(merge_kernel, zs, heads), out_shape=[jax...  3.01 us
    pallas_call x2, Pallas kernels, fetch(): pl.pallas_call(fetch_kernel, in_specs=[anywhere] * len(arrays), out_specs...  2.85 us
    pallas_call x1, Pallas kernels, project(): pl.pallas_call(functools.partial(project_kernel, grid, bl, share), grid_s...  2.79 us
  transfers between devices with their start and end apart: 32, of which 7 were waited for; matrix products, arithmetic and copies ran while one was open for 1% of the time, Pallas kernels for 34%

profile of v1, /device:TPU:0, one launch (start us, length us, event | category | flops | bytes accessed | tf_op | source)
XLA Modules:
  0.0 118.5 jit_solution(5456818162308237524)
XLA Ops:
  0.0 2.4 %collective-permute-start = (bf16[1,64,5120]{2,1,0:T(8,128)(2,1)}, bf16[1,64,5120]{2,1,0:T(8,128)(2,1)S(1)}, u32[]{:S(2)}, u32[]{:S(2)}) collective-permute-start(bf16[1,64,5120]{2,1,0:T(8,128)(2,1)} %param.9), channel_id=1, source_target_pairs={{0,16},{1,17},{2,18},{3,19},{4,20},{5,21},{6,22},{7,23},{8,24},{9,... | collective-permute-start | bytes 1966088 | tf_op jit(solution)/shard_map/ppermute | solution.py:572
  2.4 1.1 fetch.2.hidden_ref
  3.6 0.7 collective-permute-done.handed_ref
  4.3 0.7 split.1
  5.0 2.5 %collective-permute-start.1 = (bf16[64,640]{1,0:T(8,128)(2,1)S(1)}, bf16[64,640]{1,0:T(8,128)(2,1)S(1)}, u32[]{:S(2)}, u32[]{:S(2)}) collective-permute-start(bf16[64,640]{1,0:T(8,128)(2,1)S(1)} %get-tuple-element.67), channel_id=1, source_target_pairs={{0,4},{2,6},{4,0},{6,2},{8,12},{10,14},{12,8},{14,10},{1,5},{3,7},... | collective-permute-start | bytes 245768 | tf_op jit(solution)/shard_map/ppermute | solution.py:40
  7.5 2.6 %collective-permute-start.2 = (bf16[64,640]{1,0:T(8,128)(2,1)S(1)}, bf16[64,640]{1,0:T(8,128)(2,1)S(1)}, u32[]{:S(2)}, u32[]{:S(2)}) collective-permute-start(bf16[64,640]{1,0:T(8,128)(2,1)S(1)} %get-tuple-element.68), channel_id=1, source_target_pairs={{0,8},{2,10},{4,12},{6,14},{8,0},{10,2},{12,4},{14,6},{1,9},{3,11}... | collective-permute-start | bytes 245768 | tf_op jit(solution)/shard_map/ppermute | solution.py:40
  10.1 1.7 %collective-permute-start.4 = (bf16[64,640]{1,0:T(8,128)(2,1)S(1)}, bf16[64,640]{1,0:T(8,128)(2,1)S(1)}, u32[]{:S(2)}, u32[]{:S(2)}) collective-permute-start(bf16[64,640]{1,0:T(8,128)(2,1)S(1)} %get-tuple-element.70), channel_id=1, source_target_pairs={{0,2},{2,0},{4,6},{6,4},{8,10},{10,8},{12,14},{14,12},{1,3},{3,1},... | collective-permute-start | bytes 245768 | tf_op jit(solution)/shard_map/ppermute | solution.py:40
  11.8 0.6 collective-permute-start.5
  12.4 1.8 %fetch.3 = (bf16[1,640,2048]{2,1,0:T(8,128)(2,1)S(1)}, bf16[1,64,1024]{2,1,0:T(8,128)(2,1)S(1)}) custom-call(bf16[1,640,2048]{2,1,0:T(8,128)(2,1)} %refs_0_.3, bf16[1,64,1024]{2,1,0:T(8,128)(2,1)} %refs_1_), custom_call_target="tpu_custom_call" | custom-call | bytes 2752512 | tf_op jit(solution)/shard_map/fetch/pallas_call | solution.py:115
  14.2 4.5 %collective-permute-start.6 = (bf16[64,640]{1,0:T(8,128)(2,1)S(1)}, bf16[64,640]{1,0:T(8,128)(2,1)S(1)}, u32[]{:S(2)}, u32[]{:S(2)}) collective-permute-start(bf16[64,640]{1,0:T(8,128)(2,1)S(1)} %get-tuple-element.72), channel_id=1, source_target_pairs={{0,10},{2,8},{4,14},{6,12},{8,2},{10,0},{12,6},{14,4},{1,11},{3,9}... | collective-permute-start | bytes 245768 | tf_op jit(solution)/shard_map/ppermute | solution.py:40
  18.7 1.9 %collective-permute-start.7 = (bf16[64,640]{1,0:T(8,128)(2,1)S(1)}, bf16[64,640]{1,0:T(8,128)(2,1)S(1)}, u32[]{:S(2)}, u32[]{:S(2)}) collective-permute-start(bf16[64,640]{1,0:T(8,128)(2,1)S(1)} %get-tuple-element.73), channel_id=1, source_target_pairs={{0,14},{2,12},{4,10},{6,8},{8,6},{10,4},{12,2},{14,0},{1,15},{3,13... | collective-permute-start | bytes 245768 | tf_op jit(solution)/shard_map/ppermute | solution.py:40
  20.6 0.7 pad_add_fusion.meta
  21.3 2.5 %collective-permute-done.6.refs_6_ = bf16[64,640]{1,0:T(8,128)(2,1)S(1)} collective-permute-done((bf16[64,640]{1,0:T(8,128)(2,1)S(1)}, bf16[64,640]{1,0:T(8,128)(2,1)S(1)}, u32[]{:S(2)}, u32[]{:S(2)}) %collective-permute-start.6) | collective-permute-done | bytes 81952 | tf_op jit(solution)/shard_map/ppermute | solution.py:40
  23.8 2.1 %collective-permute-done.7.refs_7_ = bf16[64,640]{1,0:T(8,128)(2,1)S(1)} collective-permute-done((bf16[64,640]{1,0:T(8,128)(2,1)S(1)}, bf16[64,640]{1,0:T(8,128)(2,1)S(1)}, u32[]{:S(2)}, u32[]{:S(2)}) %collective-permute-start.7) | collective-permute-done | bytes 81952 | tf_op jit(solution)/shard_map/ppermute | solution.py:40
  25.9 2.8 %project.1 = (f32[160,1024]{1,0:T(8,128)S(1)}, f32[160,1024]{1,0:T(8,128)S(1)}, f32[160,1024]{1,0:T(8,128)S(1)}, f32[160,1024]{1,0:T(8,128)S(1)}) custom-call(s32[6,8]{1,0:T(8,128)S(1)} %pad_add_fusion.meta, bf16[64,640]{1,0:T(8,128)(2,1)S(1)} %get-tuple-element.66.refs_0_, bf16[64,640]{1,0:T(8,128)(2,1)S(1)} %collective-permute-done.1.refs_1_, ...), custom_call_target="tpu_custom_call" | custom-call | flops 838860800 | bytes 5242880 | tf_op jit(solution)/shard_map/project/pallas_call | solution.py:213
  28.8 0.6 collective-permute-start.8
  29.4 3.0 %fetch_cache.4.refs_2_ = bf16[8,2048,256]{2,1,0:T(8,128)(2,1)S(1)} custom-call(s32[6,8]{1,0:T(8,128)S(1)} %pad_add_fusion.meta, bf16[1,8,2048,1024]{3,2,1,0:T(8,128)(2,1)} %cache_ref.7), custom_call_target="tpu_custom_call" | custom-call | bytes 8388608 | tf_op jit(solution)/shard_map/fetch_cache/pallas_call | solution.py:150
  32.4 4.3 %collective-permute-done.8 = f16[4,40,1024]{2,1,0:T(8,128)(2,1)S(1)} collective-permute-done((f16[4,40,1024]{2,1,0:T(8,128)(2,1)S(1)}, f16[4,40,1024]{2,1,0:T(8,128)(2,1)S(1)}, u32[]{:S(2)}, u32[]{:S(2)}) %collective-permute-start.8) | collective-permute-done | bytes 327712 | tf_op jit(solution)/shard_map/ppermute | solution.py:40
  37.0 0.6 collective-permute-start.15
  37.5 1.0 collective-permute-start.9
  38.5 1.6 %collective-permute-start.10 = (f16[40,1024]{1,0:T(8,128)(2,1)S(1)}, f16[40,1024]{1,0:T(8,128)(2,1)S(1)}, u32[]{:S(2)}, u32[]{:S(2)}) collective-permute-start(f16[40,1024]{1,0:T(8,128)(2,1)S(1)} %get-tuple-element.81), channel_id=1, source_target_pairs={{0,8},{2,10},{4,12},{6,14},{8,0},{10,2},{12,4},{14,6},{1,9},{3,11}... | collective-permute-start | bytes 245768 | tf_op jit(solution)/shard_map/ppermute | solution.py:40
  40.1 1.8 %collective-permute-start.11 = (f16[40,1024]{1,0:T(8,128)(2,1)S(1)}, f16[40,1024]{1,0:T(8,128)(2,1)S(1)}, u32[]{:S(2)}, u32[]{:S(2)}) collective-permute-start(f16[40,1024]{1,0:T(8,128)(2,1)S(1)} %get-tuple-element.82), channel_id=1, source_target_pairs={{0,12},{2,14},{4,8},{6,10},{8,4},{10,6},{12,0},{14,2},{1,13},{3,15... | collective-permute-start | bytes 245768 | tf_op jit(solution)/shard_map/ppermute | solution.py:40
  41.9 3.0 %fetch_cache.5.refs_3_ = bf16[8,2048,256]{2,1,0:T(8,128)(2,1)S(1)} custom-call(s32[6,8]{1,0:T(8,128)S(1)} %pad_add_fusion.meta, bf16[1,8,2048,1024]{3,2,1,0:T(8,128)(2,1)} %cache_ref.7), custom_call_target="tpu_custom_call" | custom-call | bytes 8388608 | tf_op jit(solution)/shard_map/fetch_cache/pallas_call | solution.py:150
  44.9 1.6 %collective-permute-done.10 = f16[40,1024]{1,0:T(8,128)(2,1)S(1)} collective-permute-done((f16[40,1024]{1,0:T(8,128)(2,1)S(1)}, f16[40,1024]{1,0:T(8,128)(2,1)S(1)}, u32[]{:S(2)}, u32[]{:S(2)}) %collective-permute-start.10) | collective-permute-done | bytes 81952 | tf_op jit(solution)/shard_map/ppermute | solution.py:40
  46.6 2.5 %collective-permute-start.14 = (bf16[40,1024]{1,0:T(8,128)(2,1)S(1)}, bf16[40,1024]{1,0:T(8,128)(2,1)S(1)}, u32[]{:S(2)}, u32[]{:S(2)}) collective-permute-start(bf16[40,1024]{1,0:T(8,128)(2,1)S(1)} %add_convert_fusion.1), channel_id=1, source_target_pairs={{0,12},{2,14},{4,8},{6,10},{8,4},{10,6},{12,0},{14,2},{1,13},{3,15... | collective-permute-start | bytes 245768 | tf_op jit(solution)/shard_map/ppermute | solution.py:40
  49.6 1.5 %collective-permute-start.12 = (bf16[40,1024]{1,0:T(8,128)(2,1)S(1)}, bf16[40,1024]{1,0:T(8,128)(2,1)S(1)}, u32[]{:S(2)}, u32[]{:S(2)}) collective-permute-start(bf16[40,1024]{1,0:T(8,128)(2,1)S(1)} %add_convert_fusion.1), channel_id=1, source_target_pairs={{0,4},{2,6},{4,0},{6,2},{8,12},{10,14},{12,8},{14,10},{1,5},{3,7},... | collective-permute-start | bytes 245768 | tf_op jit(solution)/shard_map/ppermute | solution.py:40
  51.1 3.0 %fetch_cache.6.refs_4_ = bf16[8,2048,256]{2,1,0:T(8,128)(2,1)S(1)} custom-call(s32[6,8]{1,0:T(8,128)S(1)} %pad_add_fusion.meta, bf16[1,8,2048,1024]{3,2,1,0:T(8,128)(2,1)} %cache_ref.7), custom_call_target="tpu_custom_call" | custom-call | bytes 8388608 | tf_op jit(solution)/shard_map/fetch_cache/pallas_call | solution.py:150
  54.2 1.9 %collective-permute-start.18 = (f16[40,1024]{1,0:T(8,128)(2,1)S(1)}, f16[40,1024]{1,0:T(8,128)(2,1)S(1)}, u32[]{:S(2)}, u32[]{:S(2)}) collective-permute-start(f16[40,1024]{1,0:T(8,128)(2,1)S(1)} %get-tuple-element.123), channel_id=1, source_target_pairs={{0,12},{2,14},{4,8},{6,10},{8,4},{10,6},{12,0},{14,2},{1,13},{3,15... | collective-permute-start | bytes 245768 | tf_op jit(solution)/shard_map/ppermute | solution.py:40
  56.2 2.6 %collective-permute-start.16 = (f16[40,1024]{1,0:T(8,128)(2,1)S(1)}, f16[40,1024]{1,0:T(8,128)(2,1)S(1)}, u32[]{:S(2)}, u32[]{:S(2)}) collective-permute-start(f16[40,1024]{1,0:T(8,128)(2,1)S(1)} %get-tuple-element.125), channel_id=1, source_target_pairs={{0,4},{2,6},{4,0},{6,2},{8,12},{10,14},{12,8},{14,10},{1,5},{3,7},... | collective-permute-start | bytes 245768 | tf_op jit(solution)/shard_map/ppermute | solution.py:40
  58.8 1.7 %collective-permute-start.20 = (bf16[4,40,1024]{2,1,0:T(8,128)(2,1)S(1)}, bf16[4,40,1024]{2,1,0:T(8,128)(2,1)S(1)}, u32[]{:S(2)}, u32[]{:S(2)}) collective-permute-start(bf16[4,40,1024]{2,1,0:T(8,128)(2,1)S(1)} %pad_maximum_fusion.refs_0_), channel_id=1, source_target_pairs={{0,2},{2,0},{4,6},{6,4},{8,10},{10,8},{12,14},{14,12},{1,3},{3,1},... | collective-permute-start | bytes 983048 | tf_op jit(solution)/shard_map/ppermute | solution.py:40
  60.5 3.0 %fetch_cache.7.refs_5_ = bf16[8,2048,256]{2,1,0:T(8,128)(2,1)S(1)} custom-call(s32[6,8]{1,0:T(8,128)S(1)} %pad_add_fusion.meta, bf16[1,8,2048,1024]{3,2,1,0:T(8,128)(2,1)} %cache_ref.7), custom_call_target="tpu_custom_call" | custom-call | bytes 8388608 | tf_op jit(solution)/shard_map/fetch_cache/pallas_call | solution.py:150
  64.1 2.7 %collective-permute-done.20.refs_1_ = bf16[4,40,1024]{2,1,0:T(8,128)(2,1)S(1)} collective-permute-done((bf16[4,40,1024]{2,1,0:T(8,128)(2,1)S(1)}, bf16[4,40,1024]{2,1,0:T(8,128)(2,1)S(1)}, u32[]{:S(2)}, u32[]{:S(2)}) %collective-permute-start.20) | collective-permute-done | bytes 327712 | tf_op jit(solution)/shard_map/ppermute | solution.py:40
  66.8 6.6 %attend.4 = bf16[4,64,1152]{2,1,0:T(8,128)(2,1)S(1)} custom-call(s32[6,8]{1,0:T(8,128)S(1)} %pad_add_fusion.meta, bf16[4,40,1024]{2,1,0:T(8,128)(2,1)S(1)} %pad_maximum_fusion.refs_0_, bf16[4,40,1024]{2,1,0:T(8,128)(2,1)S(1)} %collective-permute-done.20.refs_1_, bf16[8,2048,256]{2,1,0:T(8,128)(2,1)S(1)} %fetch_cache.4.refs_2_, ...), custom_call_target="tpu_custom_call" | custom-call | flops 4294967296 | bytes 8388608 | tf_op jit(solution)/shard_map/attend/pallas_call | solution.py:488
  73.4 1.3 %collective-permute-start.21 = (bf16[4,64,1152]{2,1,0:T(8,128)(2,1)S(1)}, bf16[4,64,1152]{2,1,0:T(8,128)(2,1)S(1)}, u32[]{:S(2)}, u32[]{:S(2)}) collective-permute-start(bf16[4,64,1152]{2,1,0:T(8,128)(2,1)S(1)} %attend.4), channel_id=1, source_target_pairs={{0,2},{2,0},{4,6},{6,4},{8,10},{10,8},{12,14},{14,12},{1,3},{3,1},... | collective-permute-start | bytes 1769480 | tf_op jit(solution)/shard_map/ppermute | solution.py:40
  74.9 4.3 %collective-permute-start.22 = (bf16[2,40,1024]{2,1,0:T(8,128)(2,1)S(1)}, bf16[2,40,1024]{2,1,0:T(8,128)(2,1)S(1)}, u32[]{:S(2)}, u32[]{:S(2)}) collective-permute-start(bf16[2,40,1024]{2,1,0:T(8,128)(2,1)S(1)} %pad_maximum_fusion.1.refs_0_), channel_id=1, source_target_pairs={{0,4},{2,6},{4,0},{6,2},{8,12},{10,14},{12,8},{14,10},{1,5},{3,7},... | collective-permute-start | bytes 491528 | tf_op jit(solution)/shard_map/ppermute | solution.py:40
  79.2 6.4 %attend.5 = (bf16[4,64,1152]{2,1,0:T(8,128)(2,1)S(1)}, bf16[64,1024]{1,0:T(8,128)(2,1)S(1)}) custom-call(s32[6,8]{1,0:T(8,128)S(1)} %pad_add_fusion.meta, bf16[4,40,1024]{2,1,0:T(8,128)(2,1)S(1)} %pad_maximum_fusion.refs_0_, bf16[4,40,1024]{2,1,0:T(8,128)(2,1)S(1)} %collective-permute-done.20.refs_1_, bf16[8,2048,256]{2,1,0:T(8,128)(2,1)S(1)} %fetch_cache.4.refs_2_, ...), custom_call_target="tpu_custom_call" | custom-call | flops 4294967296 | bytes 8388608 | tf_op jit(solution)/shard_map/attend/pallas_call | solution.py:488
  85.6 1.5 %merge.2 = (bf16[64,1152]{1,0:T(8,128)(2,1)S(1)}, bf16[64,1152]{1,0:T(8,128)(2,1)S(1)}, bf16[64,1152]{1,0:T(8,128)(2,1)S(1)}, bf16[64,1152]{1,0:T(8,128)(2,1)S(1)}) custom-call(bf16[4,64,1152]{2,1,0:T(8,128)(2,1)S(1)} %get-tuple-element.98.refs_0_, bf16[4,64,1152]{2,1,0:T(8,128)(2,1)S(1)} %collective-permute-done.21.refs_1_), custom_call_target="tpu_custom_call" | custom-call | tf_op jit(solution)/shard_map/merge/pallas_call | solution.py:285
  87.1 6.6 %attend.6 = bf16[4,64,1152]{2,1,0:T(8,128)(2,1)S(1)} custom-call(s32[6,8]{1,0:T(8,128)S(1)} %pad_add_fusion.meta, bf16[2,40,1024]{2,1,0:T(8,128)(2,1)S(1)} %pad_maximum_fusion.1.refs_0_, bf16[2,40,1024]{2,1,0:T(8,128)(2,1)S(1)} %collective-permute-done.22.refs_1_, bf16[2,40,1024]{2,1,0:T(8,128)(2,1)S(1)} %collective-permute-done.23.refs_2_, ...), custom_call_target="tpu_custom_call" | custom-call | flops 4294967296 | bytes 8388608 | tf_op jit(solution)/shard_map/attend/pallas_call | solution.py:488
  93.7 0.9 collective-permute-start.28
  94.6 4.4 %collective-permute-start.27 = (bf16[64,1152]{1,0:T(8,128)(2,1)S(1)}, bf16[64,1152]{1,0:T(8,128)(2,1)S(1)}, u32[]{:S(2)}, u32[]{:S(2)}) collective-permute-start(bf16[64,1152]{1,0:T(8,128)(2,1)S(1)} %get-tuple-element.111), channel_id=1, source_target_pairs={{0,12},{2,14},{4,8},{6,10},{8,4},{10,6},{12,0},{14,2},{1,13},{3,15... | collective-permute-start | bytes 442376 | tf_op jit(solution)/shard_map/ppermute | solution.py:40
  99.0 6.4 %attend.7 = (bf16[4,64,1152]{2,1,0:T(8,128)(2,1)S(1)}, bf16[64,1024]{1,0:T(8,128)(2,1)S(1)}) custom-call(s32[6,8]{1,0:T(8,128)S(1)} %pad_add_fusion.meta, bf16[2,40,1024]{2,1,0:T(8,128)(2,1)S(1)} %pad_maximum_fusion.1.refs_0_, bf16[2,40,1024]{2,1,0:T(8,128)(2,1)S(1)} %collective-permute-done.22.refs_1_, ...), custom_call_target="tpu_custom_call" | custom-call | flops 4294967296 | bytes 8388608 | tf_op jit(solution)/shard_map/attend/pallas_call | solution.py:488
  105.4 1.5 %merge.3 = (bf16[64,1152]{1,0:T(8,128)(2,1)S(1)}, bf16[64,1152]{1,0:T(8,128)(2,1)S(1)}, bf16[64,1152]{1,0:T(8,128)(2,1)S(1)}, bf16[64,1152]{1,0:T(8,128)(2,1)S(1)}) custom-call(bf16[4,64,1152]{2,1,0:T(8,128)(2,1)S(1)} %get-tuple-element.115.refs_0_, bf16[4,64,1152]{2,1,0:T(8,128)(2,1)S(1)} %collective-permute-done.28.refs_1_), custom_call_target="tpu_custom_call" | custom-call | tf_op jit(solution)/shard_map/merge/pallas_call | solution.py:285
  107.1 4.3 %collective-permute-start.31 = (bf16[64,1152]{1,0:T(8,128)(2,1)S(1)}, bf16[64,1152]{1,0:T(8,128)(2,1)S(1)}, u32[]{:S(2)}, u32[]{:S(2)}) collective-permute-start(bf16[64,1152]{1,0:T(8,128)(2,1)S(1)} %get-tuple-element.119), channel_id=1, source_target_pairs={{0,12},{2,14},{4,8},{6,10},{8,4},{10,6},{12,0},{14,2},{1,13},{3,15... | collective-permute-start | bytes 442376 | tf_op jit(solution)/shard_map/ppermute | solution.py:40
  111.4 0.7 attend_own.2.refs_4_
  112.1 0.7 attend_own.3.refs_5_
  112.9 1.3 %finish.2.refs_0_ = bf16[1,64,1024]{2,1,0:T(8,128)(2,1)S(1)} custom-call(s32[6,8]{1,0:T(8,128)S(1)} %pad_add_fusion.meta, bf16[64,1152]{1,0:T(8,128)(2,1)S(1)} %get-tuple-element.108.refs_0_, bf16[64,1152]{1,0:T(8,128)(2,1)S(1)} %collective-permute-done.25.refs_1_, bf16[64,1152]{1,0:T(8,128)(2,1)S(1)} %collective-permute-done.26.refs_2_, ...), custom_call_target="tpu_custom_call" | custom-call | tf_op jit(solution)/shard_map/finish/pallas_call | solution.py:533
  114.2 2.4 %collective-permute-done.30.refs_3_ = bf16[64,1152]{1,0:T(8,128)(2,1)S(1)} collective-permute-done((bf16[64,1152]{1,0:T(8,128)(2,1)S(1)}, bf16[64,1152]{1,0:T(8,128)(2,1)S(1)}, u32[]{:S(2)}, u32[]{:S(2)}) %collective-permute-start.30) | collective-permute-done | bytes 147488 | tf_op jit(solution)/shard_map/ppermute | solution.py:40
  116.5 2.0 %finish.3 = bf16[1,64,2048]{2,1,0:T(8,128)(2,1)} custom-call(s32[6,8]{1,0:T(8,128)S(1)} %pad_add_fusion.meta, bf16[1,64,1024]{2,1,0:T(8,128)(2,1)S(1)} %finish.2.refs_0_, bf16[64,1152]{1,0:T(8,128)(2,1)S(1)} %get-tuple-element.116.refs_1_, bf16[64,1152]{1,0:T(8,128)(2,1)S(1)} %collective-permute-done.29.refs_2_, ...), custom_call_target="tpu_custom_call" | custom-call | tf_op jit(solution)/shard_map/finish/pallas_call | solution.py:533
  (48 shorter events, 2.0 us)
Async XLA Ops:
  0.0 4.3 %collective-permute-start = (bf16[1,64,5120]{2,1,0:T(8,128)(2,1)}, bf16[1,64,5120]{2,1,0:T(8,128)(2,1)S(1)}, u32[]{:S(2)}, u32[]{:S(2)}) collective-permute-start(bf16[1,64,5120]{2,1,0:T(8,128)(2,1)} %param.9), channel_id=1, source_target_pairs={{0,16},{1,17},{2,18},{3,19},{4,20},{5,21},{6,22},{7,23},{8,24},{9,... | collective-permute-start | bytes 1966088 | tf_op jit(solution)/shard_map/ppermute | solution.py:572
  5.0 9.2 %collective-permute-start.1 = (bf16[64,640]{1,0:T(8,128)(2,1)S(1)}, bf16[64,640]{1,0:T(8,128)(2,1)S(1)}, u32[]{:S(2)}, u32[]{:S(2)}) collective-permute-start(bf16[64,640]{1,0:T(8,128)(2,1)S(1)} %get-tuple-element.67), channel_id=1, source_target_pairs={{0,4},{2,6},{4,0},{6,2},{8,12},{10,14},{12,8},{14,10},{1,5},{3,7},... | collective-permute-start | bytes 245768 | tf_op jit(solution)/shard_map/ppermute | solution.py:40
  7.5 11.2 %collective-permute-start.2 = (bf16[64,640]{1,0:T(8,128)(2,1)S(1)}, bf16[64,640]{1,0:T(8,128)(2,1)S(1)}, u32[]{:S(2)}, u32[]{:S(2)}) collective-permute-start(bf16[64,640]{1,0:T(8,128)(2,1)S(1)} %get-tuple-element.68), channel_id=1, source_target_pairs={{0,8},{2,10},{4,12},{6,14},{8,0},{10,2},{12,4},{14,6},{1,9},{3,11}... | collective-permute-start | bytes 245768 | tf_op jit(solution)/shard_map/ppermute | solution.py:40
  10.1 11.3 %collective-permute-start.3 = (bf16[64,640]{1,0:T(8,128)(2,1)S(1)}, bf16[64,640]{1,0:T(8,128)(2,1)S(1)}, u32[]{:S(2)}, u32[]{:S(2)}) collective-permute-start(bf16[64,640]{1,0:T(8,128)(2,1)S(1)} %get-tuple-element.69), channel_id=1, source_target_pairs={{0,12},{2,14},{4,8},{6,10},{8,4},{10,6},{12,0},{14,2},{1,13},{3,15... | collective-permute-start | bytes 245768 | tf_op jit(solution)/shard_map/ppermute | solution.py:40
  10.1 11.3 %collective-permute-start.4 = (bf16[64,640]{1,0:T(8,128)(2,1)S(1)}, bf16[64,640]{1,0:T(8,128)(2,1)S(1)}, u32[]{:S(2)}, u32[]{:S(2)}) collective-permute-start(bf16[64,640]{1,0:T(8,128)(2,1)S(1)} %get-tuple-element.70), channel_id=1, source_target_pairs={{0,2},{2,0},{4,6},{6,4},{8,10},{10,8},{12,14},{14,12},{1,3},{3,1},... | collective-permute-start | bytes 245768 | tf_op jit(solution)/shard_map/ppermute | solution.py:40
  11.8 9.6 %collective-permute-start.5 = (bf16[64,640]{1,0:T(8,128)(2,1)S(1)}, bf16[64,640]{1,0:T(8,128)(2,1)S(1)}, u32[]{:S(2)}, u32[]{:S(2)}) collective-permute-start(bf16[64,640]{1,0:T(8,128)(2,1)S(1)} %get-tuple-element.71), channel_id=1, source_target_pairs={{0,6},{2,4},{4,2},{6,0},{8,14},{10,12},{12,10},{14,8},{1,7},{3,5},... | collective-permute-start | bytes 245768 | tf_op jit(solution)/shard_map/ppermute | solution.py:40
  14.2 9.6 %collective-permute-start.6 = (bf16[64,640]{1,0:T(8,128)(2,1)S(1)}, bf16[64,640]{1,0:T(8,128)(2,1)S(1)}, u32[]{:S(2)}, u32[]{:S(2)}) collective-permute-start(bf16[64,640]{1,0:T(8,128)(2,1)S(1)} %get-tuple-element.72), channel_id=1, source_target_pairs={{0,10},{2,8},{4,14},{6,12},{8,2},{10,0},{12,6},{14,4},{1,11},{3,9}... | collective-permute-start | bytes 245768 | tf_op jit(solution)/shard_map/ppermute | solution.py:40
  18.7 7.2 %collective-permute-start.7 = (bf16[64,640]{1,0:T(8,128)(2,1)S(1)}, bf16[64,640]{1,0:T(8,128)(2,1)S(1)}, u32[]{:S(2)}, u32[]{:S(2)}) collective-permute-start(bf16[64,640]{1,0:T(8,128)(2,1)S(1)} %get-tuple-element.73), channel_id=1, source_target_pairs={{0,14},{2,12},{4,10},{6,8},{8,6},{10,4},{12,2},{14,0},{1,15},{3,13... | collective-permute-start | bytes 245768 | tf_op jit(solution)/shard_map/ppermute | solution.py:40
  28.8 7.9 %collective-permute-start.8 = (f16[4,40,1024]{2,1,0:T(8,128)(2,1)S(1)}, f16[4,40,1024]{2,1,0:T(8,128)(2,1)S(1)}, u32[]{:S(2)}, u32[]{:S(2)}) collective-permute-start(f16[4,40,1024]{2,1,0:T(8,128)(2,1)S(1)} %bitcast.33), channel_id=1, source_target_pairs={{0,2},{2,0},{4,6},{6,4},{8,10},{10,8},{12,14},{14,12},{1,3},{3,1},... | collective-permute-start | bytes 983048 | tf_op jit(solution)/shard_map/ppermute | solution.py:40
  37.0 17.1 %collective-permute-start.15 = (f16[4,40,1024]{2,1,0:T(8,128)(2,1)S(1)}, f16[4,40,1024]{2,1,0:T(8,128)(2,1)S(1)}, u32[]{:S(2)}, u32[]{:S(2)}) collective-permute-start(f16[4,40,1024]{2,1,0:T(8,128)(2,1)S(1)} %multiply_convert_fusion), channel_id=1, source_target_pairs={{0,2},{2,0},{4,6},{6,4},{8,10},{10,8},{12,14},{14,12},{1,3},{3,1},... | collective-permute-start | bytes 983048 | tf_op jit(solution)/shard_map/ppermute | solution.py:40
  37.5 7.4 %collective-permute-start.9 = (f16[40,1024]{1,0:T(8,128)(2,1)S(1)}, f16[40,1024]{1,0:T(8,128)(2,1)S(1)}, u32[]{:S(2)}, u32[]{:S(2)}) collective-permute-start(f16[40,1024]{1,0:T(8,128)(2,1)S(1)} %get-tuple-element.80), channel_id=1, source_target_pairs={{0,4},{2,6},{4,0},{6,2},{8,12},{10,14},{12,8},{14,10},{1,5},{3,7},... | collective-permute-start | bytes 245768 | tf_op jit(solution)/shard_map/ppermute | solution.py:40
  38.5 8.0 %collective-permute-start.10 = (f16[40,1024]{1,0:T(8,128)(2,1)S(1)}, f16[40,1024]{1,0:T(8,128)(2,1)S(1)}, u32[]{:S(2)}, u32[]{:S(2)}) collective-permute-start(f16[40,1024]{1,0:T(8,128)(2,1)S(1)} %get-tuple-element.81), channel_id=1, source_target_pairs={{0,8},{2,10},{4,12},{6,14},{8,0},{10,2},{12,4},{14,6},{1,9},{3,11}... | collective-permute-start | bytes 245768 | tf_op jit(solution)/shard_map/ppermute | solution.py:40
  40.1 6.4 %collective-permute-start.11 = (f16[40,1024]{1,0:T(8,128)(2,1)S(1)}, f16[40,1024]{1,0:T(8,128)(2,1)S(1)}, u32[]{:S(2)}, u32[]{:S(2)}) collective-permute-start(f16[40,1024]{1,0:T(8,128)(2,1)S(1)} %get-tuple-element.82), channel_id=1, source_target_pairs={{0,12},{2,14},{4,8},{6,10},{8,4},{10,6},{12,0},{14,2},{1,13},{3,15... | collective-permute-start | bytes 245768 | tf_op jit(solution)/shard_map/ppermute | solution.py:40
  46.6 9.5 %collective-permute-start.14 = (bf16[40,1024]{1,0:T(8,128)(2,1)S(1)}, bf16[40,1024]{1,0:T(8,128)(2,1)S(1)}, u32[]{:S(2)}, u32[]{:S(2)}) collective-permute-start(bf16[40,1024]{1,0:T(8,128)(2,1)S(1)} %add_convert_fusion.1), channel_id=1, source_target_pairs={{0,12},{2,14},{4,8},{6,10},{8,4},{10,6},{12,0},{14,2},{1,13},{3,15... | collective-permute-start | bytes 245768 | tf_op jit(solution)/shard_map/ppermute | solution.py:40
  49.2 9.5 %collective-permute-start.13 = (bf16[40,1024]{1,0:T(8,128)(2,1)S(1)}, bf16[40,1024]{1,0:T(8,128)(2,1)S(1)}, u32[]{:S(2)}, u32[]{:S(2)}) collective-permute-start(bf16[40,1024]{1,0:T(8,128)(2,1)S(1)} %add_convert_fusion.1), channel_id=1, source_target_pairs={{0,8},{2,10},{4,12},{6,14},{8,0},{10,2},{12,4},{14,6},{1,9},{3,11}... | collective-permute-start | bytes 245768 | tf_op jit(solution)/shard_map/ppermute | solution.py:40
  49.6 9.1 %collective-permute-start.12 = (bf16[40,1024]{1,0:T(8,128)(2,1)S(1)}, bf16[40,1024]{1,0:T(8,128)(2,1)S(1)}, u32[]{:S(2)}, u32[]{:S(2)}) collective-permute-start(bf16[40,1024]{1,0:T(8,128)(2,1)S(1)} %add_convert_fusion.1), channel_id=1, source_target_pairs={{0,4},{2,6},{4,0},{6,2},{8,12},{10,14},{12,8},{14,10},{1,5},{3,7},... | collective-permute-start | bytes 245768 | tf_op jit(solution)/shard_map/ppermute | solution.py:40
  54.2 9.3 %collective-permute-start.18 = (f16[40,1024]{1,0:T(8,128)(2,1)S(1)}, f16[40,1024]{1,0:T(8,128)(2,1)S(1)}, u32[]{:S(2)}, u32[]{:S(2)}) collective-permute-start(f16[40,1024]{1,0:T(8,128)(2,1)S(1)} %get-tuple-element.123), channel_id=1, source_target_pairs={{0,12},{2,14},{4,8},{6,10},{8,4},{10,6},{12,0},{14,2},{1,13},{3,15... | collective-permute-start | bytes 245768 | tf_op jit(solution)/shard_map/ppermute | solution.py:40
  56.1 7.4 %collective-permute-start.17 = (f16[40,1024]{1,0:T(8,128)(2,1)S(1)}, f16[40,1024]{1,0:T(8,128)(2,1)S(1)}, u32[]{:S(2)}, u32[]{:S(2)}) collective-permute-start(f16[40,1024]{1,0:T(8,128)(2,1)S(1)} %get-tuple-element.124), channel_id=1, source_target_pairs={{0,8},{2,10},{4,12},{6,14},{8,0},{10,2},{12,4},{14,6},{1,9},{3,11}... | collective-permute-start | bytes 245768 | tf_op jit(solution)/shard_map/ppermute | solution.py:40
  56.2 7.4 %collective-permute-start.16 = (f16[40,1024]{1,0:T(8,128)(2,1)S(1)}, f16[40,1024]{1,0:T(8,128)(2,1)S(1)}, u32[]{:S(2)}, u32[]{:S(2)}) collective-permute-start(f16[40,1024]{1,0:T(8,128)(2,1)S(1)} %get-tuple-element.125), channel_id=1, source_target_pairs={{0,4},{2,6},{4,0},{6,2},{8,12},{10,14},{12,8},{14,10},{1,5},{3,7},... | collective-permute-start | bytes 245768 | tf_op jit(solution)/shard_map/ppermute | solution.py:40
  58.8 8.0 %collective-permute-start.20 = (bf16[4,40,1024]{2,1,0:T(8,128)(2,1)S(1)}, bf16[4,40,1024]{2,1,0:T(8,128)(2,1)S(1)}, u32[]{:S(2)}, u32[]{:S(2)}) collective-permute-start(bf16[4,40,1024]{2,1,0:T(8,128)(2,1)S(1)} %pad_maximum_fusion.refs_0_), channel_id=1, source_target_pairs={{0,2},{2,0},{4,6},{6,4},{8,10},{10,8},{12,14},{14,12},{1,3},{3,1},... | collective-permute-start | bytes 983048 | tf_op jit(solution)/shard_map/ppermute | solution.py:40
  63.6 11.1 %collective-permute-start.19 = (bf16[40,1024]{1,0:T(8,128)(2,1)S(1)}, bf16[40,1024]{1,0:T(8,128)(2,1)S(1)}, u32[]{:S(2)}, u32[]{:S(2)}) collective-permute-start(bf16[40,1024]{1,0:T(8,128)(2,1)S(1)} %add_convert_fusion), channel_id=1, source_target_pairs={{0,2},{2,0},{4,6},{6,4},{8,10},{10,8},{12,14},{14,12},{1,3},{3,1},... | collective-permute-start | bytes 245768 | tf_op jit(solution)/shard_map/ppermute | solution.py:40
  73.4 12.2 %collective-permute-start.21 = (bf16[4,64,1152]{2,1,0:T(8,128)(2,1)S(1)}, bf16[4,64,1152]{2,1,0:T(8,128)(2,1)S(1)}, u32[]{:S(2)}, u32[]{:S(2)}) collective-permute-start(bf16[4,64,1152]{2,1,0:T(8,128)(2,1)S(1)} %attend.4), channel_id=1, source_target_pairs={{0,2},{2,0},{4,6},{6,4},{8,10},{10,8},{12,14},{14,12},{1,3},{3,1},... | collective-permute-start | bytes 1769480 | tf_op jit(solution)/shard_map/ppermute | solution.py:40
  74.7 12.4 %collective-permute-start.24 = (bf16[2,40,1024]{2,1,0:T(8,128)(2,1)S(1)}, bf16[2,40,1024]{2,1,0:T(8,128)(2,1)S(1)}, u32[]{:S(2)}, u32[]{:S(2)}) collective-permute-start(bf16[2,40,1024]{2,1,0:T(8,128)(2,1)S(1)} %pad_maximum_fusion.1.refs_0_), channel_id=1, source_target_pairs={{0,12},{2,14},{4,8},{6,10},{8,4},{10,6},{12,0},{14,2},{1,13},{3,15... | collective-permute-start | bytes 491528 | tf_op jit(solution)/shard_map/ppermute | solution.py:40
  74.8 12.3 %collective-permute-start.23 = (bf16[2,40,1024]{2,1,0:T(8,128)(2,1)S(1)}, bf16[2,40,1024]{2,1,0:T(8,128)(2,1)S(1)}, u32[]{:S(2)}, u32[]{:S(2)}) collective-permute-start(bf16[2,40,1024]{2,1,0:T(8,128)(2,1)S(1)} %pad_maximum_fusion.1.refs_0_), channel_id=1, source_target_pairs={{0,8},{2,10},{4,12},{6,14},{8,0},{10,2},{12,4},{14,6},{1,9},{3,11}... | collective-permute-start | bytes 491528 | tf_op jit(solution)/shard_map/ppermute | solution.py:40
  74.9 12.2 %collective-permute-start.22 = (bf16[2,40,1024]{2,1,0:T(8,128)(2,1)S(1)}, bf16[2,40,1024]{2,1,0:T(8,128)(2,1)S(1)}, u32[]{:S(2)}, u32[]{:S(2)}) collective-permute-start(bf16[2,40,1024]{2,1,0:T(8,128)(2,1)S(1)} %pad_maximum_fusion.1.refs_0_), channel_id=1, source_target_pairs={{0,4},{2,6},{4,0},{6,2},{8,12},{10,14},{12,8},{14,10},{1,5},{3,7},... | collective-permute-start | bytes 491528 | tf_op jit(solution)/shard_map/ppermute | solution.py:40
  93.7 11.7 %collective-permute-start.28 = (bf16[4,64,1152]{2,1,0:T(8,128)(2,1)S(1)}, bf16[4,64,1152]{2,1,0:T(8,128)(2,1)S(1)}, u32[]{:S(2)}, u32[]{:S(2)}) collective-permute-start(bf16[4,64,1152]{2,1,0:T(8,128)(2,1)S(1)} %attend.6), channel_id=1, source_target_pairs={{0,2},{2,0},{4,6},{6,4},{8,10},{10,8},{12,14},{14,12},{1,3},{3,1},... | collective-permute-start | bytes 1769480 | tf_op jit(solution)/shard_map/ppermute | solution.py:40
  94.6 12.5 %collective-permute-start.25 = (bf16[64,1152]{1,0:T(8,128)(2,1)S(1)}, bf16[64,1152]{1,0:T(8,128)(2,1)S(1)}, u32[]{:S(2)}, u32[]{:S(2)}) collective-permute-start(bf16[64,1152]{1,0:T(8,128)(2,1)S(1)} %get-tuple-element.109), channel_id=1, source_target_pairs={{0,4},{2,6},{4,0},{6,2},{8,12},{10,14},{12,8},{14,10},{1,5},{3,7},... | collective-permute-start | bytes 442376 | tf_op jit(solution)/shard_map/ppermute | solution.py:40
  94.6 18.3 %collective-permute-start.26 = (bf16[64,1152]{1,0:T(8,128)(2,1)S(1)}, bf16[64,1152]{1,0:T(8,128)(2,1)S(1)}, u32[]{:S(2)}, u32[]{:S(2)}) collective-permute-start(bf16[64,1152]{1,0:T(8,128)(2,1)S(1)} %get-tuple-element.110), channel_id=1, source_target_pairs={{0,8},{2,10},{4,12},{6,14},{8,0},{10,2},{12,4},{14,6},{1,9},{3,11}... | collective-permute-start | bytes 442376 | tf_op jit(solution)/shard_map/ppermute | solution.py:40
  94.6 18.3 %collective-permute-start.27 = (bf16[64,1152]{1,0:T(8,128)(2,1)S(1)}, bf16[64,1152]{1,0:T(8,128)(2,1)S(1)}, u32[]{:S(2)}, u32[]{:S(2)}) collective-permute-start(bf16[64,1152]{1,0:T(8,128)(2,1)S(1)} %get-tuple-element.111), channel_id=1, source_target_pairs={{0,12},{2,14},{4,8},{6,10},{8,4},{10,6},{12,0},{14,2},{1,13},{3,15... | collective-permute-start | bytes 442376 | tf_op jit(solution)/shard_map/ppermute | solution.py:40
  107.0 7.2 %collective-permute-start.29 = (bf16[64,1152]{1,0:T(8,128)(2,1)S(1)}, bf16[64,1152]{1,0:T(8,128)(2,1)S(1)}, u32[]{:S(2)}, u32[]{:S(2)}) collective-permute-start(bf16[64,1152]{1,0:T(8,128)(2,1)S(1)} %get-tuple-element.117), channel_id=1, source_target_pairs={{0,4},{2,6},{4,0},{6,2},{8,12},{10,14},{12,8},{14,10},{1,5},{3,7},... | collective-permute-start | bytes 442376 | tf_op jit(solution)/shard_map/ppermute | solution.py:40
  107.0 9.5 %collective-permute-start.30 = (bf16[64,1152]{1,0:T(8,128)(2,1)S(1)}, bf16[64,1152]{1,0:T(8,128)(2,1)S(1)}, u32[]{:S(2)}, u32[]{:S(2)}) collective-permute-start(bf16[64,1152]{1,0:T(8,128)(2,1)S(1)} %get-tuple-element.118), channel_id=1, source_target_pairs={{0,8},{2,10},{4,12},{6,14},{8,0},{10,2},{12,4},{14,6},{1,9},{3,11}... | collective-permute-start | bytes 442376 | tf_op jit(solution)/shard_map/ppermute | solution.py:40
  107.1 9.4 %collective-permute-start.31 = (bf16[64,1152]{1,0:T(8,128)(2,1)S(1)}, bf16[64,1152]{1,0:T(8,128)(2,1)S(1)}, u32[]{:S(2)}, u32[]{:S(2)}) collective-permute-start(bf16[64,1152]{1,0:T(8,128)(2,1)S(1)} %get-tuple-element.119), channel_id=1, source_target_pairs={{0,12},{2,14},{4,8},{6,10},{8,4},{10,6},{12,0},{14,2},{1,13},{3,15... | collective-permute-start | bytes 442376 | tf_op jit(solution)/shard_map/ppermute | solution.py:40

commit v2 on v1

--- a/solution.py
+++ b/solution.py
@@ -73,14 +73,14 @@
             lax.dynamic_slice_in_dim(total, grid.owner(meta[1], kx, kz) * depth, depth, 1)
             for kx in range(grid.xs) for kz in range(grid.zs)
         ]
-    whole = pl.BlockSpec(hidden.shape, lambda i, *m: (0, 0, 0))
+    whole = pl.BlockSpec(memory_space=pltpu.VMEM)
     return pl.pallas_call(
         functools.partial(split_kernel, grid, depth),
         grid_spec=pltpu.PrefetchScalarGridSpec(
             num_scalar_prefetch=1,
             grid=(1,),
             in_specs=[whole, whole],
-            out_specs=[pl.BlockSpec((bl, depth), lambda i, *m: (0, 0))] * grid.n,
+            out_specs=[whole] * grid.n,
         ),
         out_shape=[jax.ShapeDtypeStruct((bl, depth), jnp.bfloat16)] * grid.n,
         compiler_params=pltpu.CompilerParams(vmem_limit_bytes=16 * MIB),
@@ -170,39 +170,37 @@
     x_refs, w_ref, refs = refs[:grid.n], refs[grid.n], refs[grid.n + 1:]
     out_refs, (xp_ref, starts) = refs[:-2], refs[-2:]
 
-    @pl.when(pl.program_id(0) == 0)
-    def _():
-        facts = Facts(meta)
-        shard = facts.shard
-        offset = jnp.int32(0)
-        for b in range(grid.n):
-            starts[b] = offset
-            offset = offset + facts.length(b)
-        lane = lax.broadcasted_iota(jnp.int32, (8, grid.n * bl), 1)
-        target = jnp.full(lane.shape, -1, jnp.int32)
-        owners = [
-            grid.owner(shard, kx, kz) for kx in range(grid.xs) for kz in range(grid.zs)
-        ]
-        for k, b in enumerate(owners):
-            order = lane - k * bl
-            used = (order >= 0) & (order < facts.length(b))
-            target = jnp.where(used, order + starts[b], target)
-        row = lax.broadcasted_iota(jnp.int32, (share, grid.n * bl), 0)
-        target = jnp.broadcast_to(target[:1], row.shape)
-        picks = [jnp.where(row + b * share == target, 1.0, 0.0) for b in owners]
-        pick = jnp.concatenate(picks, axis=0).astype(jnp.bfloat16)
-        x = jnp.concatenate([ref[...] for ref in x_refs], axis=0)
-        chosen = jnp.dot(pick, x, preferred_element_type=jnp.float32)
-        xp_ref[...] = chosen.astype(jnp.bfloat16)
-
-    result = jnp.dot(xp_ref[...], w_ref[0], preferred_element_type=jnp.float32)
+    facts = Facts(meta)
+    shard = facts.shard
+    offset = jnp.int32(0)
+    for b in range(grid.n):
+        starts[b] = offset
+        offset = offset + facts.length(b)
+    lane = lax.broadcasted_iota(jnp.int32, (8, grid.n * bl), 1)
+    target = jnp.full(lane.shape, -1, jnp.int32)
+    owners = [
+        grid.owner(shard, kx, kz) for kx in range(grid.xs) for kz in range(grid.zs)
+    ]
+    for k, b in enumerate(owners):
+        order = lane - k * bl
+        used = (order >= 0) & (order < facts.length(b))
+        target = jnp.where(used, order + starts[b], target)
+    row = lax.broadcasted_iota(jnp.int32, (share, grid.n * bl), 0)
+    target = jnp.broadcast_to(target[:1], row.shape)
+    picks = [jnp.where(row + b * share == target, 1.0, 0.0) for b in owners]
+    pick = jnp.concatenate(picks, axis=0).astype(jnp.bfloat16)
+    x = jnp.concatenate([ref[...] for ref in x_refs], axis=0)
+    chosen = jnp.dot(pick, x, preferred_element_type=jnp.float32)
+    xp_ref[...] = chosen.astype(jnp.bfloat16)
+
     rows = grid.zs * share
+    tile = out_refs[0].shape[1]
     for i, out_ref in enumerate(out_refs):
         chunk, kx = i // grid.xs, i % grid.xs
-
-        @pl.when(pl.program_id(0) == chunk)
-        def _(out_ref=out_ref, kx=kx):
-            out_ref[...] = result[kx * rows:(kx + 1) * rows]
+        out_ref[...] = jnp.dot(
+            xp_ref[kx * rows:(kx + 1) * rows], w_ref[0, :, chunk * tile:(chunk + 1) * tile],
+            preferred_element_type=jnp.float32,
+        )
 
 
 def project(grid, meta, xs, w, bl, share, chunks):
@@ -210,14 +208,14 @@
     rows = grid.n * share
     tile = cols // chunks
     piece = (grid.zs * share, tile)
+    whole = pl.BlockSpec(memory_space=pltpu.VMEM)
     return pl.pallas_call(
         functools.partial(project_kernel, grid, bl, share),
         grid_spec=pltpu.PrefetchScalarGridSpec(
             num_scalar_prefetch=1,
-            grid=(chunks,),
-            in_specs=[pl.BlockSpec((bl, k), lambda j, *m: (0, 0))] * grid.n
-            + [pl.BlockSpec((1, k, tile), lambda j, *m: (0, 0, j))],
-            out_specs=[pl.BlockSpec(piece, lambda j, *m: (0, 0))] * (chunks * grid.xs),
+            grid=(1,),
+            in_specs=[whole] * (grid.n + 1),
+            out_specs=[whole] * (chunks * grid.xs),
             scratch_shapes=[
                 pltpu.VMEM((rows, k), jnp.bfloat16), pltpu.SMEM((grid.n,), jnp.int32)
             ],
@@ -573,21 +571,22 @@
     depth = query_weight.shape[1]
     hidden = hidden_rows if depth % HD else fetch([hidden_rows])[0]
     slices = split(grid, place, hidden, handed, depth)
+    weight, own = fetch([query_weight, after(response_cache, handed)])
+    x = [slices[0]] + [None] * (grid.n - 1)
+    order = sorted(range(1, grid.n), key=lambda k: (k % grid.zs, k), reverse=True)
+    for k in order:
+        x[k] = grid.swap(slices[k], k // grid.zs, k % grid.zs)
     n = grid.n
     lane = lax.broadcasted_iota(jnp.int32, (1, n), 1)
-    section, shard = after((lax.axis_index("sec"), lax.axis_index("seq")), handed)
+    section, shard = after((lax.axis_index("sec"), lax.axis_index("seq")), x[order[2]])
     meta = jnp.concatenate([
         response_lengths, block_prompts[:, :, 0],
         jnp.pad(prompt_lengths, (0, n - prompt_lengths.shape[0]))[None],
         jnp.where(lane == 0, section, shard).astype(jnp.int32),
     ])
-    weight, own = fetch([query_weight, after(response_cache, handed)])
-    x = [slices[0]] + [None] * (grid.n - 1)
-    for kz in reversed(range(grid.zs)):
-        for kx in reversed(range(grid.xs)):
-            k = kx * grid.zs + kz
-            if k:
-                x[k] = grid.swap(slices[k], kx, kz)
+    half = (local_kv + 1) // 4
+    caches = [fetched(head) for head in range(half)]
+    x[0] = after(x[0], caches)
     part = project(grid, meta, x, weight, bl, share, chunks)
     part = [piece.reshape(grid.zs, share, part_cols) for piece in part]
     part = [part[c * grid.xs:(c + 1) * grid.xs] for c in range(chunks)]
@@ -635,21 +634,18 @@
     def send_z(merged):
         return [merged[0]] + [grid.swap(merged[kz], 0, kz) for kz in range(1, grid.zs)]
 
-    half = (local_kv + 1) // 4
-    caches = [fetched(head) for head in range(half)]
+    caches += [fetched(head, part[0][-1]) for head in range(half, min(heads + half, local_kv))]
     part[0][0] = after(part[0][0], caches)
     held = reduce_x(part[0])
     sends = narrow_z(held)
     if chunks > 1:
         sends, part[1][1] = both(sends, part[1][1])
         later = reduce_x(part[1])
-    caches += [fetched(head, sends) for head in range(half, heads)]
-    mine = sum_z(held, sends, caches)
+    mine = sum_z(held, sends, ())
     column = gather_z(mine)
     if chunks > 1:
-        caches += [fetched(head, mine) for head in range(heads, heads + half)]
         sends = narrow_z(after(later, mine))
-        column = after(column, (caches, sends))
+        column = after(column, sends)
     queries = gather_x(jnp.stack(column))
     if chunks == 1:
         outs, mets = call_far(0, queries)

time: 119 us -> 127 us (1.067)
  waiting for transfers between devices: 16.4 us -> 20.1 us
  Pallas kernels: 52 us -> 54.4 us
  starting transfers between devices: 48.3 us -> 50.2 us
    ppermute x31, waiting for transfers between devices: 15.7 us -> 19.4 us  [swap(): return lax.ppermute(value, 'seq', pairs)]
    pallas_call x4, Pallas kernels: 11.9 us -> 14.5 us  [fetch_cache(): pl.pallas_call(functools.partial(fetch_cache_kernel, n, chunk, width, fir...]
    ppermute x31, starting transfers between devices: 45.9 us -> 47.8 us  [swap(): return lax.ppermute(value, 'seq', pairs)]
where the time goes in v2:
time: 127 us
  Pallas kernels  54.4 us (43%)
  starting transfers between devices  50.2 us (40%)
  waiting for transfers between devices  20.1 us (16%)
  other arithmetic  1.42 us (1%)
    ppermute x31, starting transfers between devices, swap(): return lax.ppermute(value, 'seq', pairs)  47.8 us
    pallas_call x4, Pallas kernels, attend(): pl.pallas_call(functools.partial(attend_kernel, grid, kx, bl, share, head...  26.3 us
    ppermute x31, waiting for transfers between devices, swap(): return lax.ppermute(value, 'seq', pairs)  19.4 us
    pallas_call x4, Pallas kernels, fetch_cache(): pl.pallas_call(functools.partial(fetch_cache_kernel, n, chunk, width, fir...  14.5 us
    pallas_call x2, Pallas kernels, finish(): pl.pallas_call(functools.partial(finish_kernel, heads, bl, len(done)), gr...  3.27 us
    pallas_call x2, Pallas kernels, merge_column(): pl.pallas_call(functools.partial(merge_kernel, zs, heads), out_shape=[jax...  3.01 us
    pallas_call x2, Pallas kernels, fetch(): pl.pallas_call(fetch_kernel, in_specs=[anywhere] * len(arrays), out_specs...  2.85 us
  transfers between devices with their start and end apart: 32, of which 7 were waited for; matrix products, arithmetic and copies ran while one was open for 1% of the time, Pallas kernels for 34%

profile of v2, /device:TPU:0, one launch (start us, length us, event | category | flops | bytes accessed | tf_op | source)
XLA Modules:
  0.0 126.5 jit_solution(14448343003601736781)
XLA Ops:
  0.0 2.4 %collective-permute-start = (bf16[1,64,5120]{2,1,0:T(8,128)(2,1)}, bf16[1,64,5120]{2,1,0:T(8,128)(2,1)S(1)}, u32[]{:S(2)}, u32[]{:S(2)}) collective-permute-start(bf16[1,64,5120]{2,1,0:T(8,128)(2,1)} %param.9), channel_id=1, source_target_pairs={{0,16},{1,17},{2,18},{3,19},{4,20},{5,21},{6,22},{7,23},{8,24},{9,... | collective-permute-start | bytes 1966088 | tf_op jit(solution)/shard_map/ppermute | solution.py:570
  2.4 1.1 fetch.2.hidden_ref
  4.3 0.7 split.1
  5.0 4.4 %collective-permute-start.1 = (bf16[64,640]{1,0:T(8,128)(2,1)S(1)}, bf16[64,640]{1,0:T(8,128)(2,1)S(1)}, u32[]{:S(2)}, u32[]{:S(2)}) collective-permute-start(bf16[64,640]{1,0:T(8,128)(2,1)S(1)} %get-tuple-element.63), channel_id=1, source_target_pairs={{0,10},{2,8},{4,14},{6,12},{8,2},{10,0},{12,6},{14,4},{1,11},{3,9}... | collective-permute-start | bytes 245768 | tf_op jit(solution)/shard_map/ppermute | solution.py:40
  9.4 1.6 %collective-permute-start.2 = (bf16[64,640]{1,0:T(8,128)(2,1)S(1)}, bf16[64,640]{1,0:T(8,128)(2,1)S(1)}, u32[]{:S(2)}, u32[]{:S(2)}) collective-permute-start(bf16[64,640]{1,0:T(8,128)(2,1)S(1)} %get-tuple-element.68), channel_id=1, source_target_pairs={{0,4},{2,6},{4,0},{6,2},{8,12},{10,14},{12,8},{14,10},{1,5},{3,7},... | collective-permute-start | bytes 245768 | tf_op jit(solution)/shard_map/ppermute | solution.py:40
  11.3 2.5 %collective-permute-start.4 = (bf16[64,640]{1,0:T(8,128)(2,1)S(1)}, bf16[64,640]{1,0:T(8,128)(2,1)S(1)}, u32[]{:S(2)}, u32[]{:S(2)}) collective-permute-start(bf16[64,640]{1,0:T(8,128)(2,1)S(1)} %get-tuple-element.70), channel_id=1, source_target_pairs={{0,12},{2,14},{4,8},{6,10},{8,4},{10,6},{12,0},{14,2},{1,13},{3,15... | collective-permute-start | bytes 245768 | tf_op jit(solution)/shard_map/ppermute | solution.py:40
  14.3 1.8 %fetch.3 = (bf16[1,640,2048]{2,1,0:T(8,128)(2,1)S(1)}, bf16[1,64,1024]{2,1,0:T(8,128)(2,1)S(1)}) custom-call(bf16[1,640,2048]{2,1,0:T(8,128)(2,1)} %refs_0_.3, bf16[1,64,1024]{2,1,0:T(8,128)(2,1)} %refs_1_), custom_call_target="tpu_custom_call" | custom-call | bytes 2752512 | tf_op jit(solution)/shard_map/fetch/pallas_call | solution.py:115
  16.1 1.7 %collective-permute-start.6 = (bf16[64,640]{1,0:T(8,128)(2,1)S(1)}, bf16[64,640]{1,0:T(8,128)(2,1)S(1)}, u32[]{:S(2)}, u32[]{:S(2)}) collective-permute-start(bf16[64,640]{1,0:T(8,128)(2,1)S(1)} %get-tuple-element.72), channel_id=1, source_target_pairs={{0,6},{2,4},{4,2},{6,0},{8,14},{10,12},{12,10},{14,8},{1,7},{3,5},... | collective-permute-start | bytes 245768 | tf_op jit(solution)/shard_map/ppermute | solution.py:40
  17.8 1.4 %collective-permute-start.7 = (bf16[64,640]{1,0:T(8,128)(2,1)S(1)}, bf16[64,640]{1,0:T(8,128)(2,1)S(1)}, u32[]{:S(2)}, u32[]{:S(2)}) collective-permute-start(bf16[64,640]{1,0:T(8,128)(2,1)S(1)} %get-tuple-element.73), channel_id=1, source_target_pairs={{0,14},{2,12},{4,10},{6,8},{8,6},{10,4},{12,2},{14,0},{1,15},{3,13... | collective-permute-start | bytes 245768 | tf_op jit(solution)/shard_map/ppermute | solution.py:40
  19.2 0.7 pad_add_fusion.meta
  19.9 3.6 %fetch_cache.4.refs_2_ = bf16[8,2048,256]{2,1,0:T(8,128)(2,1)S(1)} custom-call(s32[6,8]{1,0:T(8,128)S(1)} %pad_add_fusion.meta, bf16[1,8,2048,1024]{3,2,1,0:T(8,128)(2,1)} %cache_ref.7), custom_call_target="tpu_custom_call" | custom-call | bytes 8388608 | tf_op jit(solution)/shard_map/fetch_cache/pallas_call | solution.py:150
  23.6 1.3 %collective-permute-done.7.refs_7_ = bf16[64,640]{1,0:T(8,128)(2,1)S(1)} collective-permute-done((bf16[64,640]{1,0:T(8,128)(2,1)S(1)}, bf16[64,640]{1,0:T(8,128)(2,1)S(1)}, u32[]{:S(2)}, u32[]{:S(2)}) %collective-permute-start.7) | collective-permute-done | bytes 81952 | tf_op jit(solution)/shard_map/ppermute | solution.py:40
  24.9 2.3 %project.1 = (f32[160,1024]{1,0:T(8,128)S(1)}, f32[160,1024]{1,0:T(8,128)S(1)}, f32[160,1024]{1,0:T(8,128)S(1)}, f32[160,1024]{1,0:T(8,128)S(1)}) custom-call(s32[6,8]{1,0:T(8,128)S(1)} %pad_add_fusion.meta, bf16[64,640]{1,0:T(8,128)(2,1)S(1)} %get-tuple-element.67.refs_0_, bf16[64,640]{1,0:T(8,128)(2,1)S(1)} %collective-permute-done.2.refs_1_, ...), custom_call_target="tpu_custom_call" | custom-call | flops 838860800 | bytes 5242880 | tf_op jit(solution)/shard_map/project/pallas_call | solution.py:212
  28.0 3.6 %fetch_cache.6.refs_4_ = bf16[8,2048,256]{2,1,0:T(8,128)(2,1)S(1)} custom-call(s32[6,8]{1,0:T(8,128)S(1)} %pad_add_fusion.meta, bf16[1,8,2048,1024]{3,2,1,0:T(8,128)(2,1)} %cache_ref.7), custom_call_target="tpu_custom_call" | custom-call | bytes 8388608 | tf_op jit(solution)/shard_map/fetch_cache/pallas_call | solution.py:150
  31.6 3.6 %fetch_cache.5.refs_3_ = bf16[8,2048,256]{2,1,0:T(8,128)(2,1)S(1)} custom-call(s32[6,8]{1,0:T(8,128)S(1)} %pad_add_fusion.meta, bf16[1,8,2048,1024]{3,2,1,0:T(8,128)(2,1)} %cache_ref.7), custom_call_target="tpu_custom_call" | custom-call | bytes 8388608 | tf_op jit(solution)/shard_map/fetch_cache/pallas_call | solution.py:150
  35.5 1.1 collective-permute-start.15
  36.6 1.7 %collective-permute-start.9 = (f16[40,1024]{1,0:T(8,128)(2,1)S(1)}, f16[40,1024]{1,0:T(8,128)(2,1)S(1)}, u32[]{:S(2)}, u32[]{:S(2)}) collective-permute-start(f16[40,1024]{1,0:T(8,128)(2,1)S(1)} %get-tuple-element.81), channel_id=1, source_target_pairs={{0,4},{2,6},{4,0},{6,2},{8,12},{10,14},{12,8},{14,10},{1,5},{3,7},... | collective-permute-start | bytes 245768 | tf_op jit(solution)/shard_map/ppermute | solution.py:40
  38.3 2.8 %collective-permute-start.10 = (f16[40,1024]{1,0:T(8,128)(2,1)S(1)}, f16[40,1024]{1,0:T(8,128)(2,1)S(1)}, u32[]{:S(2)}, u32[]{:S(2)}) collective-permute-start(f16[40,1024]{1,0:T(8,128)(2,1)S(1)} %get-tuple-element.82), channel_id=1, source_target_pairs={{0,8},{2,10},{4,12},{6,14},{8,0},{10,2},{12,4},{14,6},{1,9},{3,11}... | collective-permute-start | bytes 245768 | tf_op jit(solution)/shard_map/ppermute | solution.py:40
  41.2 1.5 %collective-permute-start.11 = (f16[40,1024]{1,0:T(8,128)(2,1)S(1)}, f16[40,1024]{1,0:T(8,128)(2,1)S(1)}, u32[]{:S(2)}, u32[]{:S(2)}) collective-permute-start(f16[40,1024]{1,0:T(8,128)(2,1)S(1)} %get-tuple-element.83), channel_id=1, source_target_pairs={{0,12},{2,14},{4,8},{6,10},{8,4},{10,6},{12,0},{14,2},{1,13},{3,15... | collective-permute-start | bytes 245768 | tf_op jit(solution)/shard_map/ppermute | solution.py:40
  42.6 5.1 %collective-permute-done.10 = f16[40,1024]{1,0:T(8,128)(2,1)S(1)} collective-permute-done((f16[40,1024]{1,0:T(8,128)(2,1)S(1)}, f16[40,1024]{1,0:T(8,128)(2,1)S(1)}, u32[]{:S(2)}, u32[]{:S(2)}) %collective-permute-start.10) | collective-permute-done | bytes 81952 | tf_op jit(solution)/shard_map/ppermute | solution.py:40
  47.8 2.4 %collective-permute-start.14 = (bf16[40,1024]{1,0:T(8,128)(2,1)S(1)}, bf16[40,1024]{1,0:T(8,128)(2,1)S(1)}, u32[]{:S(2)}, u32[]{:S(2)}) collective-permute-start(bf16[40,1024]{1,0:T(8,128)(2,1)S(1)} %add_convert_fusion.1), channel_id=1, source_target_pairs={{0,12},{2,14},{4,8},{6,10},{8,4},{10,6},{12,0},{14,2},{1,13},{3,15... | collective-permute-start | bytes 245768 | tf_op jit(solution)/shard_map/ppermute | solution.py:40
  50.2 0.9 collective-permute-start.13
  51.1 1.2 collective-permute-start.12
  52.4 2.4 %collective-permute-start.18 = (f16[40,1024]{1,0:T(8,128)(2,1)S(1)}, f16[40,1024]{1,0:T(8,128)(2,1)S(1)}, u32[]{:S(2)}, u32[]{:S(2)}) collective-permute-start(f16[40,1024]{1,0:T(8,128)(2,1)S(1)} %get-tuple-element.121), channel_id=1, source_target_pairs={{0,12},{2,14},{4,8},{6,10},{8,4},{10,6},{12,0},{14,2},{1,13},{3,15... | collective-permute-start | bytes 245768 | tf_op jit(solution)/shard_map/ppermute | solution.py:40
  54.8 2.7 %collective-permute-start.16 = (f16[40,1024]{1,0:T(8,128)(2,1)S(1)}, f16[40,1024]{1,0:T(8,128)(2,1)S(1)}, u32[]{:S(2)}, u32[]{:S(2)}) collective-permute-start(f16[40,1024]{1,0:T(8,128)(2,1)S(1)} %get-tuple-element.123), channel_id=1, source_target_pairs={{0,4},{2,6},{4,0},{6,2},{8,12},{10,14},{12,8},{14,10},{1,5},{3,7},... | collective-permute-start | bytes 245768 | tf_op jit(solution)/shard_map/ppermute | solution.py:40
  57.5 4.4 %collective-permute-done.13 = bf16[40,1024]{1,0:T(8,128)(2,1)S(1)} collective-permute-done((bf16[40,1024]{1,0:T(8,128)(2,1)S(1)}, bf16[40,1024]{1,0:T(8,128)(2,1)S(1)}, u32[]{:S(2)}, u32[]{:S(2)}) %collective-permute-start.13) | collective-permute-done | bytes 81952 | tf_op jit(solution)/shard_map/ppermute | solution.py:40
  62.0 1.3 %collective-permute-start.20 = (bf16[4,40,1024]{2,1,0:T(8,128)(2,1)S(1)}, bf16[4,40,1024]{2,1,0:T(8,128)(2,1)S(1)}, u32[]{:S(2)}, u32[]{:S(2)}) collective-permute-start(bf16[4,40,1024]{2,1,0:T(8,128)(2,1)S(1)} %pad_maximum_fusion.refs_0_), channel_id=1, source_target_pairs={{0,2},{2,0},{4,6},{6,4},{8,10},{10,8},{12,14},{14,12},{1,3},{3,1},... | collective-permute-start | bytes 983048 | tf_op jit(solution)/shard_map/ppermute | solution.py:40
  63.3 3.6 %fetch_cache.7.refs_5_ = bf16[8,2048,256]{2,1,0:T(8,128)(2,1)S(1)} custom-call(s32[6,8]{1,0:T(8,128)S(1)} %pad_add_fusion.meta, bf16[1,8,2048,1024]{3,2,1,0:T(8,128)(2,1)} %cache_ref.7), custom_call_target="tpu_custom_call" | custom-call | bytes 8388608 | tf_op jit(solution)/shard_map/fetch_cache/pallas_call | solution.py:150
  67.7 2.3 %collective-permute-done.20.refs_1_ = bf16[4,40,1024]{2,1,0:T(8,128)(2,1)S(1)} collective-permute-done((bf16[4,40,1024]{2,1,0:T(8,128)(2,1)S(1)}, bf16[4,40,1024]{2,1,0:T(8,128)(2,1)S(1)}, u32[]{:S(2)}, u32[]{:S(2)}) %collective-permute-start.20) | collective-permute-done | bytes 327712 | tf_op jit(solution)/shard_map/ppermute | solution.py:40
  70.0 6.4 %attend.4 = bf16[4,64,1152]{2,1,0:T(8,128)(2,1)S(1)} custom-call(s32[6,8]{1,0:T(8,128)S(1)} %pad_add_fusion.meta, bf16[4,40,1024]{2,1,0:T(8,128)(2,1)S(1)} %pad_maximum_fusion.refs_0_, bf16[4,40,1024]{2,1,0:T(8,128)(2,1)S(1)} %collective-permute-done.20.refs_1_, bf16[8,2048,256]{2,1,0:T(8,128)(2,1)S(1)} %fetch_cache.4.refs_2_, ...), custom_call_target="tpu_custom_call" | custom-call | flops 4294967296 | bytes 8388608 | tf_op jit(solution)/shard_map/attend/pallas_call | solution.py:486
  76.3 1.3 %collective-permute-start.21 = (bf16[4,64,1152]{2,1,0:T(8,128)(2,1)S(1)}, bf16[4,64,1152]{2,1,0:T(8,128)(2,1)S(1)}, u32[]{:S(2)}, u32[]{:S(2)}) collective-permute-start(bf16[4,64,1152]{2,1,0:T(8,128)(2,1)S(1)} %attend.4), channel_id=1, source_target_pairs={{0,2},{2,0},{4,6},{6,4},{8,10},{10,8},{12,14},{14,12},{1,3},{3,1},... | collective-permute-start | bytes 1769480 | tf_op jit(solution)/shard_map/ppermute | solution.py:40
  77.7 3.0 %collective-permute-start.24 = (bf16[2,40,1024]{2,1,0:T(8,128)(2,1)S(1)}, bf16[2,40,1024]{2,1,0:T(8,128)(2,1)S(1)}, u32[]{:S(2)}, u32[]{:S(2)}) collective-permute-start(bf16[2,40,1024]{2,1,0:T(8,128)(2,1)S(1)} %pad_maximum_fusion.1.refs_0_), channel_id=1, source_target_pairs={{0,12},{2,14},{4,8},{6,10},{8,4},{10,6},{12,0},{14,2},{1,13},{3,15... | collective-permute-start | bytes 491528 | tf_op jit(solution)/shard_map/ppermute | solution.py:40
  80.6 1.5 %collective-permute-start.22 = (bf16[2,40,1024]{2,1,0:T(8,128)(2,1)S(1)}, bf16[2,40,1024]{2,1,0:T(8,128)(2,1)S(1)}, u32[]{:S(2)}, u32[]{:S(2)}) collective-permute-start(bf16[2,40,1024]{2,1,0:T(8,128)(2,1)S(1)} %pad_maximum_fusion.1.refs_0_), channel_id=1, source_target_pairs={{0,4},{2,6},{4,0},{6,2},{8,12},{10,14},{12,8},{14,10},{1,5},{3,7},... | collective-permute-start | bytes 491528 | tf_op jit(solution)/shard_map/ppermute | solution.py:40
  82.1 6.6 %attend.5 = (bf16[4,64,1152]{2,1,0:T(8,128)(2,1)S(1)}, bf16[64,1024]{1,0:T(8,128)(2,1)S(1)}) custom-call(s32[6,8]{1,0:T(8,128)S(1)} %pad_add_fusion.meta, bf16[4,40,1024]{2,1,0:T(8,128)(2,1)S(1)} %pad_maximum_fusion.refs_0_, bf16[4,40,1024]{2,1,0:T(8,128)(2,1)S(1)} %collective-permute-done.20.refs_1_, bf16[8,2048,256]{2,1,0:T(8,128)(2,1)S(1)} %fetch_cache.4.refs_2_, ...), custom_call_target="tpu_custom_call" | custom-call | flops 4294967296 | bytes 8388608 | tf_op jit(solution)/shard_map/attend/pallas_call | solution.py:486
  88.8 1.5 %merge.2 = (bf16[64,1152]{1,0:T(8,128)(2,1)S(1)}, bf16[64,1152]{1,0:T(8,128)(2,1)S(1)}, bf16[64,1152]{1,0:T(8,128)(2,1)S(1)}, bf16[64,1152]{1,0:T(8,128)(2,1)S(1)}) custom-call(bf16[4,64,1152]{2,1,0:T(8,128)(2,1)S(1)} %get-tuple-element.96.refs_0_, bf16[4,64,1152]{2,1,0:T(8,128)(2,1)S(1)} %collective-permute-done.21.refs_1_), custom_call_target="tpu_custom_call" | custom-call | tf_op jit(solution)/shard_map/merge/pallas_call | solution.py:283
  90.3 6.4 %attend.6 = bf16[4,64,1152]{2,1,0:T(8,128)(2,1)S(1)} custom-call(s32[6,8]{1,0:T(8,128)S(1)} %pad_add_fusion.meta, bf16[2,40,1024]{2,1,0:T(8,128)(2,1)S(1)} %pad_maximum_fusion.1.refs_0_, bf16[2,40,1024]{2,1,0:T(8,128)(2,1)S(1)} %collective-permute-done.22.refs_1_, bf16[2,40,1024]{2,1,0:T(8,128)(2,1)S(1)} %collective-permute-done.23.refs_2_, ...), custom_call_target="tpu_custom_call" | custom-call | flops 4294967296 | bytes 8388608 | tf_op jit(solution)/shard_map/attend/pallas_call | solution.py:486
  96.7 1.4 %collective-permute-start.28 = (bf16[4,64,1152]{2,1,0:T(8,128)(2,1)S(1)}, bf16[4,64,1152]{2,1,0:T(8,128)(2,1)S(1)}, u32[]{:S(2)}, u32[]{:S(2)}) collective-permute-start(bf16[4,64,1152]{2,1,0:T(8,128)(2,1)S(1)} %attend.6), channel_id=1, source_target_pairs={{0,2},{2,0},{4,6},{6,4},{8,10},{10,8},{12,14},{14,12},{1,3},{3,1},... | collective-permute-start | bytes 1769480 | tf_op jit(solution)/shard_map/ppermute | solution.py:40
  98.2 1.2 collective-permute-start.26
  99.3 3.2 %collective-permute-start.27 = (bf16[64,1152]{1,0:T(8,128)(2,1)S(1)}, bf16[64,1152]{1,0:T(8,128)(2,1)S(1)}, u32[]{:S(2)}, u32[]{:S(2)}) collective-permute-start(bf16[64,1152]{1,0:T(8,128)(2,1)S(1)} %get-tuple-element.109), channel_id=1, source_target_pairs={{0,12},{2,14},{4,8},{6,10},{8,4},{10,6},{12,0},{14,2},{1,13},{3,15... | collective-permute-start | bytes 442376 | tf_op jit(solution)/shard_map/ppermute | solution.py:40
  102.6 6.9 %attend.7 = (bf16[4,64,1152]{2,1,0:T(8,128)(2,1)S(1)}, bf16[64,1024]{1,0:T(8,128)(2,1)S(1)}) custom-call(s32[6,8]{1,0:T(8,128)S(1)} %pad_add_fusion.meta, bf16[2,40,1024]{2,1,0:T(8,128)(2,1)S(1)} %pad_maximum_fusion.1.refs_0_, bf16[2,40,1024]{2,1,0:T(8,128)(2,1)S(1)} %collective-permute-done.22.refs_1_, ...), custom_call_target="tpu_custom_call" | custom-call | flops 4294967296 | bytes 8388608 | tf_op jit(solution)/shard_map/attend/pallas_call | solution.py:486
  109.5 1.3 %collective-permute-done.28.refs_1_ = bf16[4,64,1152]{2,1,0:T(8,128)(2,1)S(1)} collective-permute-done((bf16[4,64,1152]{2,1,0:T(8,128)(2,1)S(1)}, bf16[4,64,1152]{2,1,0:T(8,128)(2,1)S(1)}, u32[]{:S(2)}, u32[]{:S(2)}) %collective-permute-start.28) | collective-permute-done | bytes 589856 | tf_op jit(solution)/shard_map/ppermute | solution.py:40
  110.8 1.5 %merge.3 = (bf16[64,1152]{1,0:T(8,128)(2,1)S(1)}, bf16[64,1152]{1,0:T(8,128)(2,1)S(1)}, bf16[64,1152]{1,0:T(8,128)(2,1)S(1)}, bf16[64,1152]{1,0:T(8,128)(2,1)S(1)}) custom-call(bf16[4,64,1152]{2,1,0:T(8,128)(2,1)S(1)} %get-tuple-element.113.refs_0_, bf16[4,64,1152]{2,1,0:T(8,128)(2,1)S(1)} %collective-permute-done.28.refs_1_), custom_call_target="tpu_custom_call" | custom-call | tf_op jit(solution)/shard_map/merge/pallas_call | solution.py:283
  112.5 4.3 %collective-permute-start.31 = (bf16[64,1152]{1,0:T(8,128)(2,1)S(1)}, bf16[64,1152]{1,0:T(8,128)(2,1)S(1)}, u32[]{:S(2)}, u32[]{:S(2)}) collective-permute-start(bf16[64,1152]{1,0:T(8,128)(2,1)S(1)} %get-tuple-element.117), channel_id=1, source_target_pairs={{0,12},{2,14},{4,8},{6,10},{8,4},{10,6},{12,0},{14,2},{1,13},{3,15... | collective-permute-start | bytes 442376 | tf_op jit(solution)/shard_map/ppermute | solution.py:40
  116.7 0.7 attend_own.2.refs_4_
  117.5 0.7 attend_own.3.refs_5_
  118.2 1.3 %finish.2.refs_0_ = bf16[1,64,1024]{2,1,0:T(8,128)(2,1)S(1)} custom-call(s32[6,8]{1,0:T(8,128)S(1)} %pad_add_fusion.meta, bf16[64,1152]{1,0:T(8,128)(2,1)S(1)} %get-tuple-element.106.refs_0_, bf16[64,1152]{1,0:T(8,128)(2,1)S(1)} %collective-permute-done.25.refs_1_, bf16[64,1152]{1,0:T(8,128)(2,1)S(1)} %collective-permute-done.26.refs_2_, ...), custom_call_target="tpu_custom_call" | custom-call | tf_op jit(solution)/shard_map/finish/pallas_call | solution.py:531
  119.5 5.0 %collective-permute-done.30.refs_3_ = bf16[64,1152]{1,0:T(8,128)(2,1)S(1)} collective-permute-done((bf16[64,1152]{1,0:T(8,128)(2,1)S(1)}, bf16[64,1152]{1,0:T(8,128)(2,1)S(1)}, u32[]{:S(2)}, u32[]{:S(2)}) %collective-permute-start.30) | collective-permute-done | bytes 147488 | tf_op jit(solution)/shard_map/ppermute | solution.py:40
  124.5 2.0 %finish.3 = bf16[1,64,2048]{2,1,0:T(8,128)(2,1)} custom-call(s32[6,8]{1,0:T(8,128)S(1)} %pad_add_fusion.meta, bf16[1,64,1024]{2,1,0:T(8,128)(2,1)S(1)} %finish.2.refs_0_, bf16[64,1152]{1,0:T(8,128)(2,1)S(1)} %get-tuple-element.114.refs_1_, bf16[64,1152]{1,0:T(8,128)(2,1)S(1)} %collective-permute-done.29.refs_2_, ...), custom_call_target="tpu_custom_call" | custom-call | tf_op jit(solution)/shard_map/finish/pallas_call | solution.py:531
  (48 shorter events, 3.9 us)
Async XLA Ops:
  0.0 4.3 %collective-permute-start = (bf16[1,64,5120]{2,1,0:T(8,128)(2,1)}, bf16[1,64,5120]{2,1,0:T(8,128)(2,1)S(1)}, u32[]{:S(2)}, u32[]{:S(2)}) collective-permute-start(bf16[1,64,5120]{2,1,0:T(8,128)(2,1)} %param.9), channel_id=1, source_target_pairs={{0,16},{1,17},{2,18},{3,19},{4,20},{5,21},{6,22},{7,23},{8,24},{9,... | collective-permute-start | bytes 1966088 | tf_op jit(solution)/shard_map/ppermute | solution.py:570
  5.0 11.1 %collective-permute-start.1 = (bf16[64,640]{1,0:T(8,128)(2,1)S(1)}, bf16[64,640]{1,0:T(8,128)(2,1)S(1)}, u32[]{:S(2)}, u32[]{:S(2)}) collective-permute-start(bf16[64,640]{1,0:T(8,128)(2,1)S(1)} %get-tuple-element.63), channel_id=1, source_target_pairs={{0,10},{2,8},{4,14},{6,12},{8,2},{10,0},{12,6},{14,4},{1,11},{3,9}... | collective-permute-start | bytes 245768 | tf_op jit(solution)/shard_map/ppermute | solution.py:40
  9.4 8.4 %collective-permute-start.2 = (bf16[64,640]{1,0:T(8,128)(2,1)S(1)}, bf16[64,640]{1,0:T(8,128)(2,1)S(1)}, u32[]{:S(2)}, u32[]{:S(2)}) collective-permute-start(bf16[64,640]{1,0:T(8,128)(2,1)S(1)} %get-tuple-element.68), channel_id=1, source_target_pairs={{0,4},{2,6},{4,0},{6,2},{8,12},{10,14},{12,8},{14,10},{1,5},{3,7},... | collective-permute-start | bytes 245768 | tf_op jit(solution)/shard_map/ppermute | solution.py:40
  11.0 12.6 %collective-permute-start.3 = (bf16[64,640]{1,0:T(8,128)(2,1)S(1)}, bf16[64,640]{1,0:T(8,128)(2,1)S(1)}, u32[]{:S(2)}, u32[]{:S(2)}) collective-permute-start(bf16[64,640]{1,0:T(8,128)(2,1)S(1)} %get-tuple-element.69), channel_id=1, source_target_pairs={{0,8},{2,10},{4,12},{6,14},{8,0},{10,2},{12,4},{14,6},{1,9},{3,11}... | collective-permute-start | bytes 245768 | tf_op jit(solution)/shard_map/ppermute | solution.py:40
  11.3 12.3 %collective-permute-start.4 = (bf16[64,640]{1,0:T(8,128)(2,1)S(1)}, bf16[64,640]{1,0:T(8,128)(2,1)S(1)}, u32[]{:S(2)}, u32[]{:S(2)}) collective-permute-start(bf16[64,640]{1,0:T(8,128)(2,1)S(1)} %get-tuple-element.70), channel_id=1, source_target_pairs={{0,12},{2,14},{4,8},{6,10},{8,4},{10,6},{12,0},{14,2},{1,13},{3,15... | collective-permute-start | bytes 245768 | tf_op jit(solution)/shard_map/ppermute | solution.py:40
  13.8 9.8 %collective-permute-start.5 = (bf16[64,640]{1,0:T(8,128)(2,1)S(1)}, bf16[64,640]{1,0:T(8,128)(2,1)S(1)}, u32[]{:S(2)}, u32[]{:S(2)}) collective-permute-start(bf16[64,640]{1,0:T(8,128)(2,1)S(1)} %get-tuple-element.71), channel_id=1, source_target_pairs={{0,2},{2,0},{4,6},{6,4},{8,10},{10,8},{12,14},{14,12},{1,3},{3,1},... | collective-permute-start | bytes 245768 | tf_op jit(solution)/shard_map/ppermute | solution.py:40
  16.1 7.5 %collective-permute-start.6 = (bf16[64,640]{1,0:T(8,128)(2,1)S(1)}, bf16[64,640]{1,0:T(8,128)(2,1)S(1)}, u32[]{:S(2)}, u32[]{:S(2)}) collective-permute-start(bf16[64,640]{1,0:T(8,128)(2,1)S(1)} %get-tuple-element.72), channel_id=1, source_target_pairs={{0,6},{2,4},{4,2},{6,0},{8,14},{10,12},{12,10},{14,8},{1,7},{3,5},... | collective-permute-start | bytes 245768 | tf_op jit(solution)/shard_map/ppermute | solution.py:40
  17.8 7.1 %collective-permute-start.7 = (bf16[64,640]{1,0:T(8,128)(2,1)S(1)}, bf16[64,640]{1,0:T(8,128)(2,1)S(1)}, u32[]{:S(2)}, u32[]{:S(2)}) collective-permute-start(bf16[64,640]{1,0:T(8,128)(2,1)S(1)} %get-tuple-element.73), channel_id=1, source_target_pairs={{0,14},{2,12},{4,10},{6,8},{8,6},{10,4},{12,2},{14,0},{1,15},{3,13... | collective-permute-start | bytes 245768 | tf_op jit(solution)/shard_map/ppermute | solution.py:40
  27.3 8.0 %collective-permute-start.8 = (f16[4,40,1024]{2,1,0:T(8,128)(2,1)S(1)}, f16[4,40,1024]{2,1,0:T(8,128)(2,1)S(1)}, u32[]{:S(2)}, u32[]{:S(2)}) collective-permute-start(f16[4,40,1024]{2,1,0:T(8,128)(2,1)S(1)} %multiply_convert_fusion.1), channel_id=1, source_target_pairs={{0,2},{2,0},{4,6},{6,4},{8,10},{10,8},{12,14},{14,12},{1,3},{3,1},... | collective-permute-start | bytes 983048 | tf_op jit(solution)/shard_map/ppermute | solution.py:40
  35.5 16.7 %collective-permute-start.15 = (f16[4,40,1024]{2,1,0:T(8,128)(2,1)S(1)}, f16[4,40,1024]{2,1,0:T(8,128)(2,1)S(1)}, u32[]{:S(2)}, u32[]{:S(2)}) collective-permute-start(f16[4,40,1024]{2,1,0:T(8,128)(2,1)S(1)} %multiply_convert_fusion), channel_id=1, source_target_pairs={{0,2},{2,0},{4,6},{6,4},{8,10},{10,8},{12,14},{14,12},{1,3},{3,1},... | collective-permute-start | bytes 983048 | tf_op jit(solution)/shard_map/ppermute | solution.py:40
  36.6 6.0 %collective-permute-start.9 = (f16[40,1024]{1,0:T(8,128)(2,1)S(1)}, f16[40,1024]{1,0:T(8,128)(2,1)S(1)}, u32[]{:S(2)}, u32[]{:S(2)}) collective-permute-start(f16[40,1024]{1,0:T(8,128)(2,1)S(1)} %get-tuple-element.81), channel_id=1, source_target_pairs={{0,4},{2,6},{4,0},{6,2},{8,12},{10,14},{12,8},{14,10},{1,5},{3,7},... | collective-permute-start | bytes 245768 | tf_op jit(solution)/shard_map/ppermute | solution.py:40
  38.3 9.4 %collective-permute-start.10 = (f16[40,1024]{1,0:T(8,128)(2,1)S(1)}, f16[40,1024]{1,0:T(8,128)(2,1)S(1)}, u32[]{:S(2)}, u32[]{:S(2)}) collective-permute-start(f16[40,1024]{1,0:T(8,128)(2,1)S(1)} %get-tuple-element.82), channel_id=1, source_target_pairs={{0,8},{2,10},{4,12},{6,14},{8,0},{10,2},{12,4},{14,6},{1,9},{3,11}... | collective-permute-start | bytes 245768 | tf_op jit(solution)/shard_map/ppermute | solution.py:40
  41.2 6.6 %collective-permute-start.11 = (f16[40,1024]{1,0:T(8,128)(2,1)S(1)}, f16[40,1024]{1,0:T(8,128)(2,1)S(1)}, u32[]{:S(2)}, u32[]{:S(2)}) collective-permute-start(f16[40,1024]{1,0:T(8,128)(2,1)S(1)} %get-tuple-element.83), channel_id=1, source_target_pairs={{0,12},{2,14},{4,8},{6,10},{8,4},{10,6},{12,0},{14,2},{1,13},{3,15... | collective-permute-start | bytes 245768 | tf_op jit(solution)/shard_map/ppermute | solution.py:40
  47.8 7.0 %collective-permute-start.14 = (bf16[40,1024]{1,0:T(8,128)(2,1)S(1)}, bf16[40,1024]{1,0:T(8,128)(2,1)S(1)}, u32[]{:S(2)}, u32[]{:S(2)}) collective-permute-start(bf16[40,1024]{1,0:T(8,128)(2,1)S(1)} %add_convert_fusion.1), channel_id=1, source_target_pairs={{0,12},{2,14},{4,8},{6,10},{8,4},{10,6},{12,0},{14,2},{1,13},{3,15... | collective-permute-start | bytes 245768 | tf_op jit(solution)/shard_map/ppermute | solution.py:40
  50.2 11.7 %collective-permute-start.13 = (bf16[40,1024]{1,0:T(8,128)(2,1)S(1)}, bf16[40,1024]{1,0:T(8,128)(2,1)S(1)}, u32[]{:S(2)}, u32[]{:S(2)}) collective-permute-start(bf16[40,1024]{1,0:T(8,128)(2,1)S(1)} %add_convert_fusion.1), channel_id=1, source_target_pairs={{0,8},{2,10},{4,12},{6,14},{8,0},{10,2},{12,4},{14,6},{1,9},{3,11}... | collective-permute-start | bytes 245768 | tf_op jit(solution)/shard_map/ppermute | solution.py:40
  51.1 10.8 %collective-permute-start.12 = (bf16[40,1024]{1,0:T(8,128)(2,1)S(1)}, bf16[40,1024]{1,0:T(8,128)(2,1)S(1)}, u32[]{:S(2)}, u32[]{:S(2)}) collective-permute-start(bf16[40,1024]{1,0:T(8,128)(2,1)S(1)} %add_convert_fusion.1), channel_id=1, source_target_pairs={{0,4},{2,6},{4,0},{6,2},{8,12},{10,14},{12,8},{14,10},{1,5},{3,7},... | collective-permute-start | bytes 245768 | tf_op jit(solution)/shard_map/ppermute | solution.py:40
  52.4 14.5 %collective-permute-start.18 = (f16[40,1024]{1,0:T(8,128)(2,1)S(1)}, f16[40,1024]{1,0:T(8,128)(2,1)S(1)}, u32[]{:S(2)}, u32[]{:S(2)}) collective-permute-start(f16[40,1024]{1,0:T(8,128)(2,1)S(1)} %get-tuple-element.121), channel_id=1, source_target_pairs={{0,12},{2,14},{4,8},{6,10},{8,4},{10,6},{12,0},{14,2},{1,13},{3,15... | collective-permute-start | bytes 245768 | tf_op jit(solution)/shard_map/ppermute | solution.py:40
  54.8 12.2 %collective-permute-start.17 = (f16[40,1024]{1,0:T(8,128)(2,1)S(1)}, f16[40,1024]{1,0:T(8,128)(2,1)S(1)}, u32[]{:S(2)}, u32[]{:S(2)}) collective-permute-start(f16[40,1024]{1,0:T(8,128)(2,1)S(1)} %get-tuple-element.122), channel_id=1, source_target_pairs={{0,8},{2,10},{4,12},{6,14},{8,0},{10,2},{12,4},{14,6},{1,9},{3,11}... | collective-permute-start | bytes 245768 | tf_op jit(solution)/shard_map/ppermute | solution.py:40
  54.8 12.2 %collective-permute-start.16 = (f16[40,1024]{1,0:T(8,128)(2,1)S(1)}, f16[40,1024]{1,0:T(8,128)(2,1)S(1)}, u32[]{:S(2)}, u32[]{:S(2)}) collective-permute-start(f16[40,1024]{1,0:T(8,128)(2,1)S(1)} %get-tuple-element.123), channel_id=1, source_target_pairs={{0,4},{2,6},{4,0},{6,2},{8,12},{10,14},{12,8},{14,10},{1,5},{3,7},... | collective-permute-start | bytes 245768 | tf_op jit(solution)/shard_map/ppermute | solution.py:40
  62.0 8.0 %collective-permute-start.20 = (bf16[4,40,1024]{2,1,0:T(8,128)(2,1)S(1)}, bf16[4,40,1024]{2,1,0:T(8,128)(2,1)S(1)}, u32[]{:S(2)}, u32[]{:S(2)}) collective-permute-start(bf16[4,40,1024]{2,1,0:T(8,128)(2,1)S(1)} %pad_maximum_fusion.refs_0_), channel_id=1, source_target_pairs={{0,2},{2,0},{4,6},{6,4},{8,10},{10,8},{12,14},{14,12},{1,3},{3,1},... | collective-permute-start | bytes 983048 | tf_op jit(solution)/shard_map/ppermute | solution.py:40
  67.0 10.6 %collective-permute-start.19 = (bf16[40,1024]{1,0:T(8,128)(2,1)S(1)}, bf16[40,1024]{1,0:T(8,128)(2,1)S(1)}, u32[]{:S(2)}, u32[]{:S(2)}) collective-permute-start(bf16[40,1024]{1,0:T(8,128)(2,1)S(1)} %add_convert_fusion), channel_id=1, source_target_pairs={{0,2},{2,0},{4,6},{6,4},{8,10},{10,8},{12,14},{14,12},{1,3},{3,1},... | collective-permute-start | bytes 245768 | tf_op jit(solution)/shard_map/ppermute | solution.py:40
  76.3 12.4 %collective-permute-start.21 = (bf16[4,64,1152]{2,1,0:T(8,128)(2,1)S(1)}, bf16[4,64,1152]{2,1,0:T(8,128)(2,1)S(1)}, u32[]{:S(2)}, u32[]{:S(2)}) collective-permute-start(bf16[4,64,1152]{2,1,0:T(8,128)(2,1)S(1)} %attend.4), channel_id=1, source_target_pairs={{0,2},{2,0},{4,6},{6,4},{8,10},{10,8},{12,14},{14,12},{1,3},{3,1},... | collective-permute-start | bytes 1769480 | tf_op jit(solution)/shard_map/ppermute | solution.py:40
  77.7 12.6 %collective-permute-start.24 = (bf16[2,40,1024]{2,1,0:T(8,128)(2,1)S(1)}, bf16[2,40,1024]{2,1,0:T(8,128)(2,1)S(1)}, u32[]{:S(2)}, u32[]{:S(2)}) collective-permute-start(bf16[2,40,1024]{2,1,0:T(8,128)(2,1)S(1)} %pad_maximum_fusion.1.refs_0_), channel_id=1, source_target_pairs={{0,12},{2,14},{4,8},{6,10},{8,4},{10,6},{12,0},{14,2},{1,13},{3,15... | collective-permute-start | bytes 491528 | tf_op jit(solution)/shard_map/ppermute | solution.py:40
  80.6 9.7 %collective-permute-start.23 = (bf16[2,40,1024]{2,1,0:T(8,128)(2,1)S(1)}, bf16[2,40,1024]{2,1,0:T(8,128)(2,1)S(1)}, u32[]{:S(2)}, u32[]{:S(2)}) collective-permute-start(bf16[2,40,1024]{2,1,0:T(8,128)(2,1)S(1)} %pad_maximum_fusion.1.refs_0_), channel_id=1, source_target_pairs={{0,8},{2,10},{4,12},{6,14},{8,0},{10,2},{12,4},{14,6},{1,9},{3,11}... | collective-permute-start | bytes 491528 | tf_op jit(solution)/shard_map/ppermute | solution.py:40
  80.6 9.7 %collective-permute-start.22 = (bf16[2,40,1024]{2,1,0:T(8,128)(2,1)S(1)}, bf16[2,40,1024]{2,1,0:T(8,128)(2,1)S(1)}, u32[]{:S(2)}, u32[]{:S(2)}) collective-permute-start(bf16[2,40,1024]{2,1,0:T(8,128)(2,1)S(1)} %pad_maximum_fusion.1.refs_0_), channel_id=1, source_target_pairs={{0,4},{2,6},{4,0},{6,2},{8,12},{10,14},{12,8},{14,10},{1,5},{3,7},... | collective-permute-start | bytes 491528 | tf_op jit(solution)/shard_map/ppermute | solution.py:40
  96.7 14.0 %collective-permute-start.28 = (bf16[4,64,1152]{2,1,0:T(8,128)(2,1)S(1)}, bf16[4,64,1152]{2,1,0:T(8,128)(2,1)S(1)}, u32[]{:S(2)}, u32[]{:S(2)}) collective-permute-start(bf16[4,64,1152]{2,1,0:T(8,128)(2,1)S(1)} %attend.6), channel_id=1, source_target_pairs={{0,2},{2,0},{4,6},{6,4},{8,10},{10,8},{12,14},{14,12},{1,3},{3,1},... | collective-permute-start | bytes 1769480 | tf_op jit(solution)/shard_map/ppermute | solution.py:40
  98.2 14.3 %collective-permute-start.25 = (bf16[64,1152]{1,0:T(8,128)(2,1)S(1)}, bf16[64,1152]{1,0:T(8,128)(2,1)S(1)}, u32[]{:S(2)}, u32[]{:S(2)}) collective-permute-start(bf16[64,1152]{1,0:T(8,128)(2,1)S(1)} %get-tuple-element.107), channel_id=1, source_target_pairs={{0,4},{2,6},{4,0},{6,2},{8,12},{10,14},{12,8},{14,10},{1,5},{3,7},... | collective-permute-start | bytes 442376 | tf_op jit(solution)/shard_map/ppermute | solution.py:40
  98.2 20.0 %collective-permute-start.26 = (bf16[64,1152]{1,0:T(8,128)(2,1)S(1)}, bf16[64,1152]{1,0:T(8,128)(2,1)S(1)}, u32[]{:S(2)}, u32[]{:S(2)}) collective-permute-start(bf16[64,1152]{1,0:T(8,128)(2,1)S(1)} %get-tuple-element.108), channel_id=1, source_target_pairs={{0,8},{2,10},{4,12},{6,14},{8,0},{10,2},{12,4},{14,6},{1,9},{3,11}... | collective-permute-start | bytes 442376 | tf_op jit(solution)/shard_map/ppermute | solution.py:40
  99.3 18.9 %collective-permute-start.27 = (bf16[64,1152]{1,0:T(8,128)(2,1)S(1)}, bf16[64,1152]{1,0:T(8,128)(2,1)S(1)}, u32[]{:S(2)}, u32[]{:S(2)}) collective-permute-start(bf16[64,1152]{1,0:T(8,128)(2,1)S(1)} %get-tuple-element.109), channel_id=1, source_target_pairs={{0,12},{2,14},{4,8},{6,10},{8,4},{10,6},{12,0},{14,2},{1,13},{3,15... | collective-permute-start | bytes 442376 | tf_op jit(solution)/shard_map/ppermute | solution.py:40
  112.3 7.2 %collective-permute-start.29 = (bf16[64,1152]{1,0:T(8,128)(2,1)S(1)}, bf16[64,1152]{1,0:T(8,128)(2,1)S(1)}, u32[]{:S(2)}, u32[]{:S(2)}) collective-permute-start(bf16[64,1152]{1,0:T(8,128)(2,1)S(1)} %get-tuple-element.115), channel_id=1, source_target_pairs={{0,4},{2,6},{4,0},{6,2},{8,12},{10,14},{12,8},{14,10},{1,5},{3,7},... | collective-permute-start | bytes 442376 | tf_op jit(solution)/shard_map/ppermute | solution.py:40
  112.4 12.2 %collective-permute-start.30 = (bf16[64,1152]{1,0:T(8,128)(2,1)S(1)}, bf16[64,1152]{1,0:T(8,128)(2,1)S(1)}, u32[]{:S(2)}, u32[]{:S(2)}) collective-permute-start(bf16[64,1152]{1,0:T(8,128)(2,1)S(1)} %get-tuple-element.116), channel_id=1, source_target_pairs={{0,8},{2,10},{4,12},{6,14},{8,0},{10,2},{12,4},{14,6},{1,9},{3,11}... | collective-permute-start | bytes 442376 | tf_op jit(solution)/shard_map/ppermute | solution.py:40
  112.5 12.1 %collective-permute-start.31 = (bf16[64,1152]{1,0:T(8,128)(2,1)S(1)}, bf16[64,1152]{1,0:T(8,128)(2,1)S(1)}, u32[]{:S(2)}, u32[]{:S(2)}) collective-permute-start(bf16[64,1152]{1,0:T(8,128)(2,1)S(1)} %get-tuple-element.117), channel_id=1, source_target_pairs={{0,12},{2,14},{4,8},{6,10},{8,4},{10,6},{12,0},{14,2},{1,13},{3,15... | collective-permute-start | bytes 442376 | tf_op jit(solution)/shard_map/ppermute | solution.py:40

commit v3 on v2

--- a/solution.py
+++ b/solution.py
@@ -571,22 +571,21 @@
     depth = query_weight.shape[1]
     hidden = hidden_rows if depth % HD else fetch([hidden_rows])[0]
     slices = split(grid, place, hidden, handed, depth)
-    weight, own = fetch([query_weight, after(response_cache, handed)])
-    x = [slices[0]] + [None] * (grid.n - 1)
-    order = sorted(range(1, grid.n), key=lambda k: (k % grid.zs, k), reverse=True)
-    for k in order:
-        x[k] = grid.swap(slices[k], k // grid.zs, k % grid.zs)
     n = grid.n
     lane = lax.broadcasted_iota(jnp.int32, (1, n), 1)
-    section, shard = after((lax.axis_index("sec"), lax.axis_index("seq")), x[order[2]])
+    section, shard = after((lax.axis_index("sec"), lax.axis_index("seq")), handed)
     meta = jnp.concatenate([
         response_lengths, block_prompts[:, :, 0],
         jnp.pad(prompt_lengths, (0, n - prompt_lengths.shape[0]))[None],
         jnp.where(lane == 0, section, shard).astype(jnp.int32),
     ])
-    half = (local_kv + 1) // 4
-    caches = [fetched(head) for head in range(half)]
-    x[0] = after(x[0], caches)
+    weight, own = fetch([query_weight, after(response_cache, handed)])
+    x = [slices[0]] + [None] * (grid.n - 1)
+    for kz in reversed(range(grid.zs)):
+        for kx in reversed(range(grid.xs)):
+            k = kx * grid.zs + kz
+            if k:
+                x[k] = grid.swap(slices[k], kx, kz)
     part = project(grid, meta, x, weight, bl, share, chunks)
     part = [piece.reshape(grid.zs, share, part_cols) for piece in part]
     part = [part[c * grid.xs:(c + 1) * grid.xs] for c in range(chunks)]
@@ -634,18 +633,21 @@
     def send_z(merged):
         return [merged[0]] + [grid.swap(merged[kz], 0, kz) for kz in range(1, grid.zs)]
 
-    caches += [fetched(head, part[0][-1]) for head in range(half, min(heads + half, local_kv))]
+    half = (local_kv + 1) // 4
+    caches = [fetched(head) for head in range(half)]
     part[0][0] = after(part[0][0], caches)
     held = reduce_x(part[0])
     sends = narrow_z(held)
     if chunks > 1:
         sends, part[1][1] = both(sends, part[1][1])
         later = reduce_x(part[1])
-    mine = sum_z(held, sends, ())
+    caches += [fetched(head, sends) for head in range(half, heads)]
+    mine = sum_z(held, sends, caches)
     column = gather_z(mine)
     if chunks > 1:
+        caches += [fetched(head, mine) for head in range(heads, heads + half)]
         sends = narrow_z(after(later, mine))
-        column = after(column, sends)
+        column = after(column, (caches, sends))
     queries = gather_x(jnp.stack(column))
     if chunks == 1:
         outs, mets = call_far(0, queries)

time: 127 us -> 120 us (0.945)
  waiting for transfers between devices: 20.1 us -> 14.3 us
  starting transfers between devices: 50.2 us -> 48.4 us
    ppermute x31, waiting for transfers between devices: 19.4 us -> 13.6 us  [swap(): return lax.ppermute(value, 'seq', pairs)]
    ppermute x31, starting transfers between devices: 47.8 us -> 46 us  [swap(): return lax.ppermute(value, 'seq', pairs)]
  transfers between devices with their start and end apart: 32 -> 32, of which waited for: 7 -> 7; matrix products, arithmetic and copies ran while one was open for 1% -> 1% of each run, Pallas kernels for 34% -> 36%
where the time goes in v3:
time: 120 us; the launch traced here: 119 us
  Pallas kernels  54.4 us (45%)
  starting transfers between devices  48.4 us (40%)
  waiting for transfers between devices  14.3 us (12%)
  other arithmetic  1.41 us (1%)
    ppermute x31, starting transfers between devices, swap(): return lax.ppermute(value, 'seq', pairs)  46 us
    pallas_call x4, Pallas kernels, attend(): pl.pallas_call(functools.partial(attend_kernel, grid, kx, bl, share, head...  26.3 us
    pallas_call x4, Pallas kernels, fetch_cache(): pl.pallas_call(functools.partial(fetch_cache_kernel, n, chunk, width, fir...  14.5 us
    ppermute x31, waiting for transfers between devices, swap(): return lax.ppermute(value, 'seq', pairs)  13.6 us
    pallas_call x2, Pallas kernels, finish(): pl.pallas_call(functools.partial(finish_kernel, heads, bl, len(done)), gr...  3.27 us
    pallas_call x2, Pallas kernels, merge_column(): pl.pallas_call(functools.partial(merge_kernel, zs, heads), out_shape=[jax...  3.01 us
    pallas_call x2, Pallas kernels, fetch(): pl.pallas_call(fetch_kernel, in_specs=[anywhere] * len(arrays), out_specs...  2.85 us
  transfers between devices with their start and end apart: 32, of which 7 were waited for; matrix products, arithmetic and copies ran while one was open for 1% of the time, Pallas kernels for 36%

profile of v3, /device:TPU:0, one launch (start us, length us, event | category | flops | bytes accessed | tf_op | source)
XLA Modules:
  0.0 118.8 jit_solution(4803111595270097023)
XLA Ops:
  0.0 2.4 %collective-permute-start = (bf16[1,64,5120]{2,1,0:T(8,128)(2,1)}, bf16[1,64,5120]{2,1,0:T(8,128)(2,1)S(1)}, u32[]{:S(2)}, u32[]{:S(2)}) collective-permute-start(bf16[1,64,5120]{2,1,0:T(8,128)(2,1)} %param.9), channel_id=1, source_target_pairs={{0,16},{1,17},{2,18},{3,19},{4,20},{5,21},{6,22},{7,23},{8,24},{9,... | collective-permute-start | bytes 1966088 | tf_op jit(solution)/shard_map/ppermute | solution.py:570
  2.4 1.1 fetch.2.hidden_ref
  3.6 0.7 collective-permute-done.handed_ref
  4.3 0.7 split.1
  5.0 2.5 %collective-permute-start.1 = (bf16[64,640]{1,0:T(8,128)(2,1)S(1)}, bf16[64,640]{1,0:T(8,128)(2,1)S(1)}, u32[]{:S(2)}, u32[]{:S(2)}) collective-permute-start(bf16[64,640]{1,0:T(8,128)(2,1)S(1)} %get-tuple-element.67), channel_id=1, source_target_pairs={{0,4},{2,6},{4,0},{6,2},{8,12},{10,14},{12,8},{14,10},{1,5},{3,7},... | collective-permute-start | bytes 245768 | tf_op jit(solution)/shard_map/ppermute | solution.py:40
  7.5 2.6 %collective-permute-start.2 = (bf16[64,640]{1,0:T(8,128)(2,1)S(1)}, bf16[64,640]{1,0:T(8,128)(2,1)S(1)}, u32[]{:S(2)}, u32[]{:S(2)}) collective-permute-start(bf16[64,640]{1,0:T(8,128)(2,1)S(1)} %get-tuple-element.68), channel_id=1, source_target_pairs={{0,8},{2,10},{4,12},{6,14},{8,0},{10,2},{12,4},{14,6},{1,9},{3,11}... | collective-permute-start | bytes 245768 | tf_op jit(solution)/shard_map/ppermute | solution.py:40
  10.1 1.7 %collective-permute-start.4 = (bf16[64,640]{1,0:T(8,128)(2,1)S(1)}, bf16[64,640]{1,0:T(8,128)(2,1)S(1)}, u32[]{:S(2)}, u32[]{:S(2)}) collective-permute-start(bf16[64,640]{1,0:T(8,128)(2,1)S(1)} %get-tuple-element.70), channel_id=1, source_target_pairs={{0,2},{2,0},{4,6},{6,4},{8,10},{10,8},{12,14},{14,12},{1,3},{3,1},... | collective-permute-start | bytes 245768 | tf_op jit(solution)/shard_map/ppermute | solution.py:40
  11.8 0.6 collective-permute-start.5
  12.4 1.8 %fetch.3 = (bf16[1,640,2048]{2,1,0:T(8,128)(2,1)S(1)}, bf16[1,64,1024]{2,1,0:T(8,128)(2,1)S(1)}) custom-call(bf16[1,640,2048]{2,1,0:T(8,128)(2,1)} %refs_0_.3, bf16[1,64,1024]{2,1,0:T(8,128)(2,1)} %refs_1_), custom_call_target="tpu_custom_call" | custom-call | bytes 2752512 | tf_op jit(solution)/shard_map/fetch/pallas_call | solution.py:115
  14.2 4.5 %collective-permute-start.6 = (bf16[64,640]{1,0:T(8,128)(2,1)S(1)}, bf16[64,640]{1,0:T(8,128)(2,1)S(1)}, u32[]{:S(2)}, u32[]{:S(2)}) collective-permute-start(bf16[64,640]{1,0:T(8,128)(2,1)S(1)} %get-tuple-element.72), channel_id=1, source_target_pairs={{0,10},{2,8},{4,14},{6,12},{8,2},{10,0},{12,6},{14,4},{1,11},{3,9}... | collective-permute-start | bytes 245768 | tf_op jit(solution)/shard_map/ppermute | solution.py:40
  18.7 1.9 %collective-permute-start.7 = (bf16[64,640]{1,0:T(8,128)(2,1)S(1)}, bf16[64,640]{1,0:T(8,128)(2,1)S(1)}, u32[]{:S(2)}, u32[]{:S(2)}) collective-permute-start(bf16[64,640]{1,0:T(8,128)(2,1)S(1)} %get-tuple-element.73), channel_id=1, source_target_pairs={{0,14},{2,12},{4,10},{6,8},{8,6},{10,4},{12,2},{14,0},{1,15},{3,13... | collective-permute-start | bytes 245768 | tf_op jit(solution)/shard_map/ppermute | solution.py:40
  20.6 0.7 pad_add_fusion.meta
  21.3 2.5 %collective-permute-done.6.refs_6_ = bf16[64,640]{1,0:T(8,128)(2,1)S(1)} collective-permute-done((bf16[64,640]{1,0:T(8,128)(2,1)S(1)}, bf16[64,640]{1,0:T(8,128)(2,1)S(1)}, u32[]{:S(2)}, u32[]{:S(2)}) %collective-permute-start.6) | collective-permute-done | bytes 81952 | tf_op jit(solution)/shard_map/ppermute | solution.py:40
  23.8 2.1 %collective-permute-done.7.refs_7_ = bf16[64,640]{1,0:T(8,128)(2,1)S(1)} collective-permute-done((bf16[64,640]{1,0:T(8,128)(2,1)S(1)}, bf16[64,640]{1,0:T(8,128)(2,1)S(1)}, u32[]{:S(2)}, u32[]{:S(2)}) %collective-permute-start.7) | collective-permute-done | bytes 81952 | tf_op jit(solution)/shard_map/ppermute | solution.py:40
  25.9 2.3 %project.1 = (f32[160,1024]{1,0:T(8,128)S(1)}, f32[160,1024]{1,0:T(8,128)S(1)}, f32[160,1024]{1,0:T(8,128)S(1)}, f32[160,1024]{1,0:T(8,128)S(1)}) custom-call(s32[6,8]{1,0:T(8,128)S(1)} %pad_add_fusion.meta, bf16[64,640]{1,0:T(8,128)(2,1)S(1)} %get-tuple-element.66.refs_0_, bf16[64,640]{1,0:T(8,128)(2,1)S(1)} %collective-permute-done.1.refs_1_, ...), custom_call_target="tpu_custom_call" | custom-call | flops 838860800 | bytes 5242880 | tf_op jit(solution)/shard_map/project/pallas_call | solution.py:212
  28.9 3.6 %fetch_cache.4.refs_2_ = bf16[8,2048,256]{2,1,0:T(8,128)(2,1)S(1)} custom-call(s32[6,8]{1,0:T(8,128)S(1)} %pad_add_fusion.meta, bf16[1,8,2048,1024]{3,2,1,0:T(8,128)(2,1)} %cache_ref.7), custom_call_target="tpu_custom_call" | custom-call | bytes 8388608 | tf_op jit(solution)/shard_map/fetch_cache/pallas_call | solution.py:150
  32.5 3.4 %collective-permute-done.8 = f16[4,40,1024]{2,1,0:T(8,128)(2,1)S(1)} collective-permute-done((f16[4,40,1024]{2,1,0:T(8,128)(2,1)S(1)}, f16[4,40,1024]{2,1,0:T(8,128)(2,1)S(1)}, u32[]{:S(2)}, u32[]{:S(2)}) %collective-permute-start.8) | collective-permute-done | bytes 327712 | tf_op jit(solution)/shard_map/ppermute | solution.py:40
  36.1 0.7 collective-permute-start.15
  36.9 1.1 collective-permute-start.9
  38.0 1.6 %collective-permute-start.10 = (f16[40,1024]{1,0:T(8,128)(2,1)S(1)}, f16[40,1024]{1,0:T(8,128)(2,1)S(1)}, u32[]{:S(2)}, u32[]{:S(2)}) collective-permute-start(f16[40,1024]{1,0:T(8,128)(2,1)S(1)} %get-tuple-element.81), channel_id=1, source_target_pairs={{0,8},{2,10},{4,12},{6,14},{8,0},{10,2},{12,4},{14,6},{1,9},{3,11}... | collective-permute-start | bytes 245768 | tf_op jit(solution)/shard_map/ppermute | solution.py:40
  39.6 1.6 %collective-permute-start.11 = (f16[40,1024]{1,0:T(8,128)(2,1)S(1)}, f16[40,1024]{1,0:T(8,128)(2,1)S(1)}, u32[]{:S(2)}, u32[]{:S(2)}) collective-permute-start(f16[40,1024]{1,0:T(8,128)(2,1)S(1)} %get-tuple-element.82), channel_id=1, source_target_pairs={{0,12},{2,14},{4,8},{6,10},{8,4},{10,6},{12,0},{14,2},{1,13},{3,15... | collective-permute-start | bytes 245768 | tf_op jit(solution)/shard_map/ppermute | solution.py:40
  41.2 3.6 %fetch_cache.5.refs_3_ = bf16[8,2048,256]{2,1,0:T(8,128)(2,1)S(1)} custom-call(s32[6,8]{1,0:T(8,128)S(1)} %pad_add_fusion.meta, bf16[1,8,2048,1024]{3,2,1,0:T(8,128)(2,1)} %cache_ref.7), custom_call_target="tpu_custom_call" | custom-call | bytes 8388608 | tf_op jit(solution)/shard_map/fetch_cache/pallas_call | solution.py:150
  44.9 1.1 collective-permute-done.10
  46.1 2.6 %collective-permute-start.14 = (bf16[40,1024]{1,0:T(8,128)(2,1)S(1)}, bf16[40,1024]{1,0:T(8,128)(2,1)S(1)}, u32[]{:S(2)}, u32[]{:S(2)}) collective-permute-start(bf16[40,1024]{1,0:T(8,128)(2,1)S(1)} %add_convert_fusion.1), channel_id=1, source_target_pairs={{0,12},{2,14},{4,8},{6,10},{8,4},{10,6},{12,0},{14,2},{1,13},{3,15... | collective-permute-start | bytes 245768 | tf_op jit(solution)/shard_map/ppermute | solution.py:40
  49.1 1.5 %collective-permute-start.12 = (bf16[40,1024]{1,0:T(8,128)(2,1)S(1)}, bf16[40,1024]{1,0:T(8,128)(2,1)S(1)}, u32[]{:S(2)}, u32[]{:S(2)}) collective-permute-start(bf16[40,1024]{1,0:T(8,128)(2,1)S(1)} %add_convert_fusion.1), channel_id=1, source_target_pairs={{0,4},{2,6},{4,0},{6,2},{8,12},{10,14},{12,8},{14,10},{1,5},{3,7},... | collective-permute-start | bytes 245768 | tf_op jit(solution)/shard_map/ppermute | solution.py:40
  50.5 3.6 %fetch_cache.6.refs_4_ = bf16[8,2048,256]{2,1,0:T(8,128)(2,1)S(1)} custom-call(s32[6,8]{1,0:T(8,128)S(1)} %pad_add_fusion.meta, bf16[1,8,2048,1024]{3,2,1,0:T(8,128)(2,1)} %cache_ref.7), custom_call_target="tpu_custom_call" | custom-call | bytes 8388608 | tf_op jit(solution)/shard_map/fetch_cache/pallas_call | solution.py:150
  54.4 1.2 %collective-permute-start.18 = (f16[40,1024]{1,0:T(8,128)(2,1)S(1)}, f16[40,1024]{1,0:T(8,128)(2,1)S(1)}, u32[]{:S(2)}, u32[]{:S(2)}) collective-permute-start(f16[40,1024]{1,0:T(8,128)(2,1)S(1)} %get-tuple-element.123), channel_id=1, source_target_pairs={{0,12},{2,14},{4,8},{6,10},{8,4},{10,6},{12,0},{14,2},{1,13},{3,15... | collective-permute-start | bytes 245768 | tf_op jit(solution)/shard_map/ppermute | solution.py:40
  55.6 0.7 collective-permute-start.17
  56.3 2.5 %collective-permute-start.16 = (f16[40,1024]{1,0:T(8,128)(2,1)S(1)}, f16[40,1024]{1,0:T(8,128)(2,1)S(1)}, u32[]{:S(2)}, u32[]{:S(2)}) collective-permute-start(f16[40,1024]{1,0:T(8,128)(2,1)S(1)} %get-tuple-element.125), channel_id=1, source_target_pairs={{0,4},{2,6},{4,0},{6,2},{8,12},{10,14},{12,8},{14,10},{1,5},{3,7},... | collective-permute-start | bytes 245768 | tf_op jit(solution)/shard_map/ppermute | solution.py:40
  58.9 1.7 %collective-permute-start.20 = (bf16[4,40,1024]{2,1,0:T(8,128)(2,1)S(1)}, bf16[4,40,1024]{2,1,0:T(8,128)(2,1)S(1)}, u32[]{:S(2)}, u32[]{:S(2)}) collective-permute-start(bf16[4,40,1024]{2,1,0:T(8,128)(2,1)S(1)} %pad_maximum_fusion.refs_0_), channel_id=1, source_target_pairs={{0,2},{2,0},{4,6},{6,4},{8,10},{10,8},{12,14},{14,12},{1,3},{3,1},... | collective-permute-start | bytes 983048 | tf_op jit(solution)/shard_map/ppermute | solution.py:40
  60.6 3.6 %fetch_cache.7.refs_5_ = bf16[8,2048,256]{2,1,0:T(8,128)(2,1)S(1)} custom-call(s32[6,8]{1,0:T(8,128)S(1)} %pad_add_fusion.meta, bf16[1,8,2048,1024]{3,2,1,0:T(8,128)(2,1)} %cache_ref.7), custom_call_target="tpu_custom_call" | custom-call | bytes 8388608 | tf_op jit(solution)/shard_map/fetch_cache/pallas_call | solution.py:150
  64.8 2.1 %collective-permute-done.20.refs_1_ = bf16[4,40,1024]{2,1,0:T(8,128)(2,1)S(1)} collective-permute-done((bf16[4,40,1024]{2,1,0:T(8,128)(2,1)S(1)}, bf16[4,40,1024]{2,1,0:T(8,128)(2,1)S(1)}, u32[]{:S(2)}, u32[]{:S(2)}) %collective-permute-start.20) | collective-permute-done | bytes 327712 | tf_op jit(solution)/shard_map/ppermute | solution.py:40
  66.9 6.8 %attend.4 = bf16[4,64,1152]{2,1,0:T(8,128)(2,1)S(1)} custom-call(s32[6,8]{1,0:T(8,128)S(1)} %pad_add_fusion.meta, bf16[4,40,1024]{2,1,0:T(8,128)(2,1)S(1)} %pad_maximum_fusion.refs_0_, bf16[4,40,1024]{2,1,0:T(8,128)(2,1)S(1)} %collective-permute-done.20.refs_1_, bf16[8,2048,256]{2,1,0:T(8,128)(2,1)S(1)} %fetch_cache.4.refs_2_, ...), custom_call_target="tpu_custom_call" | custom-call | flops 4294967296 | bytes 8388608 | tf_op jit(solution)/shard_map/attend/pallas_call | solution.py:486
  74.3 1.8 %collective-permute-start.23 = (bf16[2,40,1024]{2,1,0:T(8,128)(2,1)S(1)}, bf16[2,40,1024]{2,1,0:T(8,128)(2,1)S(1)}, u32[]{:S(2)}, u32[]{:S(2)}) collective-permute-start(bf16[2,40,1024]{2,1,0:T(8,128)(2,1)S(1)} %pad_maximum_fusion.1.refs_0_), channel_id=1, source_target_pairs={{0,8},{2,10},{4,12},{6,14},{8,0},{10,2},{12,4},{14,6},{1,9},{3,11}... | collective-permute-start | bytes 491528 | tf_op jit(solution)/shard_map/ppermute | solution.py:40
  76.1 2.5 %collective-permute-start.22 = (bf16[2,40,1024]{2,1,0:T(8,128)(2,1)S(1)}, bf16[2,40,1024]{2,1,0:T(8,128)(2,1)S(1)}, u32[]{:S(2)}, u32[]{:S(2)}) collective-permute-start(bf16[2,40,1024]{2,1,0:T(8,128)(2,1)S(1)} %pad_maximum_fusion.1.refs_0_), channel_id=1, source_target_pairs={{0,4},{2,6},{4,0},{6,2},{8,12},{10,14},{12,8},{14,10},{1,5},{3,7},... | collective-permute-start | bytes 491528 | tf_op jit(solution)/shard_map/ppermute | solution.py:40
  78.7 6.2 %attend.5 = (bf16[4,64,1152]{2,1,0:T(8,128)(2,1)S(1)}, bf16[64,1024]{1,0:T(8,128)(2,1)S(1)}) custom-call(s32[6,8]{1,0:T(8,128)S(1)} %pad_add_fusion.meta, bf16[4,40,1024]{2,1,0:T(8,128)(2,1)S(1)} %pad_maximum_fusion.refs_0_, bf16[4,40,1024]{2,1,0:T(8,128)(2,1)S(1)} %collective-permute-done.20.refs_1_, bf16[8,2048,256]{2,1,0:T(8,128)(2,1)S(1)} %fetch_cache.4.refs_2_, ...), custom_call_target="tpu_custom_call" | custom-call | flops 4294967296 | bytes 8388608 | tf_op jit(solution)/shard_map/attend/pallas_call | solution.py:486
  84.9 1.5 %merge.2 = (bf16[64,1152]{1,0:T(8,128)(2,1)S(1)}, bf16[64,1152]{1,0:T(8,128)(2,1)S(1)}, bf16[64,1152]{1,0:T(8,128)(2,1)S(1)}, bf16[64,1152]{1,0:T(8,128)(2,1)S(1)}) custom-call(bf16[4,64,1152]{2,1,0:T(8,128)(2,1)S(1)} %get-tuple-element.98.refs_0_, bf16[4,64,1152]{2,1,0:T(8,128)(2,1)S(1)} %collective-permute-done.21.refs_1_), custom_call_target="tpu_custom_call" | custom-call | tf_op jit(solution)/shard_map/merge/pallas_call | solution.py:283
  86.4 6.8 %attend.6 = bf16[4,64,1152]{2,1,0:T(8,128)(2,1)S(1)} custom-call(s32[6,8]{1,0:T(8,128)S(1)} %pad_add_fusion.meta, bf16[2,40,1024]{2,1,0:T(8,128)(2,1)S(1)} %pad_maximum_fusion.1.refs_0_, bf16[2,40,1024]{2,1,0:T(8,128)(2,1)S(1)} %collective-permute-done.22.refs_1_, bf16[2,40,1024]{2,1,0:T(8,128)(2,1)S(1)} %collective-permute-done.23.refs_2_, ...), custom_call_target="tpu_custom_call" | custom-call | flops 4294967296 | bytes 8388608 | tf_op jit(solution)/shard_map/attend/pallas_call | solution.py:486
  93.3 1.7 %collective-permute-start.28 = (bf16[4,64,1152]{2,1,0:T(8,128)(2,1)S(1)}, bf16[4,64,1152]{2,1,0:T(8,128)(2,1)S(1)}, u32[]{:S(2)}, u32[]{:S(2)}) collective-permute-start(bf16[4,64,1152]{2,1,0:T(8,128)(2,1)S(1)} %attend.6), channel_id=1, source_target_pairs={{0,2},{2,0},{4,6},{6,4},{8,10},{10,8},{12,14},{14,12},{1,3},{3,1},... | collective-permute-start | bytes 1769480 | tf_op jit(solution)/shard_map/ppermute | solution.py:40
  94.9 4.4 %collective-permute-start.27 = (bf16[64,1152]{1,0:T(8,128)(2,1)S(1)}, bf16[64,1152]{1,0:T(8,128)(2,1)S(1)}, u32[]{:S(2)}, u32[]{:S(2)}) collective-permute-start(bf16[64,1152]{1,0:T(8,128)(2,1)S(1)} %get-tuple-element.111), channel_id=1, source_target_pairs={{0,12},{2,14},{4,8},{6,10},{8,4},{10,6},{12,0},{14,2},{1,13},{3,15... | collective-permute-start | bytes 442376 | tf_op jit(solution)/shard_map/ppermute | solution.py:40
  99.3 6.5 %attend.7 = (bf16[4,64,1152]{2,1,0:T(8,128)(2,1)S(1)}, bf16[64,1024]{1,0:T(8,128)(2,1)S(1)}) custom-call(s32[6,8]{1,0:T(8,128)S(1)} %pad_add_fusion.meta, bf16[2,40,1024]{2,1,0:T(8,128)(2,1)S(1)} %pad_maximum_fusion.1.refs_0_, bf16[2,40,1024]{2,1,0:T(8,128)(2,1)S(1)} %collective-permute-done.22.refs_1_, ...), custom_call_target="tpu_custom_call" | custom-call | flops 4294967296 | bytes 8388608 | tf_op jit(solution)/shard_map/attend/pallas_call | solution.py:486
  105.8 1.5 %merge.3 = (bf16[64,1152]{1,0:T(8,128)(2,1)S(1)}, bf16[64,1152]{1,0:T(8,128)(2,1)S(1)}, bf16[64,1152]{1,0:T(8,128)(2,1)S(1)}, bf16[64,1152]{1,0:T(8,128)(2,1)S(1)}) custom-call(bf16[4,64,1152]{2,1,0:T(8,128)(2,1)S(1)} %get-tuple-element.115.refs_0_, bf16[4,64,1152]{2,1,0:T(8,128)(2,1)S(1)} %collective-permute-done.28.refs_1_), custom_call_target="tpu_custom_call" | custom-call | tf_op jit(solution)/shard_map/merge/pallas_call | solution.py:283
  107.5 4.3 %collective-permute-start.31 = (bf16[64,1152]{1,0:T(8,128)(2,1)S(1)}, bf16[64,1152]{1,0:T(8,128)(2,1)S(1)}, u32[]{:S(2)}, u32[]{:S(2)}) collective-permute-start(bf16[64,1152]{1,0:T(8,128)(2,1)S(1)} %get-tuple-element.119), channel_id=1, source_target_pairs={{0,12},{2,14},{4,8},{6,10},{8,4},{10,6},{12,0},{14,2},{1,13},{3,15... | collective-permute-start | bytes 442376 | tf_op jit(solution)/shard_map/ppermute | solution.py:40
  111.8 0.7 attend_own.2.refs_4_
  112.5 0.7 attend_own.3.refs_5_
  113.2 1.3 %finish.2.refs_0_ = bf16[1,64,1024]{2,1,0:T(8,128)(2,1)S(1)} custom-call(s32[6,8]{1,0:T(8,128)S(1)} %pad_add_fusion.meta, bf16[64,1152]{1,0:T(8,128)(2,1)S(1)} %get-tuple-element.108.refs_0_, bf16[64,1152]{1,0:T(8,128)(2,1)S(1)} %collective-permute-done.25.refs_1_, bf16[64,1152]{1,0:T(8,128)(2,1)S(1)} %collective-permute-done.26.refs_2_, ...), custom_call_target="tpu_custom_call" | custom-call | tf_op jit(solution)/shard_map/finish/pallas_call | solution.py:531
  114.5 2.3 %collective-permute-done.30.refs_3_ = bf16[64,1152]{1,0:T(8,128)(2,1)S(1)} collective-permute-done((bf16[64,1152]{1,0:T(8,128)(2,1)S(1)}, bf16[64,1152]{1,0:T(8,128)(2,1)S(1)}, u32[]{:S(2)}, u32[]{:S(2)}) %collective-permute-start.30) | collective-permute-done | bytes 147488 | tf_op jit(solution)/shard_map/ppermute | solution.py:40
  116.9 2.0 %finish.3 = bf16[1,64,2048]{2,1,0:T(8,128)(2,1)} custom-call(s32[6,8]{1,0:T(8,128)S(1)} %pad_add_fusion.meta, bf16[1,64,1024]{2,1,0:T(8,128)(2,1)S(1)} %finish.2.refs_0_, bf16[64,1152]{1,0:T(8,128)(2,1)S(1)} %get-tuple-element.116.refs_1_, bf16[64,1152]{1,0:T(8,128)(2,1)S(1)} %collective-permute-done.29.refs_2_, ...), custom_call_target="tpu_custom_call" | custom-call | tf_op jit(solution)/shard_map/finish/pallas_call | solution.py:531
  (48 shorter events, 2.9 us)
Async XLA Ops:
  0.0 4.3 %collective-permute-start = (bf16[1,64,5120]{2,1,0:T(8,128)(2,1)}, bf16[1,64,5120]{2,1,0:T(8,128)(2,1)S(1)}, u32[]{:S(2)}, u32[]{:S(2)}) collective-permute-start(bf16[1,64,5120]{2,1,0:T(8,128)(2,1)} %param.9), channel_id=1, source_target_pairs={{0,16},{1,17},{2,18},{3,19},{4,20},{5,21},{6,22},{7,23},{8,24},{9,... | collective-permute-start | bytes 1966088 | tf_op jit(solution)/shard_map/ppermute | solution.py:570
  5.0 9.2 %collective-permute-start.1 = (bf16[64,640]{1,0:T(8,128)(2,1)S(1)}, bf16[64,640]{1,0:T(8,128)(2,1)S(1)}, u32[]{:S(2)}, u32[]{:S(2)}) collective-permute-start(bf16[64,640]{1,0:T(8,128)(2,1)S(1)} %get-tuple-element.67), channel_id=1, source_target_pairs={{0,4},{2,6},{4,0},{6,2},{8,12},{10,14},{12,8},{14,10},{1,5},{3,7},... | collective-permute-start | bytes 245768 | tf_op jit(solution)/shard_map/ppermute | solution.py:40
  7.5 11.2 %collective-permute-start.2 = (bf16[64,640]{1,0:T(8,128)(2,1)S(1)}, bf16[64,640]{1,0:T(8,128)(2,1)S(1)}, u32[]{:S(2)}, u32[]{:S(2)}) collective-permute-start(bf16[64,640]{1,0:T(8,128)(2,1)S(1)} %get-tuple-element.68), channel_id=1, source_target_pairs={{0,8},{2,10},{4,12},{6,14},{8,0},{10,2},{12,4},{14,6},{1,9},{3,11}... | collective-permute-start | bytes 245768 | tf_op jit(solution)/shard_map/ppermute | solution.py:40
  10.1 11.3 %collective-permute-start.3 = (bf16[64,640]{1,0:T(8,128)(2,1)S(1)}, bf16[64,640]{1,0:T(8,128)(2,1)S(1)}, u32[]{:S(2)}, u32[]{:S(2)}) collective-permute-start(bf16[64,640]{1,0:T(8,128)(2,1)S(1)} %get-tuple-element.69), channel_id=1, source_target_pairs={{0,12},{2,14},{4,8},{6,10},{8,4},{10,6},{12,0},{14,2},{1,13},{3,15... | collective-permute-start | bytes 245768 | tf_op jit(solution)/shard_map/ppermute | solution.py:40
  10.1 11.3 %collective-permute-start.4 = (bf16[64,640]{1,0:T(8,128)(2,1)S(1)}, bf16[64,640]{1,0:T(8,128)(2,1)S(1)}, u32[]{:S(2)}, u32[]{:S(2)}) collective-permute-start(bf16[64,640]{1,0:T(8,128)(2,1)S(1)} %get-tuple-element.70), channel_id=1, source_target_pairs={{0,2},{2,0},{4,6},{6,4},{8,10},{10,8},{12,14},{14,12},{1,3},{3,1},... | collective-permute-start | bytes 245768 | tf_op jit(solution)/shard_map/ppermute | solution.py:40
  11.8 9.6 %collective-permute-start.5 = (bf16[64,640]{1,0:T(8,128)(2,1)S(1)}, bf16[64,640]{1,0:T(8,128)(2,1)S(1)}, u32[]{:S(2)}, u32[]{:S(2)}) collective-permute-start(bf16[64,640]{1,0:T(8,128)(2,1)S(1)} %get-tuple-element.71), channel_id=1, source_target_pairs={{0,6},{2,4},{4,2},{6,0},{8,14},{10,12},{12,10},{14,8},{1,7},{3,5},... | collective-permute-start | bytes 245768 | tf_op jit(solution)/shard_map/ppermute | solution.py:40
  14.2 9.6 %collective-permute-start.6 = (bf16[64,640]{1,0:T(8,128)(2,1)S(1)}, bf16[64,640]{1,0:T(8,128)(2,1)S(1)}, u32[]{:S(2)}, u32[]{:S(2)}) collective-permute-start(bf16[64,640]{1,0:T(8,128)(2,1)S(1)} %get-tuple-element.72), channel_id=1, source_target_pairs={{0,10},{2,8},{4,14},{6,12},{8,2},{10,0},{12,6},{14,4},{1,11},{3,9}... | collective-permute-start | bytes 245768 | tf_op jit(solution)/shard_map/ppermute | solution.py:40
  18.7 7.2 %collective-permute-start.7 = (bf16[64,640]{1,0:T(8,128)(2,1)S(1)}, bf16[64,640]{1,0:T(8,128)(2,1)S(1)}, u32[]{:S(2)}, u32[]{:S(2)}) collective-permute-start(bf16[64,640]{1,0:T(8,128)(2,1)S(1)} %get-tuple-element.73), channel_id=1, source_target_pairs={{0,14},{2,12},{4,10},{6,8},{8,6},{10,4},{12,2},{14,0},{1,15},{3,13... | collective-permute-start | bytes 245768 | tf_op jit(solution)/shard_map/ppermute | solution.py:40
  28.3 7.6 %collective-permute-start.8 = (f16[4,40,1024]{2,1,0:T(8,128)(2,1)S(1)}, f16[4,40,1024]{2,1,0:T(8,128)(2,1)S(1)}, u32[]{:S(2)}, u32[]{:S(2)}) collective-permute-start(f16[4,40,1024]{2,1,0:T(8,128)(2,1)S(1)} %bitcast.33), channel_id=1, source_target_pairs={{0,2},{2,0},{4,6},{6,4},{8,10},{10,8},{12,14},{14,12},{1,3},{3,1},... | collective-permute-start | bytes 983048 | tf_op jit(solution)/shard_map/ppermute | solution.py:40
  36.1 18.0 %collective-permute-start.15 = (f16[4,40,1024]{2,1,0:T(8,128)(2,1)S(1)}, f16[4,40,1024]{2,1,0:T(8,128)(2,1)S(1)}, u32[]{:S(2)}, u32[]{:S(2)}) collective-permute-start(f16[4,40,1024]{2,1,0:T(8,128)(2,1)S(1)} %multiply_convert_fusion), channel_id=1, source_target_pairs={{0,2},{2,0},{4,6},{6,4},{8,10},{10,8},{12,14},{14,12},{1,3},{3,1},... | collective-permute-start | bytes 983048 | tf_op jit(solution)/shard_map/ppermute | solution.py:40
  36.9 8.0 %collective-permute-start.9 = (f16[40,1024]{1,0:T(8,128)(2,1)S(1)}, f16[40,1024]{1,0:T(8,128)(2,1)S(1)}, u32[]{:S(2)}, u32[]{:S(2)}) collective-permute-start(f16[40,1024]{1,0:T(8,128)(2,1)S(1)} %get-tuple-element.80), channel_id=1, source_target_pairs={{0,4},{2,6},{4,0},{6,2},{8,12},{10,14},{12,8},{14,10},{1,5},{3,7},... | collective-permute-start | bytes 245768 | tf_op jit(solution)/shard_map/ppermute | solution.py:40
  38.0 8.0 %collective-permute-start.10 = (f16[40,1024]{1,0:T(8,128)(2,1)S(1)}, f16[40,1024]{1,0:T(8,128)(2,1)S(1)}, u32[]{:S(2)}, u32[]{:S(2)}) collective-permute-start(f16[40,1024]{1,0:T(8,128)(2,1)S(1)} %get-tuple-element.81), channel_id=1, source_target_pairs={{0,8},{2,10},{4,12},{6,14},{8,0},{10,2},{12,4},{14,6},{1,9},{3,11}... | collective-permute-start | bytes 245768 | tf_op jit(solution)/shard_map/ppermute | solution.py:40
  39.6 6.4 %collective-permute-start.11 = (f16[40,1024]{1,0:T(8,128)(2,1)S(1)}, f16[40,1024]{1,0:T(8,128)(2,1)S(1)}, u32[]{:S(2)}, u32[]{:S(2)}) collective-permute-start(f16[40,1024]{1,0:T(8,128)(2,1)S(1)} %get-tuple-element.82), channel_id=1, source_target_pairs={{0,12},{2,14},{4,8},{6,10},{8,4},{10,6},{12,0},{14,2},{1,13},{3,15... | collective-permute-start | bytes 245768 | tf_op jit(solution)/shard_map/ppermute | solution.py:40
  46.1 10.2 %collective-permute-start.14 = (bf16[40,1024]{1,0:T(8,128)(2,1)S(1)}, bf16[40,1024]{1,0:T(8,128)(2,1)S(1)}, u32[]{:S(2)}, u32[]{:S(2)}) collective-permute-start(bf16[40,1024]{1,0:T(8,128)(2,1)S(1)} %add_convert_fusion.1), channel_id=1, source_target_pairs={{0,12},{2,14},{4,8},{6,10},{8,4},{10,6},{12,0},{14,2},{1,13},{3,15... | collective-permute-start | bytes 245768 | tf_op jit(solution)/shard_map/ppermute | solution.py:40
  48.6 10.2 %collective-permute-start.13 = (bf16[40,1024]{1,0:T(8,128)(2,1)S(1)}, bf16[40,1024]{1,0:T(8,128)(2,1)S(1)}, u32[]{:S(2)}, u32[]{:S(2)}) collective-permute-start(bf16[40,1024]{1,0:T(8,128)(2,1)S(1)} %add_convert_fusion.1), channel_id=1, source_target_pairs={{0,8},{2,10},{4,12},{6,14},{8,0},{10,2},{12,4},{14,6},{1,9},{3,11}... | collective-permute-start | bytes 245768 | tf_op jit(solution)/shard_map/ppermute | solution.py:40
  49.1 9.8 %collective-permute-start.12 = (bf16[40,1024]{1,0:T(8,128)(2,1)S(1)}, bf16[40,1024]{1,0:T(8,128)(2,1)S(1)}, u32[]{:S(2)}, u32[]{:S(2)}) collective-permute-start(bf16[40,1024]{1,0:T(8,128)(2,1)S(1)} %add_convert_fusion.1), channel_id=1, source_target_pairs={{0,4},{2,6},{4,0},{6,2},{8,12},{10,14},{12,8},{14,10},{1,5},{3,7},... | collective-permute-start | bytes 245768 | tf_op jit(solution)/shard_map/ppermute | solution.py:40
  54.4 9.9 %collective-permute-start.18 = (f16[40,1024]{1,0:T(8,128)(2,1)S(1)}, f16[40,1024]{1,0:T(8,128)(2,1)S(1)}, u32[]{:S(2)}, u32[]{:S(2)}) collective-permute-start(f16[40,1024]{1,0:T(8,128)(2,1)S(1)} %get-tuple-element.123), channel_id=1, source_target_pairs={{0,12},{2,14},{4,8},{6,10},{8,4},{10,6},{12,0},{14,2},{1,13},{3,15... | collective-permute-start | bytes 245768 | tf_op jit(solution)/shard_map/ppermute | solution.py:40
  55.6 8.7 %collective-permute-start.17 = (f16[40,1024]{1,0:T(8,128)(2,1)S(1)}, f16[40,1024]{1,0:T(8,128)(2,1)S(1)}, u32[]{:S(2)}, u32[]{:S(2)}) collective-permute-start(f16[40,1024]{1,0:T(8,128)(2,1)S(1)} %get-tuple-element.124), channel_id=1, source_target_pairs={{0,8},{2,10},{4,12},{6,14},{8,0},{10,2},{12,4},{14,6},{1,9},{3,11}... | collective-permute-start | bytes 245768 | tf_op jit(solution)/shard_map/ppermute | solution.py:40
  56.3 8.0 %collective-permute-start.16 = (f16[40,1024]{1,0:T(8,128)(2,1)S(1)}, f16[40,1024]{1,0:T(8,128)(2,1)S(1)}, u32[]{:S(2)}, u32[]{:S(2)}) collective-permute-start(f16[40,1024]{1,0:T(8,128)(2,1)S(1)} %get-tuple-element.125), channel_id=1, source_target_pairs={{0,4},{2,6},{4,0},{6,2},{8,12},{10,14},{12,8},{14,10},{1,5},{3,7},... | collective-permute-start | bytes 245768 | tf_op jit(solution)/shard_map/ppermute | solution.py:40
  58.9 8.0 %collective-permute-start.20 = (bf16[4,40,1024]{2,1,0:T(8,128)(2,1)S(1)}, bf16[4,40,1024]{2,1,0:T(8,128)(2,1)S(1)}, u32[]{:S(2)}, u32[]{:S(2)}) collective-permute-start(bf16[4,40,1024]{2,1,0:T(8,128)(2,1)S(1)} %pad_maximum_fusion.refs_0_), channel_id=1, source_target_pairs={{0,2},{2,0},{4,6},{6,4},{8,10},{10,8},{12,14},{14,12},{1,3},{3,1},... | collective-permute-start | bytes 983048 | tf_op jit(solution)/shard_map/ppermute | solution.py:40
  64.4 9.8 %collective-permute-start.19 = (bf16[40,1024]{1,0:T(8,128)(2,1)S(1)}, bf16[40,1024]{1,0:T(8,128)(2,1)S(1)}, u32[]{:S(2)}, u32[]{:S(2)}) collective-permute-start(bf16[40,1024]{1,0:T(8,128)(2,1)S(1)} %add_convert_fusion), channel_id=1, source_target_pairs={{0,2},{2,0},{4,6},{6,4},{8,10},{10,8},{12,14},{14,12},{1,3},{3,1},... | collective-permute-start | bytes 245768 | tf_op jit(solution)/shard_map/ppermute | solution.py:40
  73.7 11.2 %collective-permute-start.21 = (bf16[4,64,1152]{2,1,0:T(8,128)(2,1)S(1)}, bf16[4,64,1152]{2,1,0:T(8,128)(2,1)S(1)}, u32[]{:S(2)}, u32[]{:S(2)}) collective-permute-start(bf16[4,64,1152]{2,1,0:T(8,128)(2,1)S(1)} %attend.4), channel_id=1, source_target_pairs={{0,2},{2,0},{4,6},{6,4},{8,10},{10,8},{12,14},{14,12},{1,3},{3,1},... | collective-permute-start | bytes 1769480 | tf_op jit(solution)/shard_map/ppermute | solution.py:40
  74.2 12.2 %collective-permute-start.24 = (bf16[2,40,1024]{2,1,0:T(8,128)(2,1)S(1)}, bf16[2,40,1024]{2,1,0:T(8,128)(2,1)S(1)}, u32[]{:S(2)}, u32[]{:S(2)}) collective-permute-start(bf16[2,40,1024]{2,1,0:T(8,128)(2,1)S(1)} %pad_maximum_fusion.1.refs_0_), channel_id=1, source_target_pairs={{0,12},{2,14},{4,8},{6,10},{8,4},{10,6},{12,0},{14,2},{1,13},{3,15... | collective-permute-start | bytes 491528 | tf_op jit(solution)/shard_map/ppermute | solution.py:40
  74.3 12.1 %collective-permute-start.23 = (bf16[2,40,1024]{2,1,0:T(8,128)(2,1)S(1)}, bf16[2,40,1024]{2,1,0:T(8,128)(2,1)S(1)}, u32[]{:S(2)}, u32[]{:S(2)}) collective-permute-start(bf16[2,40,1024]{2,1,0:T(8,128)(2,1)S(1)} %pad_maximum_fusion.1.refs_0_), channel_id=1, source_target_pairs={{0,8},{2,10},{4,12},{6,14},{8,0},{10,2},{12,4},{14,6},{1,9},{3,11}... | collective-permute-start | bytes 491528 | tf_op jit(solution)/shard_map/ppermute | solution.py:40
  76.1 10.3 %collective-permute-start.22 = (bf16[2,40,1024]{2,1,0:T(8,128)(2,1)S(1)}, bf16[2,40,1024]{2,1,0:T(8,128)(2,1)S(1)}, u32[]{:S(2)}, u32[]{:S(2)}) collective-permute-start(bf16[2,40,1024]{2,1,0:T(8,128)(2,1)S(1)} %pad_maximum_fusion.1.refs_0_), channel_id=1, source_target_pairs={{0,4},{2,6},{4,0},{6,2},{8,12},{10,14},{12,8},{14,10},{1,5},{3,7},... | collective-permute-start | bytes 491528 | tf_op jit(solution)/shard_map/ppermute | solution.py:40
  93.3 12.5 %collective-permute-start.28 = (bf16[4,64,1152]{2,1,0:T(8,128)(2,1)S(1)}, bf16[4,64,1152]{2,1,0:T(8,128)(2,1)S(1)}, u32[]{:S(2)}, u32[]{:S(2)}) collective-permute-start(bf16[4,64,1152]{2,1,0:T(8,128)(2,1)S(1)} %attend.6), channel_id=1, source_target_pairs={{0,2},{2,0},{4,6},{6,4},{8,10},{10,8},{12,14},{14,12},{1,3},{3,1},... | collective-permute-start | bytes 1769480 | tf_op jit(solution)/shard_map/ppermute | solution.py:40
  94.9 12.6 %collective-permute-start.25 = (bf16[64,1152]{1,0:T(8,128)(2,1)S(1)}, bf16[64,1152]{1,0:T(8,128)(2,1)S(1)}, u32[]{:S(2)}, u32[]{:S(2)}) collective-permute-start(bf16[64,1152]{1,0:T(8,128)(2,1)S(1)} %get-tuple-element.109), channel_id=1, source_target_pairs={{0,4},{2,6},{4,0},{6,2},{8,12},{10,14},{12,8},{14,10},{1,5},{3,7},... | collective-permute-start | bytes 442376 | tf_op jit(solution)/shard_map/ppermute | solution.py:40
  94.9 18.3 %collective-permute-start.26 = (bf16[64,1152]{1,0:T(8,128)(2,1)S(1)}, bf16[64,1152]{1,0:T(8,128)(2,1)S(1)}, u32[]{:S(2)}, u32[]{:S(2)}) collective-permute-start(bf16[64,1152]{1,0:T(8,128)(2,1)S(1)} %get-tuple-element.110), channel_id=1, source_target_pairs={{0,8},{2,10},{4,12},{6,14},{8,0},{10,2},{12,4},{14,6},{1,9},{3,11}... | collective-permute-start | bytes 442376 | tf_op jit(solution)/shard_map/ppermute | solution.py:40
  94.9 18.3 %collective-permute-start.27 = (bf16[64,1152]{1,0:T(8,128)(2,1)S(1)}, bf16[64,1152]{1,0:T(8,128)(2,1)S(1)}, u32[]{:S(2)}, u32[]{:S(2)}) collective-permute-start(bf16[64,1152]{1,0:T(8,128)(2,1)S(1)} %get-tuple-element.111), channel_id=1, source_target_pairs={{0,12},{2,14},{4,8},{6,10},{8,4},{10,6},{12,0},{14,2},{1,13},{3,15... | collective-permute-start | bytes 442376 | tf_op jit(solution)/shard_map/ppermute | solution.py:40
  107.3 7.2 %collective-permute-start.29 = (bf16[64,1152]{1,0:T(8,128)(2,1)S(1)}, bf16[64,1152]{1,0:T(8,128)(2,1)S(1)}, u32[]{:S(2)}, u32[]{:S(2)}) collective-permute-start(bf16[64,1152]{1,0:T(8,128)(2,1)S(1)} %get-tuple-element.117), channel_id=1, source_target_pairs={{0,4},{2,6},{4,0},{6,2},{8,12},{10,14},{12,8},{14,10},{1,5},{3,7},... | collective-permute-start | bytes 442376 | tf_op jit(solution)/shard_map/ppermute | solution.py:40
  107.4 9.5 %collective-permute-start.30 = (bf16[64,1152]{1,0:T(8,128)(2,1)S(1)}, bf16[64,1152]{1,0:T(8,128)(2,1)S(1)}, u32[]{:S(2)}, u32[]{:S(2)}) collective-permute-start(bf16[64,1152]{1,0:T(8,128)(2,1)S(1)} %get-tuple-element.118), channel_id=1, source_target_pairs={{0,8},{2,10},{4,12},{6,14},{8,0},{10,2},{12,4},{14,6},{1,9},{3,11}... | collective-permute-start | bytes 442376 | tf_op jit(solution)/shard_map/ppermute | solution.py:40
  107.5 9.4 %collective-permute-start.31 = (bf16[64,1152]{1,0:T(8,128)(2,1)S(1)}, bf16[64,1152]{1,0:T(8,128)(2,1)S(1)}, u32[]{:S(2)}, u32[]{:S(2)}) collective-permute-start(bf16[64,1152]{1,0:T(8,128)(2,1)S(1)} %get-tuple-element.119), channel_id=1, source_target_pairs={{0,12},{2,14},{4,8},{6,10},{8,4},{10,6},{12,0},{14,2},{1,13},{3,15... | collective-permute-start | bytes 442376 | tf_op jit(solution)/shard_map/ppermute | solution.py:40

commit v4 on v3

--- a/solution.py
+++ b/solution.py
@@ -634,20 +634,20 @@
         return [merged[0]] + [grid.swap(merged[kz], 0, kz) for kz in range(1, grid.zs)]
 
     half = (local_kv + 1) // 4
-    caches = [fetched(head) for head in range(half)]
+    caches = [fetched(head) for head in range(heads)]
     part[0][0] = after(part[0][0], caches)
     held = reduce_x(part[0])
     sends = narrow_z(held)
     if chunks > 1:
         sends, part[1][1] = both(sends, part[1][1])
         later = reduce_x(part[1])
-    caches += [fetched(head, sends) for head in range(half, heads)]
+    if chunks > 1:
+        caches += [fetched(head, sends) for head in range(heads, heads + half)]
     mine = sum_z(held, sends, caches)
     column = gather_z(mine)
     if chunks > 1:
-        caches += [fetched(head, mine) for head in range(heads, heads + half)]
         sends = narrow_z(after(later, mine))
-        column = after(column, (caches, sends))
+        column = after(column, sends)
     queries = gather_x(jnp.stack(column))
     if chunks == 1:
         outs, mets = call_far(0, queries)

time: 120 us -> 120 us (level); the launches traced: 119 us -> 120 us
  waiting for transfers between devices: 14.3 us -> 19.2 us
  Pallas kernels: 54.4 us -> 52.2 us
  starting transfers between devices: 48.4 us -> 46.9 us
    ppermute x31, waiting for transfers between devices: 13.6 us -> 18.5 us  [swap(): return lax.ppermute(value, 'seq', pairs)]
    ppermute x31, starting transfers between devices: 46 us -> 44.5 us  [swap(): return lax.ppermute(value, 'seq', pairs)]
    pallas_call x4, Pallas kernels: 14.5 us -> 13.2 us  [fetch_cache(): pl.pallas_call(functools.partial(fetch_cache_kernel, n, chunk, width, fir...]
  transfers between devices with their start and end apart: 32 -> 32, of which waited for: 7 -> 9; matrix products, arithmetic and copies ran while one was open for 1% -> 1% of each run, Pallas kernels for 36% -> 34%
where the time goes in v4:
time: 120 us
  Pallas kernels  52.2 us (44%)
  starting transfers between devices  46.9 us (39%)
  waiting for transfers between devices  19.2 us (16%)
  other arithmetic  1.41 us (1%)
    ppermute x31, starting transfers between devices, swap(): return lax.ppermute(value, 'seq', pairs)  44.5 us
    pallas_call x4, Pallas kernels, attend(): pl.pallas_call(functools.partial(attend_kernel, grid, kx, bl, share, head...  25.5 us
    ppermute x31, waiting for transfers between devices, swap(): return lax.ppermute(value, 'seq', pairs)  18.5 us
    pallas_call x4, Pallas kernels, fetch_cache(): pl.pallas_call(functools.partial(fetch_cache_kernel, n, chunk, width, fir...  13.2 us
    pallas_call x2, Pallas kernels, finish(): pl.pallas_call(functools.partial(finish_kernel, heads, bl, len(done)), gr...  3.26 us
    pallas_call x2, Pallas kernels, merge_column(): pl.pallas_call(functools.partial(merge_kernel, zs, heads), out_shape=[jax...  3.01 us
    pallas_call x2, Pallas kernels, fetch(): pl.pallas_call(fetch_kernel, in_specs=[anywhere] * len(arrays), out_specs...  2.85 us
  transfers between devices with their start and end apart: 32, of which 9 were waited for; matrix products, arithmetic and copies ran while one was open for 1% of the time, Pallas kernels for 34%

profile of v4, /device:TPU:0, one launch (start us, length us, event | category | flops | bytes accessed | tf_op | source)
XLA Modules:
  0.0 120.2 jit_solution(6709311546708212730)
XLA Ops:
  0.0 2.4 %collective-permute-start = (bf16[1,64,5120]{2,1,0:T(8,128)(2,1)}, bf16[1,64,5120]{2,1,0:T(8,128)(2,1)S(1)}, u32[]{:S(2)}, u32[]{:S(2)}) collective-permute-start(bf16[1,64,5120]{2,1,0:T(8,128)(2,1)} %param.9), channel_id=1, source_target_pairs={{0,16},{1,17},{2,18},{3,19},{4,20},{5,21},{6,22},{7,23},{8,24},{9,... | collective-permute-start | bytes 1966088 | tf_op jit(solution)/shard_map/ppermute | solution.py:570
  2.4 1.1 fetch.2.hidden_ref
  3.6 0.7 collective-permute-done.handed_ref
  4.3 0.7 split.1
  5.0 2.5 %collective-permute-start.1 = (bf16[64,640]{1,0:T(8,128)(2,1)S(1)}, bf16[64,640]{1,0:T(8,128)(2,1)S(1)}, u32[]{:S(2)}, u32[]{:S(2)}) collective-permute-start(bf16[64,640]{1,0:T(8,128)(2,1)S(1)} %get-tuple-element.66), channel_id=1, source_target_pairs={{0,4},{2,6},{4,0},{6,2},{8,12},{10,14},{12,8},{14,10},{1,5},{3,7},... | collective-permute-start | bytes 245768 | tf_op jit(solution)/shard_map/ppermute | solution.py:40
  7.5 2.6 %collective-permute-start.2 = (bf16[64,640]{1,0:T(8,128)(2,1)S(1)}, bf16[64,640]{1,0:T(8,128)(2,1)S(1)}, u32[]{:S(2)}, u32[]{:S(2)}) collective-permute-start(bf16[64,640]{1,0:T(8,128)(2,1)S(1)} %get-tuple-element.67), channel_id=1, source_target_pairs={{0,8},{2,10},{4,12},{6,14},{8,0},{10,2},{12,4},{14,6},{1,9},{3,11}... | collective-permute-start | bytes 245768 | tf_op jit(solution)/shard_map/ppermute | solution.py:40
  10.1 1.7 %collective-permute-start.4 = (bf16[64,640]{1,0:T(8,128)(2,1)S(1)}, bf16[64,640]{1,0:T(8,128)(2,1)S(1)}, u32[]{:S(2)}, u32[]{:S(2)}) collective-permute-start(bf16[64,640]{1,0:T(8,128)(2,1)S(1)} %get-tuple-element.69), channel_id=1, source_target_pairs={{0,2},{2,0},{4,6},{6,4},{8,10},{10,8},{12,14},{14,12},{1,3},{3,1},... | collective-permute-start | bytes 245768 | tf_op jit(solution)/shard_map/ppermute | solution.py:40
  11.8 0.6 collective-permute-start.5
  12.4 1.8 %fetch.3 = (bf16[1,640,2048]{2,1,0:T(8,128)(2,1)S(1)}, bf16[1,64,1024]{2,1,0:T(8,128)(2,1)S(1)}) custom-call(bf16[1,640,2048]{2,1,0:T(8,128)(2,1)} %refs_0_.3, bf16[1,64,1024]{2,1,0:T(8,128)(2,1)} %refs_1_), custom_call_target="tpu_custom_call" | custom-call | bytes 2752512 | tf_op jit(solution)/shard_map/fetch/pallas_call | solution.py:115
  14.2 4.5 %collective-permute-start.6 = (bf16[64,640]{1,0:T(8,128)(2,1)S(1)}, bf16[64,640]{1,0:T(8,128)(2,1)S(1)}, u32[]{:S(2)}, u32[]{:S(2)}) collective-permute-start(bf16[64,640]{1,0:T(8,128)(2,1)S(1)} %get-tuple-element.71), channel_id=1, source_target_pairs={{0,10},{2,8},{4,14},{6,12},{8,2},{10,0},{12,6},{14,4},{1,11},{3,9}... | collective-permute-start | bytes 245768 | tf_op jit(solution)/shard_map/ppermute | solution.py:40
  18.7 1.9 %collective-permute-start.7 = (bf16[64,640]{1,0:T(8,128)(2,1)S(1)}, bf16[64,640]{1,0:T(8,128)(2,1)S(1)}, u32[]{:S(2)}, u32[]{:S(2)}) collective-permute-start(bf16[64,640]{1,0:T(8,128)(2,1)S(1)} %get-tuple-element.72), channel_id=1, source_target_pairs={{0,14},{2,12},{4,10},{6,8},{8,6},{10,4},{12,2},{14,0},{1,15},{3,13... | collective-permute-start | bytes 245768 | tf_op jit(solution)/shard_map/ppermute | solution.py:40
  20.6 0.7 pad_add_fusion.meta
  21.3 2.5 %collective-permute-done.6.refs_6_ = bf16[64,640]{1,0:T(8,128)(2,1)S(1)} collective-permute-done((bf16[64,640]{1,0:T(8,128)(2,1)S(1)}, bf16[64,640]{1,0:T(8,128)(2,1)S(1)}, u32[]{:S(2)}, u32[]{:S(2)}) %collective-permute-start.6) | collective-permute-done | bytes 81952 | tf_op jit(solution)/shard_map/ppermute | solution.py:40
  23.8 2.1 %collective-permute-done.7.refs_7_ = bf16[64,640]{1,0:T(8,128)(2,1)S(1)} collective-permute-done((bf16[64,640]{1,0:T(8,128)(2,1)S(1)}, bf16[64,640]{1,0:T(8,128)(2,1)S(1)}, u32[]{:S(2)}, u32[]{:S(2)}) %collective-permute-start.7) | collective-permute-done | bytes 81952 | tf_op jit(solution)/shard_map/ppermute | solution.py:40
  25.9 2.3 %project.1 = (f32[160,1024]{1,0:T(8,128)S(1)}, f32[160,1024]{1,0:T(8,128)S(1)}, f32[160,1024]{1,0:T(8,128)S(1)}, f32[160,1024]{1,0:T(8,128)S(1)}) custom-call(s32[6,8]{1,0:T(8,128)S(1)} %pad_add_fusion.meta, bf16[64,640]{1,0:T(8,128)(2,1)S(1)} %get-tuple-element.65.refs_0_, bf16[64,640]{1,0:T(8,128)(2,1)S(1)} %collective-permute-done.1.refs_1_, ...), custom_call_target="tpu_custom_call" | custom-call | flops 838860800 | bytes 5242880 | tf_op jit(solution)/shard_map/project/pallas_call | solution.py:212
  28.3 0.6 collective-permute-start.8
  28.9 3.3 %fetch_cache.5.refs_3_ = bf16[8,2048,256]{2,1,0:T(8,128)(2,1)S(1)} custom-call(s32[6,8]{1,0:T(8,128)S(1)} %pad_add_fusion.meta, bf16[1,8,2048,1024]{3,2,1,0:T(8,128)(2,1)} %cache_ref.7), custom_call_target="tpu_custom_call" | custom-call | bytes 8388608 | tf_op jit(solution)/shard_map/fetch_cache/pallas_call | solution.py:150
  32.2 3.3 %fetch_cache.4.refs_2_ = bf16[8,2048,256]{2,1,0:T(8,128)(2,1)S(1)} custom-call(s32[6,8]{1,0:T(8,128)S(1)} %pad_add_fusion.meta, bf16[1,8,2048,1024]{3,2,1,0:T(8,128)(2,1)} %cache_ref.7), custom_call_target="tpu_custom_call" | custom-call | bytes 8388608 | tf_op jit(solution)/shard_map/fetch_cache/pallas_call | solution.py:150
  36.3 1.7 %collective-permute-start.9 = (f16[40,1024]{1,0:T(8,128)(2,1)S(1)}, f16[40,1024]{1,0:T(8,128)(2,1)S(1)}, u32[]{:S(2)}, u32[]{:S(2)}) collective-permute-start(f16[40,1024]{1,0:T(8,128)(2,1)S(1)} %get-tuple-element.79), channel_id=1, source_target_pairs={{0,4},{2,6},{4,0},{6,2},{8,12},{10,14},{12,8},{14,10},{1,5},{3,7},... | collective-permute-start | bytes 245768 | tf_op jit(solution)/shard_map/ppermute | solution.py:40
  38.0 1.6 %collective-permute-start.10 = (f16[40,1024]{1,0:T(8,128)(2,1)S(1)}, f16[40,1024]{1,0:T(8,128)(2,1)S(1)}, u32[]{:S(2)}, u32[]{:S(2)}) collective-permute-start(f16[40,1024]{1,0:T(8,128)(2,1)S(1)} %get-tuple-element.80), channel_id=1, source_target_pairs={{0,8},{2,10},{4,12},{6,14},{8,0},{10,2},{12,4},{14,6},{1,9},{3,11}... | collective-permute-start | bytes 245768 | tf_op jit(solution)/shard_map/ppermute | solution.py:40
  39.6 1.5 %collective-permute-start.11 = (f16[40,1024]{1,0:T(8,128)(2,1)S(1)}, f16[40,1024]{1,0:T(8,128)(2,1)S(1)}, u32[]{:S(2)}, u32[]{:S(2)}) collective-permute-start(f16[40,1024]{1,0:T(8,128)(2,1)S(1)} %get-tuple-element.81), channel_id=1, source_target_pairs={{0,12},{2,14},{4,8},{6,10},{8,4},{10,6},{12,0},{14,2},{1,13},{3,15... | collective-permute-start | bytes 245768 | tf_op jit(solution)/shard_map/ppermute | solution.py:40
  41.1 3.3 %fetch_cache.6.refs_4_ = bf16[8,2048,256]{2,1,0:T(8,128)(2,1)S(1)} custom-call(s32[6,8]{1,0:T(8,128)S(1)} %pad_add_fusion.meta, bf16[1,8,2048,1024]{3,2,1,0:T(8,128)(2,1)} %cache_ref.7), custom_call_target="tpu_custom_call" | custom-call | bytes 8388608 | tf_op jit(solution)/shard_map/fetch_cache/pallas_call | solution.py:150
  44.4 1.6 %collective-permute-done.10 = f16[40,1024]{1,0:T(8,128)(2,1)S(1)} collective-permute-done((f16[40,1024]{1,0:T(8,128)(2,1)S(1)}, f16[40,1024]{1,0:T(8,128)(2,1)S(1)}, u32[]{:S(2)}, u32[]{:S(2)}) %collective-permute-start.10) | collective-permute-done | bytes 81952 | tf_op jit(solution)/shard_map/ppermute | solution.py:40
  46.1 2.6 %collective-permute-start.14 = (bf16[40,1024]{1,0:T(8,128)(2,1)S(1)}, bf16[40,1024]{1,0:T(8,128)(2,1)S(1)}, u32[]{:S(2)}, u32[]{:S(2)}) collective-permute-start(bf16[40,1024]{1,0:T(8,128)(2,1)S(1)} %add_convert_fusion.1), channel_id=1, source_target_pairs={{0,12},{2,14},{4,8},{6,10},{8,4},{10,6},{12,0},{14,2},{1,13},{3,15... | collective-permute-start | bytes 245768 | tf_op jit(solution)/shard_map/ppermute | solution.py:40
  48.6 0.4 collective-permute-start.13
  49.1 1.5 %collective-permute-start.12 = (bf16[40,1024]{1,0:T(8,128)(2,1)S(1)}, bf16[40,1024]{1,0:T(8,128)(2,1)S(1)}, u32[]{:S(2)}, u32[]{:S(2)}) collective-permute-start(bf16[40,1024]{1,0:T(8,128)(2,1)S(1)} %add_convert_fusion.1), channel_id=1, source_target_pairs={{0,4},{2,6},{4,0},{6,2},{8,12},{10,14},{12,8},{14,10},{1,5},{3,7},... | collective-permute-start | bytes 245768 | tf_op jit(solution)/shard_map/ppermute | solution.py:40
  50.7 2.5 %collective-permute-start.18 = (f16[40,1024]{1,0:T(8,128)(2,1)S(1)}, f16[40,1024]{1,0:T(8,128)(2,1)S(1)}, u32[]{:S(2)}, u32[]{:S(2)}) collective-permute-start(f16[40,1024]{1,0:T(8,128)(2,1)S(1)} %get-tuple-element.121), channel_id=1, source_target_pairs={{0,12},{2,14},{4,8},{6,10},{8,4},{10,6},{12,0},{14,2},{1,13},{3,15... | collective-permute-start | bytes 245768 | tf_op jit(solution)/shard_map/ppermute | solution.py:40
  53.3 2.8 %collective-permute-start.16 = (f16[40,1024]{1,0:T(8,128)(2,1)S(1)}, f16[40,1024]{1,0:T(8,128)(2,1)S(1)}, u32[]{:S(2)}, u32[]{:S(2)}) collective-permute-start(f16[40,1024]{1,0:T(8,128)(2,1)S(1)} %get-tuple-element.123), channel_id=1, source_target_pairs={{0,4},{2,6},{4,0},{6,2},{8,12},{10,14},{12,8},{14,10},{1,5},{3,7},... | collective-permute-start | bytes 245768 | tf_op jit(solution)/shard_map/ppermute | solution.py:40
  56.1 3.8 %collective-permute-done.13 = bf16[40,1024]{1,0:T(8,128)(2,1)S(1)} collective-permute-done((bf16[40,1024]{1,0:T(8,128)(2,1)S(1)}, bf16[40,1024]{1,0:T(8,128)(2,1)S(1)}, u32[]{:S(2)}, u32[]{:S(2)}) %collective-permute-start.13) | collective-permute-done | bytes 81952 | tf_op jit(solution)/shard_map/ppermute | solution.py:40
  60.0 1.9 %collective-permute-start.20 = (bf16[4,40,1024]{2,1,0:T(8,128)(2,1)S(1)}, bf16[4,40,1024]{2,1,0:T(8,128)(2,1)S(1)}, u32[]{:S(2)}, u32[]{:S(2)}) collective-permute-start(bf16[4,40,1024]{2,1,0:T(8,128)(2,1)S(1)} %pad_maximum_fusion.refs_0_), channel_id=1, source_target_pairs={{0,2},{2,0},{4,6},{6,4},{8,10},{10,8},{12,14},{14,12},{1,3},{3,1},... | collective-permute-start | bytes 983048 | tf_op jit(solution)/shard_map/ppermute | solution.py:40
  61.9 3.3 %fetch_cache.7.refs_5_ = bf16[8,2048,256]{2,1,0:T(8,128)(2,1)S(1)} custom-call(s32[6,8]{1,0:T(8,128)S(1)} %pad_add_fusion.meta, bf16[1,8,2048,1024]{3,2,1,0:T(8,128)(2,1)} %cache_ref.7), custom_call_target="tpu_custom_call" | custom-call | bytes 8388608 | tf_op jit(solution)/shard_map/fetch_cache/pallas_call | solution.py:150
  65.4 2.2 %collective-permute-done.20.refs_1_ = bf16[4,40,1024]{2,1,0:T(8,128)(2,1)S(1)} collective-permute-done((bf16[4,40,1024]{2,1,0:T(8,128)(2,1)S(1)}, bf16[4,40,1024]{2,1,0:T(8,128)(2,1)S(1)}, u32[]{:S(2)}, u32[]{:S(2)}) %collective-permute-start.20) | collective-permute-done | bytes 327712 | tf_op jit(solution)/shard_map/ppermute | solution.py:40
  67.5 6.4 %attend.4 = bf16[4,64,1152]{2,1,0:T(8,128)(2,1)S(1)} custom-call(s32[6,8]{1,0:T(8,128)S(1)} %pad_add_fusion.meta, bf16[4,40,1024]{2,1,0:T(8,128)(2,1)S(1)} %pad_maximum_fusion.refs_0_, bf16[4,40,1024]{2,1,0:T(8,128)(2,1)S(1)} %collective-permute-done.20.refs_1_, bf16[8,2048,256]{2,1,0:T(8,128)(2,1)S(1)} %fetch_cache.4.refs_2_, ...), custom_call_target="tpu_custom_call" | custom-call | flops 4294967296 | bytes 8388608 | tf_op jit(solution)/shard_map/attend/pallas_call | solution.py:486
  74.2 4.3 %collective-permute-start.22 = (bf16[2,40,1024]{2,1,0:T(8,128)(2,1)S(1)}, bf16[2,40,1024]{2,1,0:T(8,128)(2,1)S(1)}, u32[]{:S(2)}, u32[]{:S(2)}) collective-permute-start(bf16[2,40,1024]{2,1,0:T(8,128)(2,1)S(1)} %pad_maximum_fusion.1.refs_0_), channel_id=1, source_target_pairs={{0,4},{2,6},{4,0},{6,2},{8,12},{10,14},{12,8},{14,10},{1,5},{3,7},... | collective-permute-start | bytes 491528 | tf_op jit(solution)/shard_map/ppermute | solution.py:40
  78.5 6.2 %attend.5 = (bf16[4,64,1152]{2,1,0:T(8,128)(2,1)S(1)}, bf16[64,1024]{1,0:T(8,128)(2,1)S(1)}) custom-call(s32[6,8]{1,0:T(8,128)S(1)} %pad_add_fusion.meta, bf16[4,40,1024]{2,1,0:T(8,128)(2,1)S(1)} %pad_maximum_fusion.refs_0_, bf16[4,40,1024]{2,1,0:T(8,128)(2,1)S(1)} %collective-permute-done.20.refs_1_, bf16[8,2048,256]{2,1,0:T(8,128)(2,1)S(1)} %fetch_cache.4.refs_2_, ...), custom_call_target="tpu_custom_call" | custom-call | flops 4294967296 | bytes 8388608 | tf_op jit(solution)/shard_map/attend/pallas_call | solution.py:486
  84.7 1.5 %merge.2 = (bf16[64,1152]{1,0:T(8,128)(2,1)S(1)}, bf16[64,1152]{1,0:T(8,128)(2,1)S(1)}, bf16[64,1152]{1,0:T(8,128)(2,1)S(1)}, bf16[64,1152]{1,0:T(8,128)(2,1)S(1)}) custom-call(bf16[4,64,1152]{2,1,0:T(8,128)(2,1)S(1)} %get-tuple-element.96.refs_0_, bf16[4,64,1152]{2,1,0:T(8,128)(2,1)S(1)} %collective-permute-done.21.refs_1_), custom_call_target="tpu_custom_call" | custom-call | tf_op jit(solution)/shard_map/merge/pallas_call | solution.py:283
  86.2 6.4 %attend.6 = bf16[4,64,1152]{2,1,0:T(8,128)(2,1)S(1)} custom-call(s32[6,8]{1,0:T(8,128)S(1)} %pad_add_fusion.meta, bf16[2,40,1024]{2,1,0:T(8,128)(2,1)S(1)} %pad_maximum_fusion.1.refs_0_, bf16[2,40,1024]{2,1,0:T(8,128)(2,1)S(1)} %collective-permute-done.22.refs_1_, bf16[2,40,1024]{2,1,0:T(8,128)(2,1)S(1)} %collective-permute-done.23.refs_2_, ...), custom_call_target="tpu_custom_call" | custom-call | flops 4294967296 | bytes 8388608 | tf_op jit(solution)/shard_map/attend/pallas_call | solution.py:486
  92.9 4.3 %collective-permute-start.27 = (bf16[64,1152]{1,0:T(8,128)(2,1)S(1)}, bf16[64,1152]{1,0:T(8,128)(2,1)S(1)}, u32[]{:S(2)}, u32[]{:S(2)}) collective-permute-start(bf16[64,1152]{1,0:T(8,128)(2,1)S(1)} %get-tuple-element.109), channel_id=1, source_target_pairs={{0,12},{2,14},{4,8},{6,10},{8,4},{10,6},{12,0},{14,2},{1,13},{3,15... | collective-permute-start | bytes 442376 | tf_op jit(solution)/shard_map/ppermute | solution.py:40
  97.2 6.5 %attend.7 = (bf16[4,64,1152]{2,1,0:T(8,128)(2,1)S(1)}, bf16[64,1024]{1,0:T(8,128)(2,1)S(1)}) custom-call(s32[6,8]{1,0:T(8,128)S(1)} %pad_add_fusion.meta, bf16[2,40,1024]{2,1,0:T(8,128)(2,1)S(1)} %pad_maximum_fusion.1.refs_0_, bf16[2,40,1024]{2,1,0:T(8,128)(2,1)S(1)} %collective-permute-done.22.refs_1_, ...), custom_call_target="tpu_custom_call" | custom-call | flops 4294967296 | bytes 8388608 | tf_op jit(solution)/shard_map/attend/pallas_call | solution.py:486
  103.7 1.6 %collective-permute-done.28.refs_1_ = bf16[4,64,1152]{2,1,0:T(8,128)(2,1)S(1)} collective-permute-done((bf16[4,64,1152]{2,1,0:T(8,128)(2,1)S(1)}, bf16[4,64,1152]{2,1,0:T(8,128)(2,1)S(1)}, u32[]{:S(2)}, u32[]{:S(2)}) %collective-permute-start.28) | collective-permute-done | bytes 589856 | tf_op jit(solution)/shard_map/ppermute | solution.py:40
  105.3 1.5 %merge.3 = (bf16[64,1152]{1,0:T(8,128)(2,1)S(1)}, bf16[64,1152]{1,0:T(8,128)(2,1)S(1)}, bf16[64,1152]{1,0:T(8,128)(2,1)S(1)}, bf16[64,1152]{1,0:T(8,128)(2,1)S(1)}) custom-call(bf16[4,64,1152]{2,1,0:T(8,128)(2,1)S(1)} %get-tuple-element.113.refs_0_, bf16[4,64,1152]{2,1,0:T(8,128)(2,1)S(1)} %collective-permute-done.28.refs_1_), custom_call_target="tpu_custom_call" | custom-call | tf_op jit(solution)/shard_map/merge/pallas_call | solution.py:283
  106.9 0.5 collective-permute-start.30
  107.5 3.8 %collective-permute-start.31 = (bf16[64,1152]{1,0:T(8,128)(2,1)S(1)}, bf16[64,1152]{1,0:T(8,128)(2,1)S(1)}, u32[]{:S(2)}, u32[]{:S(2)}) collective-permute-start(bf16[64,1152]{1,0:T(8,128)(2,1)S(1)} %get-tuple-element.117), channel_id=1, source_target_pairs={{0,12},{2,14},{4,8},{6,10},{8,4},{10,6},{12,0},{14,2},{1,13},{3,15... | collective-permute-start | bytes 442376 | tf_op jit(solution)/shard_map/ppermute | solution.py:40
  111.3 0.7 attend_own.2.refs_4_
  112.0 0.7 attend_own.3.refs_5_
  112.8 1.3 %finish.2.refs_0_ = bf16[1,64,1024]{2,1,0:T(8,128)(2,1)S(1)} custom-call(s32[6,8]{1,0:T(8,128)S(1)} %pad_add_fusion.meta, bf16[64,1152]{1,0:T(8,128)(2,1)S(1)} %get-tuple-element.106.refs_0_, bf16[64,1152]{1,0:T(8,128)(2,1)S(1)} %collective-permute-done.25.refs_1_, bf16[64,1152]{1,0:T(8,128)(2,1)S(1)} %collective-permute-done.26.refs_2_, ...), custom_call_target="tpu_custom_call" | custom-call | tf_op jit(solution)/shard_map/finish/pallas_call | solution.py:531
  114.1 4.1 %collective-permute-done.30.refs_3_ = bf16[64,1152]{1,0:T(8,128)(2,1)S(1)} collective-permute-done((bf16[64,1152]{1,0:T(8,128)(2,1)S(1)}, bf16[64,1152]{1,0:T(8,128)(2,1)S(1)}, u32[]{:S(2)}, u32[]{:S(2)}) %collective-permute-start.30) | collective-permute-done | bytes 147488 | tf_op jit(solution)/shard_map/ppermute | solution.py:40
  118.2 2.0 %finish.3 = bf16[1,64,2048]{2,1,0:T(8,128)(2,1)} custom-call(s32[6,8]{1,0:T(8,128)S(1)} %pad_add_fusion.meta, bf16[1,64,1024]{2,1,0:T(8,128)(2,1)S(1)} %finish.2.refs_0_, bf16[64,1152]{1,0:T(8,128)(2,1)S(1)} %get-tuple-element.114.refs_1_, bf16[64,1152]{1,0:T(8,128)(2,1)S(1)} %collective-permute-done.29.refs_2_, ...), custom_call_target="tpu_custom_call" | custom-call | tf_op jit(solution)/shard_map/finish/pallas_call | solution.py:531
  (48 shorter events, 1.9 us)
Async XLA Ops:
  0.0 4.3 %collective-permute-start = (bf16[1,64,5120]{2,1,0:T(8,128)(2,1)}, bf16[1,64,5120]{2,1,0:T(8,128)(2,1)S(1)}, u32[]{:S(2)}, u32[]{:S(2)}) collective-permute-start(bf16[1,64,5120]{2,1,0:T(8,128)(2,1)} %param.9), channel_id=1, source_target_pairs={{0,16},{1,17},{2,18},{3,19},{4,20},{5,21},{6,22},{7,23},{8,24},{9,... | collective-permute-start | bytes 1966088 | tf_op jit(solution)/shard_map/ppermute | solution.py:570
  5.0 9.2 %collective-permute-start.1 = (bf16[64,640]{1,0:T(8,128)(2,1)S(1)}, bf16[64,640]{1,0:T(8,128)(2,1)S(1)}, u32[]{:S(2)}, u32[]{:S(2)}) collective-permute-start(bf16[64,640]{1,0:T(8,128)(2,1)S(1)} %get-tuple-element.66), channel_id=1, source_target_pairs={{0,4},{2,6},{4,0},{6,2},{8,12},{10,14},{12,8},{14,10},{1,5},{3,7},... | collective-permute-start | bytes 245768 | tf_op jit(solution)/shard_map/ppermute | solution.py:40
  7.5 11.2 %collective-permute-start.2 = (bf16[64,640]{1,0:T(8,128)(2,1)S(1)}, bf16[64,640]{1,0:T(8,128)(2,1)S(1)}, u32[]{:S(2)}, u32[]{:S(2)}) collective-permute-start(bf16[64,640]{1,0:T(8,128)(2,1)S(1)} %get-tuple-element.67), channel_id=1, source_target_pairs={{0,8},{2,10},{4,12},{6,14},{8,0},{10,2},{12,4},{14,6},{1,9},{3,11}... | collective-permute-start | bytes 245768 | tf_op jit(solution)/shard_map/ppermute | solution.py:40
  10.1 11.3 %collective-permute-start.3 = (bf16[64,640]{1,0:T(8,128)(2,1)S(1)}, bf16[64,640]{1,0:T(8,128)(2,1)S(1)}, u32[]{:S(2)}, u32[]{:S(2)}) collective-permute-start(bf16[64,640]{1,0:T(8,128)(2,1)S(1)} %get-tuple-element.68), channel_id=1, source_target_pairs={{0,12},{2,14},{4,8},{6,10},{8,4},{10,6},{12,0},{14,2},{1,13},{3,15... | collective-permute-start | bytes 245768 | tf_op jit(solution)/shard_map/ppermute | solution.py:40
  10.1 11.3 %collective-permute-start.4 = (bf16[64,640]{1,0:T(8,128)(2,1)S(1)}, bf16[64,640]{1,0:T(8,128)(2,1)S(1)}, u32[]{:S(2)}, u32[]{:S(2)}) collective-permute-start(bf16[64,640]{1,0:T(8,128)(2,1)S(1)} %get-tuple-element.69), channel_id=1, source_target_pairs={{0,2},{2,0},{4,6},{6,4},{8,10},{10,8},{12,14},{14,12},{1,3},{3,1},... | collective-permute-start | bytes 245768 | tf_op jit(solution)/shard_map/ppermute | solution.py:40
  11.8 9.6 %collective-permute-start.5 = (bf16[64,640]{1,0:T(8,128)(2,1)S(1)}, bf16[64,640]{1,0:T(8,128)(2,1)S(1)}, u32[]{:S(2)}, u32[]{:S(2)}) collective-permute-start(bf16[64,640]{1,0:T(8,128)(2,1)S(1)} %get-tuple-element.70), channel_id=1, source_target_pairs={{0,6},{2,4},{4,2},{6,0},{8,14},{10,12},{12,10},{14,8},{1,7},{3,5},... | collective-permute-start | bytes 245768 | tf_op jit(solution)/shard_map/ppermute | solution.py:40
  14.2 9.6 %collective-permute-start.6 = (bf16[64,640]{1,0:T(8,128)(2,1)S(1)}, bf16[64,640]{1,0:T(8,128)(2,1)S(1)}, u32[]{:S(2)}, u32[]{:S(2)}) collective-permute-start(bf16[64,640]{1,0:T(8,128)(2,1)S(1)} %get-tuple-element.71), channel_id=1, source_target_pairs={{0,10},{2,8},{4,14},{6,12},{8,2},{10,0},{12,6},{14,4},{1,11},{3,9}... | collective-permute-start | bytes 245768 | tf_op jit(solution)/shard_map/ppermute | solution.py:40
  18.7 7.2 %collective-permute-start.7 = (bf16[64,640]{1,0:T(8,128)(2,1)S(1)}, bf16[64,640]{1,0:T(8,128)(2,1)S(1)}, u32[]{:S(2)}, u32[]{:S(2)}) collective-permute-start(bf16[64,640]{1,0:T(8,128)(2,1)S(1)} %get-tuple-element.72), channel_id=1, source_target_pairs={{0,14},{2,12},{4,10},{6,8},{8,6},{10,4},{12,2},{14,0},{1,15},{3,13... | collective-permute-start | bytes 245768 | tf_op jit(solution)/shard_map/ppermute | solution.py:40
  28.3 7.6 %collective-permute-start.8 = (f16[4,40,1024]{2,1,0:T(8,128)(2,1)S(1)}, f16[4,40,1024]{2,1,0:T(8,128)(2,1)S(1)}, u32[]{:S(2)}, u32[]{:S(2)}) collective-permute-start(f16[4,40,1024]{2,1,0:T(8,128)(2,1)S(1)} %bitcast.33), channel_id=1, source_target_pairs={{0,2},{2,0},{4,6},{6,4},{8,10},{10,8},{12,14},{14,12},{1,3},{3,1},... | collective-permute-start | bytes 983048 | tf_op jit(solution)/shard_map/ppermute | solution.py:40
  36.1 14.4 %collective-permute-start.15 = (f16[4,40,1024]{2,1,0:T(8,128)(2,1)S(1)}, f16[4,40,1024]{2,1,0:T(8,128)(2,1)S(1)}, u32[]{:S(2)}, u32[]{:S(2)}) collective-permute-start(f16[4,40,1024]{2,1,0:T(8,128)(2,1)S(1)} %multiply_convert_fusion), channel_id=1, source_target_pairs={{0,2},{2,0},{4,6},{6,4},{8,10},{10,8},{12,14},{14,12},{1,3},{3,1},... | collective-permute-start | bytes 983048 | tf_op jit(solution)/shard_map/ppermute | solution.py:40
  36.3 8.1 %collective-permute-start.9 = (f16[40,1024]{1,0:T(8,128)(2,1)S(1)}, f16[40,1024]{1,0:T(8,128)(2,1)S(1)}, u32[]{:S(2)}, u32[]{:S(2)}) collective-permute-start(f16[40,1024]{1,0:T(8,128)(2,1)S(1)} %get-tuple-element.79), channel_id=1, source_target_pairs={{0,4},{2,6},{4,0},{6,2},{8,12},{10,14},{12,8},{14,10},{1,5},{3,7},... | collective-permute-start | bytes 245768 | tf_op jit(solution)/shard_map/ppermute | solution.py:40
  38.0 8.0 %collective-permute-start.10 = (f16[40,1024]{1,0:T(8,128)(2,1)S(1)}, f16[40,1024]{1,0:T(8,128)(2,1)S(1)}, u32[]{:S(2)}, u32[]{:S(2)}) collective-permute-start(f16[40,1024]{1,0:T(8,128)(2,1)S(1)} %get-tuple-element.80), channel_id=1, source_target_pairs={{0,8},{2,10},{4,12},{6,14},{8,0},{10,2},{12,4},{14,6},{1,9},{3,11}... | collective-permute-start | bytes 245768 | tf_op jit(solution)/shard_map/ppermute | solution.py:40
  39.6 6.4 %collective-permute-start.11 = (f16[40,1024]{1,0:T(8,128)(2,1)S(1)}, f16[40,1024]{1,0:T(8,128)(2,1)S(1)}, u32[]{:S(2)}, u32[]{:S(2)}) collective-permute-start(f16[40,1024]{1,0:T(8,128)(2,1)S(1)} %get-tuple-element.81), channel_id=1, source_target_pairs={{0,12},{2,14},{4,8},{6,10},{8,4},{10,6},{12,0},{14,2},{1,13},{3,15... | collective-permute-start | bytes 245768 | tf_op jit(solution)/shard_map/ppermute | solution.py:40
  46.1 7.2 %collective-permute-start.14 = (bf16[40,1024]{1,0:T(8,128)(2,1)S(1)}, bf16[40,1024]{1,0:T(8,128)(2,1)S(1)}, u32[]{:S(2)}, u32[]{:S(2)}) collective-permute-start(bf16[40,1024]{1,0:T(8,128)(2,1)S(1)} %add_convert_fusion.1), channel_id=1, source_target_pairs={{0,12},{2,14},{4,8},{6,10},{8,4},{10,6},{12,0},{14,2},{1,13},{3,15... | collective-permute-start | bytes 245768 | tf_op jit(solution)/shard_map/ppermute | solution.py:40
  48.6 11.3 %collective-permute-start.13 = (bf16[40,1024]{1,0:T(8,128)(2,1)S(1)}, bf16[40,1024]{1,0:T(8,128)(2,1)S(1)}, u32[]{:S(2)}, u32[]{:S(2)}) collective-permute-start(bf16[40,1024]{1,0:T(8,128)(2,1)S(1)} %add_convert_fusion.1), channel_id=1, source_target_pairs={{0,8},{2,10},{4,12},{6,14},{8,0},{10,2},{12,4},{14,6},{1,9},{3,11}... | collective-permute-start | bytes 245768 | tf_op jit(solution)/shard_map/ppermute | solution.py:40
  49.1 10.8 %collective-permute-start.12 = (bf16[40,1024]{1,0:T(8,128)(2,1)S(1)}, bf16[40,1024]{1,0:T(8,128)(2,1)S(1)}, u32[]{:S(2)}, u32[]{:S(2)}) collective-permute-start(bf16[40,1024]{1,0:T(8,128)(2,1)S(1)} %add_convert_fusion.1), channel_id=1, source_target_pairs={{0,4},{2,6},{4,0},{6,2},{8,12},{10,14},{12,8},{14,10},{1,5},{3,7},... | collective-permute-start | bytes 245768 | tf_op jit(solution)/shard_map/ppermute | solution.py:40
  50.7 14.5 %collective-permute-start.18 = (f16[40,1024]{1,0:T(8,128)(2,1)S(1)}, f16[40,1024]{1,0:T(8,128)(2,1)S(1)}, u32[]{:S(2)}, u32[]{:S(2)}) collective-permute-start(f16[40,1024]{1,0:T(8,128)(2,1)S(1)} %get-tuple-element.121), channel_id=1, source_target_pairs={{0,12},{2,14},{4,8},{6,10},{8,4},{10,6},{12,0},{14,2},{1,13},{3,15... | collective-permute-start | bytes 245768 | tf_op jit(solution)/shard_map/ppermute | solution.py:40
  53.3 11.9 %collective-permute-start.17 = (f16[40,1024]{1,0:T(8,128)(2,1)S(1)}, f16[40,1024]{1,0:T(8,128)(2,1)S(1)}, u32[]{:S(2)}, u32[]{:S(2)}) collective-permute-start(f16[40,1024]{1,0:T(8,128)(2,1)S(1)} %get-tuple-element.122), channel_id=1, source_target_pairs={{0,8},{2,10},{4,12},{6,14},{8,0},{10,2},{12,4},{14,6},{1,9},{3,11}... | collective-permute-start | bytes 245768 | tf_op jit(solution)/shard_map/ppermute | solution.py:40
  53.3 11.9 %collective-permute-start.16 = (f16[40,1024]{1,0:T(8,128)(2,1)S(1)}, f16[40,1024]{1,0:T(8,128)(2,1)S(1)}, u32[]{:S(2)}, u32[]{:S(2)}) collective-permute-start(f16[40,1024]{1,0:T(8,128)(2,1)S(1)} %get-tuple-element.123), channel_id=1, source_target_pairs={{0,4},{2,6},{4,0},{6,2},{8,12},{10,14},{12,8},{14,10},{1,5},{3,7},... | collective-permute-start | bytes 245768 | tf_op jit(solution)/shard_map/ppermute | solution.py:40
  60.0 7.6 %collective-permute-start.20 = (bf16[4,40,1024]{2,1,0:T(8,128)(2,1)S(1)}, bf16[4,40,1024]{2,1,0:T(8,128)(2,1)S(1)}, u32[]{:S(2)}, u32[]{:S(2)}) collective-permute-start(bf16[4,40,1024]{2,1,0:T(8,128)(2,1)S(1)} %pad_maximum_fusion.refs_0_), channel_id=1, source_target_pairs={{0,2},{2,0},{4,6},{6,4},{8,10},{10,8},{12,14},{14,12},{1,3},{3,1},... | collective-permute-start | bytes 983048 | tf_op jit(solution)/shard_map/ppermute | solution.py:40
  65.3 8.7 %collective-permute-start.19 = (bf16[40,1024]{1,0:T(8,128)(2,1)S(1)}, bf16[40,1024]{1,0:T(8,128)(2,1)S(1)}, u32[]{:S(2)}, u32[]{:S(2)}) collective-permute-start(bf16[40,1024]{1,0:T(8,128)(2,1)S(1)} %add_convert_fusion), channel_id=1, source_target_pairs={{0,2},{2,0},{4,6},{6,4},{8,10},{10,8},{12,14},{14,12},{1,3},{3,1},... | collective-permute-start | bytes 245768 | tf_op jit(solution)/shard_map/ppermute | solution.py:40
  73.9 10.8 %collective-permute-start.21 = (bf16[4,64,1152]{2,1,0:T(8,128)(2,1)S(1)}, bf16[4,64,1152]{2,1,0:T(8,128)(2,1)S(1)}, u32[]{:S(2)}, u32[]{:S(2)}) collective-permute-start(bf16[4,64,1152]{2,1,0:T(8,128)(2,1)S(1)} %attend.4), channel_id=1, source_target_pairs={{0,2},{2,0},{4,6},{6,4},{8,10},{10,8},{12,14},{14,12},{1,3},{3,1},... | collective-permute-start | bytes 1769480 | tf_op jit(solution)/shard_map/ppermute | solution.py:40
  74.0 12.2 %collective-permute-start.24 = (bf16[2,40,1024]{2,1,0:T(8,128)(2,1)S(1)}, bf16[2,40,1024]{2,1,0:T(8,128)(2,1)S(1)}, u32[]{:S(2)}, u32[]{:S(2)}) collective-permute-start(bf16[2,40,1024]{2,1,0:T(8,128)(2,1)S(1)} %pad_maximum_fusion.1.refs_0_), channel_id=1, source_target_pairs={{0,12},{2,14},{4,8},{6,10},{8,4},{10,6},{12,0},{14,2},{1,13},{3,15... | collective-permute-start | bytes 491528 | tf_op jit(solution)/shard_map/ppermute | solution.py:40
  74.1 12.1 %collective-permute-start.23 = (bf16[2,40,1024]{2,1,0:T(8,128)(2,1)S(1)}, bf16[2,40,1024]{2,1,0:T(8,128)(2,1)S(1)}, u32[]{:S(2)}, u32[]{:S(2)}) collective-permute-start(bf16[2,40,1024]{2,1,0:T(8,128)(2,1)S(1)} %pad_maximum_fusion.1.refs_0_), channel_id=1, source_target_pairs={{0,8},{2,10},{4,12},{6,14},{8,0},{10,2},{12,4},{14,6},{1,9},{3,11}... | collective-permute-start | bytes 491528 | tf_op jit(solution)/shard_map/ppermute | solution.py:40
  74.2 12.1 %collective-permute-start.22 = (bf16[2,40,1024]{2,1,0:T(8,128)(2,1)S(1)}, bf16[2,40,1024]{2,1,0:T(8,128)(2,1)S(1)}, u32[]{:S(2)}, u32[]{:S(2)}) collective-permute-start(bf16[2,40,1024]{2,1,0:T(8,128)(2,1)S(1)} %pad_maximum_fusion.1.refs_0_), channel_id=1, source_target_pairs={{0,4},{2,6},{4,0},{6,2},{8,12},{10,14},{12,8},{14,10},{1,5},{3,7},... | collective-permute-start | bytes 491528 | tf_op jit(solution)/shard_map/ppermute | solution.py:40
  92.7 12.7 %collective-permute-start.28 = (bf16[4,64,1152]{2,1,0:T(8,128)(2,1)S(1)}, bf16[4,64,1152]{2,1,0:T(8,128)(2,1)S(1)}, u32[]{:S(2)}, u32[]{:S(2)}) collective-permute-start(bf16[4,64,1152]{2,1,0:T(8,128)(2,1)S(1)} %attend.6), channel_id=1, source_target_pairs={{0,2},{2,0},{4,6},{6,4},{8,10},{10,8},{12,14},{14,12},{1,3},{3,1},... | collective-permute-start | bytes 1769480 | tf_op jit(solution)/shard_map/ppermute | solution.py:40
  92.7 14.7 %collective-permute-start.25 = (bf16[64,1152]{1,0:T(8,128)(2,1)S(1)}, bf16[64,1152]{1,0:T(8,128)(2,1)S(1)}, u32[]{:S(2)}, u32[]{:S(2)}) collective-permute-start(bf16[64,1152]{1,0:T(8,128)(2,1)S(1)} %get-tuple-element.107), channel_id=1, source_target_pairs={{0,4},{2,6},{4,0},{6,2},{8,12},{10,14},{12,8},{14,10},{1,5},{3,7},... | collective-permute-start | bytes 442376 | tf_op jit(solution)/shard_map/ppermute | solution.py:40
  92.8 19.9 %collective-permute-start.26 = (bf16[64,1152]{1,0:T(8,128)(2,1)S(1)}, bf16[64,1152]{1,0:T(8,128)(2,1)S(1)}, u32[]{:S(2)}, u32[]{:S(2)}) collective-permute-start(bf16[64,1152]{1,0:T(8,128)(2,1)S(1)} %get-tuple-element.108), channel_id=1, source_target_pairs={{0,8},{2,10},{4,12},{6,14},{8,0},{10,2},{12,4},{14,6},{1,9},{3,11}... | collective-permute-start | bytes 442376 | tf_op jit(solution)/shard_map/ppermute | solution.py:40
  92.9 19.9 %collective-permute-start.27 = (bf16[64,1152]{1,0:T(8,128)(2,1)S(1)}, bf16[64,1152]{1,0:T(8,128)(2,1)S(1)}, u32[]{:S(2)}, u32[]{:S(2)}) collective-permute-start(bf16[64,1152]{1,0:T(8,128)(2,1)S(1)} %get-tuple-element.109), channel_id=1, source_target_pairs={{0,12},{2,14},{4,8},{6,10},{8,4},{10,6},{12,0},{14,2},{1,13},{3,15... | collective-permute-start | bytes 442376 | tf_op jit(solution)/shard_map/ppermute | solution.py:40
  106.8 7.2 %collective-permute-start.29 = (bf16[64,1152]{1,0:T(8,128)(2,1)S(1)}, bf16[64,1152]{1,0:T(8,128)(2,1)S(1)}, u32[]{:S(2)}, u32[]{:S(2)}) collective-permute-start(bf16[64,1152]{1,0:T(8,128)(2,1)S(1)} %get-tuple-element.115), channel_id=1, source_target_pairs={{0,4},{2,6},{4,0},{6,2},{8,12},{10,14},{12,8},{14,10},{1,5},{3,7},... | collective-permute-start | bytes 442376 | tf_op jit(solution)/shard_map/ppermute | solution.py:40
  106.9 11.3 %collective-permute-start.30 = (bf16[64,1152]{1,0:T(8,128)(2,1)S(1)}, bf16[64,1152]{1,0:T(8,128)(2,1)S(1)}, u32[]{:S(2)}, u32[]{:S(2)}) collective-permute-start(bf16[64,1152]{1,0:T(8,128)(2,1)S(1)} %get-tuple-element.116), channel_id=1, source_target_pairs={{0,8},{2,10},{4,12},{6,14},{8,0},{10,2},{12,4},{14,6},{1,9},{3,11}... | collective-permute-start | bytes 442376 | tf_op jit(solution)/shard_map/ppermute | solution.py:40
  107.5 10.7 %collective-permute-start.31 = (bf16[64,1152]{1,0:T(8,128)(2,1)S(1)}, bf16[64,1152]{1,0:T(8,128)(2,1)S(1)}, u32[]{:S(2)}, u32[]{:S(2)}) collective-permute-start(bf16[64,1152]{1,0:T(8,128)(2,1)S(1)} %get-tuple-element.117), channel_id=1, source_target_pairs={{0,12},{2,14},{4,8},{6,10},{8,4},{10,6},{12,0},{14,2},{1,13},{3,15... | collective-permute-start | bytes 442376 | tf_op jit(solution)/shard_map/ppermute | solution.py:40

commit v5 on v4

--- a/solution.py
+++ b/solution.py
@@ -571,21 +571,22 @@
     depth = query_weight.shape[1]
     hidden = hidden_rows if depth % HD else fetch([hidden_rows])[0]
     slices = split(grid, place, hidden, handed, depth)
-    n = grid.n
-    lane = lax.broadcasted_iota(jnp.int32, (1, n), 1)
-    section, shard = after((lax.axis_index("sec"), lax.axis_index("seq")), handed)
-    meta = jnp.concatenate([
-        response_lengths, block_prompts[:, :, 0],
-        jnp.pad(prompt_lengths, (0, n - prompt_lengths.shape[0]))[None],
-        jnp.where(lane == 0, section, shard).astype(jnp.int32),
-    ])
-    weight, own = fetch([query_weight, after(response_cache, handed)])
     x = [slices[0]] + [None] * (grid.n - 1)
     for kz in reversed(range(grid.zs)):
         for kx in reversed(range(grid.xs)):
             k = kx * grid.zs + kz
             if k:
                 x[k] = grid.swap(slices[k], kx, kz)
+    early = x[1:grid.zs][:3]
+    weight, own = fetch([query_weight, after(response_cache, early)])
+    n = grid.n
+    lane = lax.broadcasted_iota(jnp.int32, (1, n), 1)
+    section, shard = after((lax.axis_index("sec"), lax.axis_index("seq")), early)
+    meta = jnp.concatenate([
+        response_lengths, block_prompts[:, :, 0],
+        jnp.pad(prompt_lengths, (0, n - prompt_lengths.shape[0]))[None],
+        jnp.where(lane == 0, section, shard).astype(jnp.int32),
+    ])
     part = project(grid, meta, x, weight, bl, share, chunks)
     part = [piece.reshape(grid.zs, share, part_cols) for piece in part]
     part = [part[c * grid.xs:(c + 1) * grid.xs] for c in range(chunks)]

time: 120 us -> 120 us (level)
  starting transfers between devices: 46.9 us -> 49.5 us
  waiting for transfers between devices: 19.2 us -> 17.3 us
  Pallas kernels: 52.2 us -> 50.9 us
    ppermute x31, starting transfers between devices: 44.5 us -> 47.1 us  [swap(): return lax.ppermute(value, 'seq', pairs)]
    ppermute x31, waiting for transfers between devices: 18.5 us -> 16.7 us  [swap(): return lax.ppermute(value, 'seq', pairs)]
  transfers between devices with their start and end apart: 32 -> 32, of which waited for: 9 -> 9; matrix products, arithmetic and copies ran while one was open for 1% -> 1% of each run, Pallas kernels for 34% -> 33%
where the time goes in v5:
time: 120 us
  Pallas kernels  50.9 us (42%)
  starting transfers between devices  49.5 us (41%)
  waiting for transfers between devices  17.3 us (14%)
  other arithmetic  1.41 us (1%)
    ppermute x31, starting transfers between devices, swap(): return lax.ppermute(value, 'seq', pairs)  47.1 us
    pallas_call x4, Pallas kernels, attend(): pl.pallas_call(functools.partial(attend_kernel, grid, kx, bl, share, head...  24.8 us
    ppermute x31, waiting for transfers between devices, swap(): return lax.ppermute(value, 'seq', pairs)  16.7 us
    pallas_call x4, Pallas kernels, fetch_cache(): pl.pallas_call(functools.partial(fetch_cache_kernel, n, chunk, width, fir...  12.6 us
    pallas_call x2, Pallas kernels, finish(): pl.pallas_call(functools.partial(finish_kernel, heads, bl, len(done)), gr...  3.26 us
    pallas_call x2, Pallas kernels, merge_column(): pl.pallas_call(functools.partial(merge_kernel, zs, heads), out_shape=[jax...  3.01 us
    pallas_call x2, Pallas kernels, fetch(): pl.pallas_call(fetch_kernel, in_specs=[anywhere] * len(arrays), out_specs...  2.86 us
  transfers between devices with their start and end apart: 32, of which 9 were waited for; matrix products, arithmetic and copies ran while one was open for 1% of the time, Pallas kernels for 33%

profile of v5, /device:TPU:0, one launch (start us, length us, event | category | flops | bytes accessed | tf_op | source)
XLA Modules:
  0.0 119.6 jit_solution(6672662276227195941)
XLA Ops:
  0.0 2.4 %collective-permute-start = (bf16[1,64,5120]{2,1,0:T(8,128)(2,1)}, bf16[1,64,5120]{2,1,0:T(8,128)(2,1)S(1)}, u32[]{:S(2)}, u32[]{:S(2)}) collective-permute-start(bf16[1,64,5120]{2,1,0:T(8,128)(2,1)} %param.9), channel_id=1, source_target_pairs={{0,16},{1,17},{2,18},{3,19},{4,20},{5,21},{6,22},{7,23},{8,24},{9,... | collective-permute-start | bytes 1966088 | tf_op jit(solution)/shard_map/ppermute | solution.py:570
  2.4 1.1 fetch.2.hidden_ref
  3.6 0.7 collective-permute-done.handed_ref
  4.3 0.7 split.1
  5.0 2.5 %collective-permute-start.1 = (bf16[64,640]{1,0:T(8,128)(2,1)S(1)}, bf16[64,640]{1,0:T(8,128)(2,1)S(1)}, u32[]{:S(2)}, u32[]{:S(2)}) collective-permute-start(bf16[64,640]{1,0:T(8,128)(2,1)S(1)} %get-tuple-element.63), channel_id=1, source_target_pairs={{0,4},{2,6},{4,0},{6,2},{8,12},{10,14},{12,8},{14,10},{1,5},{3,7},... | collective-permute-start | bytes 245768 | tf_op jit(solution)/shard_map/ppermute | solution.py:40
  7.5 2.6 %collective-permute-start.2 = (bf16[64,640]{1,0:T(8,128)(2,1)S(1)}, bf16[64,640]{1,0:T(8,128)(2,1)S(1)}, u32[]{:S(2)}, u32[]{:S(2)}) collective-permute-start(bf16[64,640]{1,0:T(8,128)(2,1)S(1)} %get-tuple-element.64), channel_id=1, source_target_pairs={{0,8},{2,10},{4,12},{6,14},{8,0},{10,2},{12,4},{14,6},{1,9},{3,11}... | collective-permute-start | bytes 245768 | tf_op jit(solution)/shard_map/ppermute | solution.py:40
  10.1 1.7 %collective-permute-start.4 = (bf16[64,640]{1,0:T(8,128)(2,1)S(1)}, bf16[64,640]{1,0:T(8,128)(2,1)S(1)}, u32[]{:S(2)}, u32[]{:S(2)}) collective-permute-start(bf16[64,640]{1,0:T(8,128)(2,1)S(1)} %get-tuple-element.69), channel_id=1, source_target_pairs={{0,2},{2,0},{4,6},{6,4},{8,10},{10,8},{12,14},{14,12},{1,3},{3,1},... | collective-permute-start | bytes 245768 | tf_op jit(solution)/shard_map/ppermute | solution.py:40
  11.8 0.6 collective-permute-start.5
  12.4 4.4 %collective-permute-start.6 = (bf16[64,640]{1,0:T(8,128)(2,1)S(1)}, bf16[64,640]{1,0:T(8,128)(2,1)S(1)}, u32[]{:S(2)}, u32[]{:S(2)}) collective-permute-start(bf16[64,640]{1,0:T(8,128)(2,1)S(1)} %get-tuple-element.71), channel_id=1, source_target_pairs={{0,10},{2,8},{4,14},{6,12},{8,2},{10,0},{12,6},{14,4},{1,11},{3,9}... | collective-permute-start | bytes 245768 | tf_op jit(solution)/shard_map/ppermute | solution.py:40
  16.8 4.1 %collective-permute-start.7 = (bf16[64,640]{1,0:T(8,128)(2,1)S(1)}, bf16[64,640]{1,0:T(8,128)(2,1)S(1)}, u32[]{:S(2)}, u32[]{:S(2)}) collective-permute-start(bf16[64,640]{1,0:T(8,128)(2,1)S(1)} %get-tuple-element.72), channel_id=1, source_target_pairs={{0,14},{2,12},{4,10},{6,8},{8,6},{10,4},{12,2},{14,0},{1,15},{3,13... | collective-permute-start | bytes 245768 | tf_op jit(solution)/shard_map/ppermute | solution.py:40
  20.9 1.8 %fetch.3 = (bf16[1,640,2048]{2,1,0:T(8,128)(2,1)S(1)}, bf16[1,64,1024]{2,1,0:T(8,128)(2,1)S(1)}) custom-call(bf16[1,640,2048]{2,1,0:T(8,128)(2,1)} %refs_0_.3, bf16[1,64,1024]{2,1,0:T(8,128)(2,1)} %refs_1_), custom_call_target="tpu_custom_call" | custom-call | bytes 2752512 | tf_op jit(solution)/shard_map/fetch/pallas_call | solution.py:115
  22.7 0.7 pad_add_fusion.meta
  23.5 1.4 %collective-permute-done.6.refs_6_ = bf16[64,640]{1,0:T(8,128)(2,1)S(1)} collective-permute-done((bf16[64,640]{1,0:T(8,128)(2,1)S(1)}, bf16[64,640]{1,0:T(8,128)(2,1)S(1)}, u32[]{:S(2)}, u32[]{:S(2)}) %collective-permute-start.6) | collective-permute-done | bytes 81952 | tf_op jit(solution)/shard_map/ppermute | solution.py:40
  24.9 2.3 %project.1 = (f32[160,1024]{1,0:T(8,128)S(1)}, f32[160,1024]{1,0:T(8,128)S(1)}, f32[160,1024]{1,0:T(8,128)S(1)}, f32[160,1024]{1,0:T(8,128)S(1)}) custom-call(s32[6,8]{1,0:T(8,128)S(1)} %pad_add_fusion.meta, bf16[64,640]{1,0:T(8,128)(2,1)S(1)} %get-tuple-element.68.refs_0_, bf16[64,640]{1,0:T(8,128)(2,1)S(1)} %collective-permute-done.1.refs_1_, ...), custom_call_target="tpu_custom_call" | custom-call | flops 838860800 | bytes 5242880 | tf_op jit(solution)/shard_map/project/pallas_call | solution.py:212
  27.2 0.6 collective-permute-start.8
  27.8 3.1 %fetch_cache.5.refs_3_ = bf16[8,2048,256]{2,1,0:T(8,128)(2,1)S(1)} custom-call(s32[6,8]{1,0:T(8,128)S(1)} %pad_add_fusion.meta, bf16[1,8,2048,1024]{3,2,1,0:T(8,128)(2,1)} %cache_ref.7), custom_call_target="tpu_custom_call" | custom-call | bytes 8388608 | tf_op jit(solution)/shard_map/fetch_cache/pallas_call | solution.py:150
  31.0 3.1 %fetch_cache.4.refs_2_ = bf16[8,2048,256]{2,1,0:T(8,128)(2,1)S(1)} custom-call(s32[6,8]{1,0:T(8,128)S(1)} %pad_add_fusion.meta, bf16[1,8,2048,1024]{3,2,1,0:T(8,128)(2,1)} %cache_ref.7), custom_call_target="tpu_custom_call" | custom-call | bytes 8388608 | tf_op jit(solution)/shard_map/fetch_cache/pallas_call | solution.py:150
  34.1 0.8 collective-permute-done.8
  35.8 3.2 %collective-permute-start.9 = (f16[40,1024]{1,0:T(8,128)(2,1)S(1)}, f16[40,1024]{1,0:T(8,128)(2,1)S(1)}, u32[]{:S(2)}, u32[]{:S(2)}) collective-permute-start(f16[40,1024]{1,0:T(8,128)(2,1)S(1)} %get-tuple-element.79), channel_id=1, source_target_pairs={{0,4},{2,6},{4,0},{6,2},{8,12},{10,14},{12,8},{14,10},{1,5},{3,7},... | collective-permute-start | bytes 245768 | tf_op jit(solution)/shard_map/ppermute | solution.py:40
  39.0 1.7 %collective-permute-start.10 = (f16[40,1024]{1,0:T(8,128)(2,1)S(1)}, f16[40,1024]{1,0:T(8,128)(2,1)S(1)}, u32[]{:S(2)}, u32[]{:S(2)}) collective-permute-start(f16[40,1024]{1,0:T(8,128)(2,1)S(1)} %get-tuple-element.80), channel_id=1, source_target_pairs={{0,8},{2,10},{4,12},{6,14},{8,0},{10,2},{12,4},{14,6},{1,9},{3,11}... | collective-permute-start | bytes 245768 | tf_op jit(solution)/shard_map/ppermute | solution.py:40
  40.7 0.6 collective-permute-start.11
  41.3 3.1 %fetch_cache.6.refs_4_ = bf16[8,2048,256]{2,1,0:T(8,128)(2,1)S(1)} custom-call(s32[6,8]{1,0:T(8,128)S(1)} %pad_add_fusion.meta, bf16[1,8,2048,1024]{3,2,1,0:T(8,128)(2,1)} %cache_ref.7), custom_call_target="tpu_custom_call" | custom-call | bytes 8388608 | tf_op jit(solution)/shard_map/fetch_cache/pallas_call | solution.py:150
  44.5 1.0 collective-permute-done.10
  45.5 1.5 %collective-permute-done.11 = f16[40,1024]{1,0:T(8,128)(2,1)S(1)} collective-permute-done((f16[40,1024]{1,0:T(8,128)(2,1)S(1)}, f16[40,1024]{1,0:T(8,128)(2,1)S(1)}, u32[]{:S(2)}, u32[]{:S(2)}) %collective-permute-start.11) | collective-permute-done | bytes 81952 | tf_op jit(solution)/shard_map/ppermute | solution.py:40
  47.1 0.9 collective-permute-start.14
  48.0 1.4 %collective-permute-start.13 = (bf16[40,1024]{1,0:T(8,128)(2,1)S(1)}, bf16[40,1024]{1,0:T(8,128)(2,1)S(1)}, u32[]{:S(2)}, u32[]{:S(2)}) collective-permute-start(bf16[40,1024]{1,0:T(8,128)(2,1)S(1)} %add_convert_fusion.1), channel_id=1, source_target_pairs={{0,8},{2,10},{4,12},{6,14},{8,0},{10,2},{12,4},{14,6},{1,9},{3,11}... | collective-permute-start | bytes 245768 | tf_op jit(solution)/shard_map/ppermute | solution.py:40
  49.4 2.1 %collective-permute-start.12 = (bf16[40,1024]{1,0:T(8,128)(2,1)S(1)}, bf16[40,1024]{1,0:T(8,128)(2,1)S(1)}, u32[]{:S(2)}, u32[]{:S(2)}) collective-permute-start(bf16[40,1024]{1,0:T(8,128)(2,1)S(1)} %add_convert_fusion.1), channel_id=1, source_target_pairs={{0,4},{2,6},{4,0},{6,2},{8,12},{10,14},{12,8},{14,10},{1,5},{3,7},... | collective-permute-start | bytes 245768 | tf_op jit(solution)/shard_map/ppermute | solution.py:40
  51.7 0.9 collective-permute-start.18
  53.2 1.0 collective-permute-done.14
  54.3 2.5 %collective-permute-start.16 = (f16[40,1024]{1,0:T(8,128)(2,1)S(1)}, f16[40,1024]{1,0:T(8,128)(2,1)S(1)}, u32[]{:S(2)}, u32[]{:S(2)}) collective-permute-start(f16[40,1024]{1,0:T(8,128)(2,1)S(1)} %get-tuple-element.123), channel_id=1, source_target_pairs={{0,4},{2,6},{4,0},{6,2},{8,12},{10,14},{12,8},{14,10},{1,5},{3,7},... | collective-permute-start | bytes 245768 | tf_op jit(solution)/shard_map/ppermute | solution.py:40
  56.8 2.9 %collective-permute-done.13 = bf16[40,1024]{1,0:T(8,128)(2,1)S(1)} collective-permute-done((bf16[40,1024]{1,0:T(8,128)(2,1)S(1)}, bf16[40,1024]{1,0:T(8,128)(2,1)S(1)}, u32[]{:S(2)}, u32[]{:S(2)}) %collective-permute-start.13) | collective-permute-done | bytes 81952 | tf_op jit(solution)/shard_map/ppermute | solution.py:40
  59.7 1.5 %collective-permute-start.20 = (bf16[4,40,1024]{2,1,0:T(8,128)(2,1)S(1)}, bf16[4,40,1024]{2,1,0:T(8,128)(2,1)S(1)}, u32[]{:S(2)}, u32[]{:S(2)}) collective-permute-start(bf16[4,40,1024]{2,1,0:T(8,128)(2,1)S(1)} %pad_maximum_fusion.refs_0_), channel_id=1, source_target_pairs={{0,2},{2,0},{4,6},{6,4},{8,10},{10,8},{12,14},{14,12},{1,3},{3,1},... | collective-permute-start | bytes 983048 | tf_op jit(solution)/shard_map/ppermute | solution.py:40
  61.3 3.1 %fetch_cache.7.refs_5_ = bf16[8,2048,256]{2,1,0:T(8,128)(2,1)S(1)} custom-call(s32[6,8]{1,0:T(8,128)S(1)} %pad_add_fusion.meta, bf16[1,8,2048,1024]{3,2,1,0:T(8,128)(2,1)} %cache_ref.7), custom_call_target="tpu_custom_call" | custom-call | bytes 8388608 | tf_op jit(solution)/shard_map/fetch_cache/pallas_call | solution.py:150
  65.0 1.9 %collective-permute-done.20.refs_1_ = bf16[4,40,1024]{2,1,0:T(8,128)(2,1)S(1)} collective-permute-done((bf16[4,40,1024]{2,1,0:T(8,128)(2,1)S(1)}, bf16[4,40,1024]{2,1,0:T(8,128)(2,1)S(1)}, u32[]{:S(2)}, u32[]{:S(2)}) %collective-permute-start.20) | collective-permute-done | bytes 327712 | tf_op jit(solution)/shard_map/ppermute | solution.py:40
  66.9 6.3 %attend.4 = bf16[4,64,1152]{2,1,0:T(8,128)(2,1)S(1)} custom-call(s32[6,8]{1,0:T(8,128)S(1)} %pad_add_fusion.meta, bf16[4,40,1024]{2,1,0:T(8,128)(2,1)S(1)} %pad_maximum_fusion.refs_0_, bf16[4,40,1024]{2,1,0:T(8,128)(2,1)S(1)} %collective-permute-done.20.refs_1_, bf16[8,2048,256]{2,1,0:T(8,128)(2,1)S(1)} %fetch_cache.4.refs_2_, ...), custom_call_target="tpu_custom_call" | custom-call | flops 4294967296 | bytes 8388608 | tf_op jit(solution)/shard_map/attend/pallas_call | solution.py:486
  74.0 4.3 %collective-permute-start.22 = (bf16[2,40,1024]{2,1,0:T(8,128)(2,1)S(1)}, bf16[2,40,1024]{2,1,0:T(8,128)(2,1)S(1)}, u32[]{:S(2)}, u32[]{:S(2)}) collective-permute-start(bf16[2,40,1024]{2,1,0:T(8,128)(2,1)S(1)} %pad_maximum_fusion.1.refs_0_), channel_id=1, source_target_pairs={{0,4},{2,6},{4,0},{6,2},{8,12},{10,14},{12,8},{14,10},{1,5},{3,7},... | collective-permute-start | bytes 491528 | tf_op jit(solution)/shard_map/ppermute | solution.py:40
  78.3 5.9 %attend.5 = (bf16[4,64,1152]{2,1,0:T(8,128)(2,1)S(1)}, bf16[64,1024]{1,0:T(8,128)(2,1)S(1)}) custom-call(s32[6,8]{1,0:T(8,128)S(1)} %pad_add_fusion.meta, bf16[4,40,1024]{2,1,0:T(8,128)(2,1)S(1)} %pad_maximum_fusion.refs_0_, bf16[4,40,1024]{2,1,0:T(8,128)(2,1)S(1)} %collective-permute-done.20.refs_1_, bf16[8,2048,256]{2,1,0:T(8,128)(2,1)S(1)} %fetch_cache.4.refs_2_, ...), custom_call_target="tpu_custom_call" | custom-call | flops 4294967296 | bytes 8388608 | tf_op jit(solution)/shard_map/attend/pallas_call | solution.py:486
  84.2 1.5 %merge.2 = (bf16[64,1152]{1,0:T(8,128)(2,1)S(1)}, bf16[64,1152]{1,0:T(8,128)(2,1)S(1)}, bf16[64,1152]{1,0:T(8,128)(2,1)S(1)}, bf16[64,1152]{1,0:T(8,128)(2,1)S(1)}) custom-call(bf16[4,64,1152]{2,1,0:T(8,128)(2,1)S(1)} %get-tuple-element.96.refs_0_, bf16[4,64,1152]{2,1,0:T(8,128)(2,1)S(1)} %collective-permute-done.21.refs_1_), custom_call_target="tpu_custom_call" | custom-call | tf_op jit(solution)/shard_map/merge/pallas_call | solution.py:283
  85.8 6.4 %attend.6 = bf16[4,64,1152]{2,1,0:T(8,128)(2,1)S(1)} custom-call(s32[6,8]{1,0:T(8,128)S(1)} %pad_add_fusion.meta, bf16[2,40,1024]{2,1,0:T(8,128)(2,1)S(1)} %pad_maximum_fusion.1.refs_0_, bf16[2,40,1024]{2,1,0:T(8,128)(2,1)S(1)} %collective-permute-done.22.refs_1_, bf16[2,40,1024]{2,1,0:T(8,128)(2,1)S(1)} %collective-permute-done.23.refs_2_, ...), custom_call_target="tpu_custom_call" | custom-call | flops 4294967296 | bytes 8388608 | tf_op jit(solution)/shard_map/attend/pallas_call | solution.py:486
  92.4 4.3 %collective-permute-start.27 = (bf16[64,1152]{1,0:T(8,128)(2,1)S(1)}, bf16[64,1152]{1,0:T(8,128)(2,1)S(1)}, u32[]{:S(2)}, u32[]{:S(2)}) collective-permute-start(bf16[64,1152]{1,0:T(8,128)(2,1)S(1)} %get-tuple-element.109), channel_id=1, source_target_pairs={{0,12},{2,14},{4,8},{6,10},{8,4},{10,6},{12,0},{14,2},{1,13},{3,15... | collective-permute-start | bytes 442376 | tf_op jit(solution)/shard_map/ppermute | solution.py:40
  96.7 6.2 %attend.7 = (bf16[4,64,1152]{2,1,0:T(8,128)(2,1)S(1)}, bf16[64,1024]{1,0:T(8,128)(2,1)S(1)}) custom-call(s32[6,8]{1,0:T(8,128)S(1)} %pad_add_fusion.meta, bf16[2,40,1024]{2,1,0:T(8,128)(2,1)S(1)} %pad_maximum_fusion.1.refs_0_, bf16[2,40,1024]{2,1,0:T(8,128)(2,1)S(1)} %collective-permute-done.22.refs_1_, ...), custom_call_target="tpu_custom_call" | custom-call | flops 4294967296 | bytes 8388608 | tf_op jit(solution)/shard_map/attend/pallas_call | solution.py:486
  102.9 1.5 %merge.3 = (bf16[64,1152]{1,0:T(8,128)(2,1)S(1)}, bf16[64,1152]{1,0:T(8,128)(2,1)S(1)}, bf16[64,1152]{1,0:T(8,128)(2,1)S(1)}, bf16[64,1152]{1,0:T(8,128)(2,1)S(1)}) custom-call(bf16[4,64,1152]{2,1,0:T(8,128)(2,1)S(1)} %get-tuple-element.113.refs_0_, bf16[4,64,1152]{2,1,0:T(8,128)(2,1)S(1)} %collective-permute-done.28.refs_1_), custom_call_target="tpu_custom_call" | custom-call | tf_op jit(solution)/shard_map/merge/pallas_call | solution.py:283
  104.8 4.0 %collective-permute-start.31 = (bf16[64,1152]{1,0:T(8,128)(2,1)S(1)}, bf16[64,1152]{1,0:T(8,128)(2,1)S(1)}, u32[]{:S(2)}, u32[]{:S(2)}) collective-permute-start(bf16[64,1152]{1,0:T(8,128)(2,1)S(1)} %get-tuple-element.117), channel_id=1, source_target_pairs={{0,12},{2,14},{4,8},{6,10},{8,4},{10,6},{12,0},{14,2},{1,13},{3,15... | collective-permute-start | bytes 442376 | tf_op jit(solution)/shard_map/ppermute | solution.py:40
  108.8 0.7 attend_own.2.refs_4_
  109.6 0.7 attend_own.3.refs_5_
  110.3 1.3 %finish.2.refs_0_ = bf16[1,64,1024]{2,1,0:T(8,128)(2,1)S(1)} custom-call(s32[6,8]{1,0:T(8,128)S(1)} %pad_add_fusion.meta, bf16[64,1152]{1,0:T(8,128)(2,1)S(1)} %get-tuple-element.106.refs_0_, bf16[64,1152]{1,0:T(8,128)(2,1)S(1)} %collective-permute-done.25.refs_1_, bf16[64,1152]{1,0:T(8,128)(2,1)S(1)} %collective-permute-done.26.refs_2_, ...), custom_call_target="tpu_custom_call" | custom-call | tf_op jit(solution)/shard_map/finish/pallas_call | solution.py:531
  111.6 6.0 %collective-permute-done.30.refs_3_ = bf16[64,1152]{1,0:T(8,128)(2,1)S(1)} collective-permute-done((bf16[64,1152]{1,0:T(8,128)(2,1)S(1)}, bf16[64,1152]{1,0:T(8,128)(2,1)S(1)}, u32[]{:S(2)}, u32[]{:S(2)}) %collective-permute-start.30) | collective-permute-done | bytes 147488 | tf_op jit(solution)/shard_map/ppermute | solution.py:40
  117.6 2.0 %finish.3 = bf16[1,64,2048]{2,1,0:T(8,128)(2,1)} custom-call(s32[6,8]{1,0:T(8,128)S(1)} %pad_add_fusion.meta, bf16[1,64,1024]{2,1,0:T(8,128)(2,1)S(1)} %finish.2.refs_0_, bf16[64,1152]{1,0:T(8,128)(2,1)S(1)} %get-tuple-element.114.refs_1_, bf16[64,1152]{1,0:T(8,128)(2,1)S(1)} %collective-permute-done.29.refs_2_, ...), custom_call_target="tpu_custom_call" | custom-call | tf_op jit(solution)/shard_map/finish/pallas_call | solution.py:531
  (48 shorter events, 3.8 us)
Async XLA Ops:
  0.0 4.3 %collective-permute-start = (bf16[1,64,5120]{2,1,0:T(8,128)(2,1)}, bf16[1,64,5120]{2,1,0:T(8,128)(2,1)S(1)}, u32[]{:S(2)}, u32[]{:S(2)}) collective-permute-start(bf16[1,64,5120]{2,1,0:T(8,128)(2,1)} %param.9), channel_id=1, source_target_pairs={{0,16},{1,17},{2,18},{3,19},{4,20},{5,21},{6,22},{7,23},{8,24},{9,... | collective-permute-start | bytes 1966088 | tf_op jit(solution)/shard_map/ppermute | solution.py:570
  5.0 7.4 %collective-permute-start.1 = (bf16[64,640]{1,0:T(8,128)(2,1)S(1)}, bf16[64,640]{1,0:T(8,128)(2,1)S(1)}, u32[]{:S(2)}, u32[]{:S(2)}) collective-permute-start(bf16[64,640]{1,0:T(8,128)(2,1)S(1)} %get-tuple-element.63), channel_id=1, source_target_pairs={{0,4},{2,6},{4,0},{6,2},{8,12},{10,14},{12,8},{14,10},{1,5},{3,7},... | collective-permute-start | bytes 245768 | tf_op jit(solution)/shard_map/ppermute | solution.py:40
  7.5 9.4 %collective-permute-start.2 = (bf16[64,640]{1,0:T(8,128)(2,1)S(1)}, bf16[64,640]{1,0:T(8,128)(2,1)S(1)}, u32[]{:S(2)}, u32[]{:S(2)}) collective-permute-start(bf16[64,640]{1,0:T(8,128)(2,1)S(1)} %get-tuple-element.64), channel_id=1, source_target_pairs={{0,8},{2,10},{4,12},{6,14},{8,0},{10,2},{12,4},{14,6},{1,9},{3,11}... | collective-permute-start | bytes 245768 | tf_op jit(solution)/shard_map/ppermute | solution.py:40
  10.1 10.9 %collective-permute-start.3 = (bf16[64,640]{1,0:T(8,128)(2,1)S(1)}, bf16[64,640]{1,0:T(8,128)(2,1)S(1)}, u32[]{:S(2)}, u32[]{:S(2)}) collective-permute-start(bf16[64,640]{1,0:T(8,128)(2,1)S(1)} %get-tuple-element.65), channel_id=1, source_target_pairs={{0,12},{2,14},{4,8},{6,10},{8,4},{10,6},{12,0},{14,2},{1,13},{3,15... | collective-permute-start | bytes 245768 | tf_op jit(solution)/shard_map/ppermute | solution.py:40
  10.1 13.4 %collective-permute-start.4 = (bf16[64,640]{1,0:T(8,128)(2,1)S(1)}, bf16[64,640]{1,0:T(8,128)(2,1)S(1)}, u32[]{:S(2)}, u32[]{:S(2)}) collective-permute-start(bf16[64,640]{1,0:T(8,128)(2,1)S(1)} %get-tuple-element.69), channel_id=1, source_target_pairs={{0,2},{2,0},{4,6},{6,4},{8,10},{10,8},{12,14},{14,12},{1,3},{3,1},... | collective-permute-start | bytes 245768 | tf_op jit(solution)/shard_map/ppermute | solution.py:40
  11.8 11.7 %collective-permute-start.5 = (bf16[64,640]{1,0:T(8,128)(2,1)S(1)}, bf16[64,640]{1,0:T(8,128)(2,1)S(1)}, u32[]{:S(2)}, u32[]{:S(2)}) collective-permute-start(bf16[64,640]{1,0:T(8,128)(2,1)S(1)} %get-tuple-element.70), channel_id=1, source_target_pairs={{0,6},{2,4},{4,2},{6,0},{8,14},{10,12},{12,10},{14,8},{1,7},{3,5},... | collective-permute-start | bytes 245768 | tf_op jit(solution)/shard_map/ppermute | solution.py:40
  12.4 12.4 %collective-permute-start.6 = (bf16[64,640]{1,0:T(8,128)(2,1)S(1)}, bf16[64,640]{1,0:T(8,128)(2,1)S(1)}, u32[]{:S(2)}, u32[]{:S(2)}) collective-permute-start(bf16[64,640]{1,0:T(8,128)(2,1)S(1)} %get-tuple-element.71), channel_id=1, source_target_pairs={{0,10},{2,8},{4,14},{6,12},{8,2},{10,0},{12,6},{14,4},{1,11},{3,9}... | collective-permute-start | bytes 245768 | tf_op jit(solution)/shard_map/ppermute | solution.py:40
  16.8 8.0 %collective-permute-start.7 = (bf16[64,640]{1,0:T(8,128)(2,1)S(1)}, bf16[64,640]{1,0:T(8,128)(2,1)S(1)}, u32[]{:S(2)}, u32[]{:S(2)}) collective-permute-start(bf16[64,640]{1,0:T(8,128)(2,1)S(1)} %get-tuple-element.72), channel_id=1, source_target_pairs={{0,14},{2,12},{4,10},{6,8},{8,6},{10,4},{12,2},{14,0},{1,15},{3,13... | collective-permute-start | bytes 245768 | tf_op jit(solution)/shard_map/ppermute | solution.py:40
  27.2 7.7 %collective-permute-start.8 = (f16[4,40,1024]{2,1,0:T(8,128)(2,1)S(1)}, f16[4,40,1024]{2,1,0:T(8,128)(2,1)S(1)}, u32[]{:S(2)}, u32[]{:S(2)}) collective-permute-start(f16[4,40,1024]{2,1,0:T(8,128)(2,1)S(1)} %bitcast.33), channel_id=1, source_target_pairs={{0,2},{2,0},{4,6},{6,4},{8,10},{10,8},{12,14},{14,12},{1,3},{3,1},... | collective-permute-start | bytes 983048 | tf_op jit(solution)/shard_map/ppermute | solution.py:40
  35.2 16.4 %collective-permute-start.15 = (f16[4,40,1024]{2,1,0:T(8,128)(2,1)S(1)}, f16[4,40,1024]{2,1,0:T(8,128)(2,1)S(1)}, u32[]{:S(2)}, u32[]{:S(2)}) collective-permute-start(f16[4,40,1024]{2,1,0:T(8,128)(2,1)S(1)} %multiply_convert_fusion), channel_id=1, source_target_pairs={{0,2},{2,0},{4,6},{6,4},{8,10},{10,8},{12,14},{14,12},{1,3},{3,1},... | collective-permute-start | bytes 983048 | tf_op jit(solution)/shard_map/ppermute | solution.py:40
  35.8 8.7 %collective-permute-start.9 = (f16[40,1024]{1,0:T(8,128)(2,1)S(1)}, f16[40,1024]{1,0:T(8,128)(2,1)S(1)}, u32[]{:S(2)}, u32[]{:S(2)}) collective-permute-start(f16[40,1024]{1,0:T(8,128)(2,1)S(1)} %get-tuple-element.79), channel_id=1, source_target_pairs={{0,4},{2,6},{4,0},{6,2},{8,12},{10,14},{12,8},{14,10},{1,5},{3,7},... | collective-permute-start | bytes 245768 | tf_op jit(solution)/shard_map/ppermute | solution.py:40
  39.0 6.6 %collective-permute-start.10 = (f16[40,1024]{1,0:T(8,128)(2,1)S(1)}, f16[40,1024]{1,0:T(8,128)(2,1)S(1)}, u32[]{:S(2)}, u32[]{:S(2)}) collective-permute-start(f16[40,1024]{1,0:T(8,128)(2,1)S(1)} %get-tuple-element.80), channel_id=1, source_target_pairs={{0,8},{2,10},{4,12},{6,14},{8,0},{10,2},{12,4},{14,6},{1,9},{3,11}... | collective-permute-start | bytes 245768 | tf_op jit(solution)/shard_map/ppermute | solution.py:40
  40.7 6.3 %collective-permute-start.11 = (f16[40,1024]{1,0:T(8,128)(2,1)S(1)}, f16[40,1024]{1,0:T(8,128)(2,1)S(1)}, u32[]{:S(2)}, u32[]{:S(2)}) collective-permute-start(f16[40,1024]{1,0:T(8,128)(2,1)S(1)} %get-tuple-element.81), channel_id=1, source_target_pairs={{0,12},{2,14},{4,8},{6,10},{8,4},{10,6},{12,0},{14,2},{1,13},{3,15... | collective-permute-start | bytes 245768 | tf_op jit(solution)/shard_map/ppermute | solution.py:40
  47.1 7.2 %collective-permute-start.14 = (bf16[40,1024]{1,0:T(8,128)(2,1)S(1)}, bf16[40,1024]{1,0:T(8,128)(2,1)S(1)}, u32[]{:S(2)}, u32[]{:S(2)}) collective-permute-start(bf16[40,1024]{1,0:T(8,128)(2,1)S(1)} %add_convert_fusion.1), channel_id=1, source_target_pairs={{0,12},{2,14},{4,8},{6,10},{8,4},{10,6},{12,0},{14,2},{1,13},{3,15... | collective-permute-start | bytes 245768 | tf_op jit(solution)/shard_map/ppermute | solution.py:40
  48.0 11.7 %collective-permute-start.13 = (bf16[40,1024]{1,0:T(8,128)(2,1)S(1)}, bf16[40,1024]{1,0:T(8,128)(2,1)S(1)}, u32[]{:S(2)}, u32[]{:S(2)}) collective-permute-start(bf16[40,1024]{1,0:T(8,128)(2,1)S(1)} %add_convert_fusion.1), channel_id=1, source_target_pairs={{0,8},{2,10},{4,12},{6,14},{8,0},{10,2},{12,4},{14,6},{1,9},{3,11}... | collective-permute-start | bytes 245768 | tf_op jit(solution)/shard_map/ppermute | solution.py:40
  49.4 10.3 %collective-permute-start.12 = (bf16[40,1024]{1,0:T(8,128)(2,1)S(1)}, bf16[40,1024]{1,0:T(8,128)(2,1)S(1)}, u32[]{:S(2)}, u32[]{:S(2)}) collective-permute-start(bf16[40,1024]{1,0:T(8,128)(2,1)S(1)} %add_convert_fusion.1), channel_id=1, source_target_pairs={{0,4},{2,6},{4,0},{6,2},{8,12},{10,14},{12,8},{14,10},{1,5},{3,7},... | collective-permute-start | bytes 245768 | tf_op jit(solution)/shard_map/ppermute | solution.py:40
  51.7 12.7 %collective-permute-start.18 = (f16[40,1024]{1,0:T(8,128)(2,1)S(1)}, f16[40,1024]{1,0:T(8,128)(2,1)S(1)}, u32[]{:S(2)}, u32[]{:S(2)}) collective-permute-start(f16[40,1024]{1,0:T(8,128)(2,1)S(1)} %get-tuple-element.121), channel_id=1, source_target_pairs={{0,12},{2,14},{4,8},{6,10},{8,4},{10,6},{12,0},{14,2},{1,13},{3,15... | collective-permute-start | bytes 245768 | tf_op jit(solution)/shard_map/ppermute | solution.py:40
  52.7 11.8 %collective-permute-start.17 = (f16[40,1024]{1,0:T(8,128)(2,1)S(1)}, f16[40,1024]{1,0:T(8,128)(2,1)S(1)}, u32[]{:S(2)}, u32[]{:S(2)}) collective-permute-start(f16[40,1024]{1,0:T(8,128)(2,1)S(1)} %get-tuple-element.122), channel_id=1, source_target_pairs={{0,8},{2,10},{4,12},{6,14},{8,0},{10,2},{12,4},{14,6},{1,9},{3,11}... | collective-permute-start | bytes 245768 | tf_op jit(solution)/shard_map/ppermute | solution.py:40
  54.3 10.2 %collective-permute-start.16 = (f16[40,1024]{1,0:T(8,128)(2,1)S(1)}, f16[40,1024]{1,0:T(8,128)(2,1)S(1)}, u32[]{:S(2)}, u32[]{:S(2)}) collective-permute-start(f16[40,1024]{1,0:T(8,128)(2,1)S(1)} %get-tuple-element.123), channel_id=1, source_target_pairs={{0,4},{2,6},{4,0},{6,2},{8,12},{10,14},{12,8},{14,10},{1,5},{3,7},... | collective-permute-start | bytes 245768 | tf_op jit(solution)/shard_map/ppermute | solution.py:40
  59.7 7.1 %collective-permute-start.20 = (bf16[4,40,1024]{2,1,0:T(8,128)(2,1)S(1)}, bf16[4,40,1024]{2,1,0:T(8,128)(2,1)S(1)}, u32[]{:S(2)}, u32[]{:S(2)}) collective-permute-start(bf16[4,40,1024]{2,1,0:T(8,128)(2,1)S(1)} %pad_maximum_fusion.refs_0_), channel_id=1, source_target_pairs={{0,2},{2,0},{4,6},{6,4},{8,10},{10,8},{12,14},{14,12},{1,3},{3,1},... | collective-permute-start | bytes 983048 | tf_op jit(solution)/shard_map/ppermute | solution.py:40
  64.6 9.3 %collective-permute-start.19 = (bf16[40,1024]{1,0:T(8,128)(2,1)S(1)}, bf16[40,1024]{1,0:T(8,128)(2,1)S(1)}, u32[]{:S(2)}, u32[]{:S(2)}) collective-permute-start(bf16[40,1024]{1,0:T(8,128)(2,1)S(1)} %add_convert_fusion), channel_id=1, source_target_pairs={{0,2},{2,0},{4,6},{6,4},{8,10},{10,8},{12,14},{14,12},{1,3},{3,1},... | collective-permute-start | bytes 245768 | tf_op jit(solution)/shard_map/ppermute | solution.py:40
  73.2 11.0 %collective-permute-start.21 = (bf16[4,64,1152]{2,1,0:T(8,128)(2,1)S(1)}, bf16[4,64,1152]{2,1,0:T(8,128)(2,1)S(1)}, u32[]{:S(2)}, u32[]{:S(2)}) collective-permute-start(bf16[4,64,1152]{2,1,0:T(8,128)(2,1)S(1)} %attend.4), channel_id=1, source_target_pairs={{0,2},{2,0},{4,6},{6,4},{8,10},{10,8},{12,14},{14,12},{1,3},{3,1},... | collective-permute-start | bytes 1769480 | tf_op jit(solution)/shard_map/ppermute | solution.py:40
  73.8 11.9 %collective-permute-start.24 = (bf16[2,40,1024]{2,1,0:T(8,128)(2,1)S(1)}, bf16[2,40,1024]{2,1,0:T(8,128)(2,1)S(1)}, u32[]{:S(2)}, u32[]{:S(2)}) collective-permute-start(bf16[2,40,1024]{2,1,0:T(8,128)(2,1)S(1)} %pad_maximum_fusion.1.refs_0_), channel_id=1, source_target_pairs={{0,12},{2,14},{4,8},{6,10},{8,4},{10,6},{12,0},{14,2},{1,13},{3,15... | collective-permute-start | bytes 491528 | tf_op jit(solution)/shard_map/ppermute | solution.py:40
  73.9 11.8 %collective-permute-start.23 = (bf16[2,40,1024]{2,1,0:T(8,128)(2,1)S(1)}, bf16[2,40,1024]{2,1,0:T(8,128)(2,1)S(1)}, u32[]{:S(2)}, u32[]{:S(2)}) collective-permute-start(bf16[2,40,1024]{2,1,0:T(8,128)(2,1)S(1)} %pad_maximum_fusion.1.refs_0_), channel_id=1, source_target_pairs={{0,8},{2,10},{4,12},{6,14},{8,0},{10,2},{12,4},{14,6},{1,9},{3,11}... | collective-permute-start | bytes 491528 | tf_op jit(solution)/shard_map/ppermute | solution.py:40
  74.0 11.8 %collective-permute-start.22 = (bf16[2,40,1024]{2,1,0:T(8,128)(2,1)S(1)}, bf16[2,40,1024]{2,1,0:T(8,128)(2,1)S(1)}, u32[]{:S(2)}, u32[]{:S(2)}) collective-permute-start(bf16[2,40,1024]{2,1,0:T(8,128)(2,1)S(1)} %pad_maximum_fusion.1.refs_0_), channel_id=1, source_target_pairs={{0,4},{2,6},{4,0},{6,2},{8,12},{10,14},{12,8},{14,10},{1,5},{3,7},... | collective-permute-start | bytes 491528 | tf_op jit(solution)/shard_map/ppermute | solution.py:40
  92.1 10.7 %collective-permute-start.28 = (bf16[4,64,1152]{2,1,0:T(8,128)(2,1)S(1)}, bf16[4,64,1152]{2,1,0:T(8,128)(2,1)S(1)}, u32[]{:S(2)}, u32[]{:S(2)}) collective-permute-start(bf16[4,64,1152]{2,1,0:T(8,128)(2,1)S(1)} %attend.6), channel_id=1, source_target_pairs={{0,2},{2,0},{4,6},{6,4},{8,10},{10,8},{12,14},{14,12},{1,3},{3,1},... | collective-permute-start | bytes 1769480 | tf_op jit(solution)/shard_map/ppermute | solution.py:40
  92.2 12.6 %collective-permute-start.25 = (bf16[64,1152]{1,0:T(8,128)(2,1)S(1)}, bf16[64,1152]{1,0:T(8,128)(2,1)S(1)}, u32[]{:S(2)}, u32[]{:S(2)}) collective-permute-start(bf16[64,1152]{1,0:T(8,128)(2,1)S(1)} %get-tuple-element.107), channel_id=1, source_target_pairs={{0,4},{2,6},{4,0},{6,2},{8,12},{10,14},{12,8},{14,10},{1,5},{3,7},... | collective-permute-start | bytes 442376 | tf_op jit(solution)/shard_map/ppermute | solution.py:40
  92.3 18.0 %collective-permute-start.26 = (bf16[64,1152]{1,0:T(8,128)(2,1)S(1)}, bf16[64,1152]{1,0:T(8,128)(2,1)S(1)}, u32[]{:S(2)}, u32[]{:S(2)}) collective-permute-start(bf16[64,1152]{1,0:T(8,128)(2,1)S(1)} %get-tuple-element.108), channel_id=1, source_target_pairs={{0,8},{2,10},{4,12},{6,14},{8,0},{10,2},{12,4},{14,6},{1,9},{3,11}... | collective-permute-start | bytes 442376 | tf_op jit(solution)/shard_map/ppermute | solution.py:40
  92.4 17.9 %collective-permute-start.27 = (bf16[64,1152]{1,0:T(8,128)(2,1)S(1)}, bf16[64,1152]{1,0:T(8,128)(2,1)S(1)}, u32[]{:S(2)}, u32[]{:S(2)}) collective-permute-start(bf16[64,1152]{1,0:T(8,128)(2,1)S(1)} %get-tuple-element.109), channel_id=1, source_target_pairs={{0,12},{2,14},{4,8},{6,10},{8,4},{10,6},{12,0},{14,2},{1,13},{3,15... | collective-permute-start | bytes 442376 | tf_op jit(solution)/shard_map/ppermute | solution.py:40
  104.4 7.2 %collective-permute-start.29 = (bf16[64,1152]{1,0:T(8,128)(2,1)S(1)}, bf16[64,1152]{1,0:T(8,128)(2,1)S(1)}, u32[]{:S(2)}, u32[]{:S(2)}) collective-permute-start(bf16[64,1152]{1,0:T(8,128)(2,1)S(1)} %get-tuple-element.115), channel_id=1, source_target_pairs={{0,4},{2,6},{4,0},{6,2},{8,12},{10,14},{12,8},{14,10},{1,5},{3,7},... | collective-permute-start | bytes 442376 | tf_op jit(solution)/shard_map/ppermute | solution.py:40
  104.6 13.0 %collective-permute-start.30 = (bf16[64,1152]{1,0:T(8,128)(2,1)S(1)}, bf16[64,1152]{1,0:T(8,128)(2,1)S(1)}, u32[]{:S(2)}, u32[]{:S(2)}) collective-permute-start(bf16[64,1152]{1,0:T(8,128)(2,1)S(1)} %get-tuple-element.116), channel_id=1, source_target_pairs={{0,8},{2,10},{4,12},{6,14},{8,0},{10,2},{12,4},{14,6},{1,9},{3,11}... | collective-permute-start | bytes 442376 | tf_op jit(solution)/shard_map/ppermute | solution.py:40
  104.8 12.8 %collective-permute-start.31 = (bf16[64,1152]{1,0:T(8,128)(2,1)S(1)}, bf16[64,1152]{1,0:T(8,128)(2,1)S(1)}, u32[]{:S(2)}, u32[]{:S(2)}) collective-permute-start(bf16[64,1152]{1,0:T(8,128)(2,1)S(1)} %get-tuple-element.117), channel_id=1, source_target_pairs={{0,12},{2,14},{4,8},{6,10},{8,4},{10,6},{12,0},{14,2},{1,13},{3,15... | collective-permute-start | bytes 442376 | tf_op jit(solution)/shard_map/ppermute | solution.py:40
